TPU v7x, 256 devices: a whole 4x4x8 slice. The times are simulated.
256 devices in a mesh: lon: 16 (over y_lo, z), lat: 8 (over x, core), dep: 2 (over y_hi).
Axes of the slice: x: 4, y: 4 (y_hi: 2, y_lo: 2; y = y_hi * 2 + y_lo), z: 8, core: 2. Of those that a mesh axis runs over, the one named last changes fastest.
Arguments:
- source: float32 [4, 16, 64, 4096], P(None, 'dep', 'lat', 'lon'), may hold values from -48 to 48
- sea_mask: int32 [16, 64, 4096], P('dep', 'lat', 'lon'), may hold values 0 or 1
- classes: int32 [16, 64, 4096], P('dep', 'lat', 'lon'), may hold values from 0 to 7
- kappa_table: float32 [8, 4], replicated, may hold values from 0.05 to 2
- coupling: float32 [4, 4], replicated, may hold values from -0.8 to 0.8
Outputs:
- first_pass: float32 [4, 16, 64, 4096], P(None, 'dep', 'lat', 'lon')
- second_pass: float32 [4, 16, 64, 4096], P(None, 'dep', 'lat', 'lon')
All inputs are finite; a program needn't handle non-finite values. No bound on the sum of `sea_mask` on one device may be relied on, other than what follows from the above.
Results may differ from a plain program's by a relative error of at most 0.00011.
Values sent between devices are 32-bit elements; how exact they have to be, the bound alone decides.
No kernel may reach another device: no remote copies, remote signals or barrier semaphores. Data moves between devices by JAX's collectives and lax.ppermute only.
A program may use at most 128 MiB of HBM per device.

v0:
```python
import jax
import jax.numpy as jnp
from jax import lax
from jax.sharding import PartitionSpec as P

PRE = 3
POST = 3
COARSE = 4


omega = 0.8


def padded_2(block, sides, width):
    for axis, dim in sides:
        count = lax.axis_size(axis)
        forward = [(i, i + 1) for i in range(count - 1)]
        forward.append((count - 1, 0))
        backward = [(target, source) for source, target in forward]
        low = lax.ppermute(
            lax.slice_in_dim(block, block.shape[dim] - width, None, axis=dim), axis, forward
        )
        high = lax.ppermute(lax.slice_in_dim(block, 0, width, axis=dim), axis, backward)
        block = jnp.concatenate([low, block, high], axis=dim)
    return block


def lookup(classes, table):
    kap = jnp.zeros((table.shape[1],) + classes.shape, jnp.float32)
    for c in range(table.shape[0]):
        kap = kap + jnp.where(classes[None] == c, table[c][:, None, None, None], jnp.float32(0.0))
    return kap


def couple(coupling, u):
    total = coupling[:, 0][:, None, None, None] * u[0][None]
    for g in range(1, u.shape[0]):
        total = total + coupling[:, g][:, None, None, None] * u[g][None]
    return total


def clear_lat(padded, width):
    lat_pos = lax.axis_index("lat")
    lat_last = lax.axis_size("lat") - 1
    rows_lat = lax.broadcasted_iota(jnp.int32, padded.shape, 2)
    cut = (rows_lat < width) & (lat_pos == 0) | (rows_lat >= padded.shape[2] - width) & (
        lat_pos == lat_last
    )
    return jnp.where(cut, jnp.float32(0.0), padded)


def clear_rims(padded, width):
    dep_pos = lax.axis_index("dep")
    dep_last = lax.axis_size("dep") - 1
    rows_dep = lax.broadcasted_iota(jnp.int32, padded.shape, 1)
    cut = (rows_dep < width) & (dep_pos == 0) | (rows_dep >= padded.shape[1] - width) & (
        dep_pos == dep_last
    )
    return jnp.where(cut, jnp.float32(0.0), clear_lat(padded, width))


def six_sum(padded):
    total = padded[:, 1:-1, 1:-1, 2:] + padded[:, 1:-1, 1:-1, :-2]
    total = total + padded[:, 1:-1, 2:, 1:-1] + padded[:, 1:-1, :-2, 1:-1]
    total = total + padded[:, 2:, 1:-1, 1:-1] + padded[:, :-2, 1:-1, 1:-1]
    return total


def fine_near(v):
    padded = padded_2(v, (("lon", 3), ("lat", 2), ("dep", 1)), 1)
    return six_sum(clear_rims(padded, 1))


def coarse_near(v):
    padded = padded_2(v, (("lon", 3), ("lat", 2), ("dep", 1)), 1)
    return six_sum(clear_rims(padded, 1))


def apply_op(u, sea, kap, coupling, scale, near_fn):
    near = near_fn(sea * u)
    return sea * (kap * u + couple(coupling, u) + scale * (6.0 * u - near)) + (1.0 - sea) * u


def diag_of(sea, kap, coupling, scale):
    return sea * (kap + jnp.diagonal(coupling)[:, None, None, None] + 6.0 * scale) + (1.0 - sea)


def sweep(u, b, sea, kap, coupling, scale, diag, near_fn):
    return u + omega * (b - apply_op(u, sea, kap, coupling, scale, near_fn)) / diag


def coarsen(x):
    f, d, a, o = x.shape
    return x.reshape(f, d // 2, 2, a // 2, 2, o // 2, 2).mean(axis=(2, 4, 6))


def prolong(e):
    return jnp.repeat(jnp.repeat(jnp.repeat(e, 2, 1), 2, 2), 2, 3)


def vcycle(b, fine_set, coarse_set, coupling):
    sea, kap, diag, sea_p, kap_p, diag_p = fine_set
    sea_c, kap_c, diag_c = coarse_set
    u = jnp.zeros_like(b)
    for step in range(PRE):
        u = sweep(u, b, sea, kap, coupling, 1.0, diag, fine_near)
    resid = b - apply_op(u, sea, kap, coupling, 1.0, fine_near)
    rc = coarsen(resid)
    rc = sea_c * rc
    e = jnp.zeros_like(rc)
    for step in range(COARSE):
        e = sweep(e, rc, sea_c, kap_c, coupling, 0.25, diag_c, coarse_near)
    u = u + sea * prolong(e)
    for step in range(POST):
        u = sweep(u, b, sea, kap, coupling, 1.0, diag, fine_near)
    return u


def per_device(source, sea_mask, classes, kappa_table, coupling):
    sea = sea_mask.astype(jnp.float32)[None]
    kap = lookup(classes, kappa_table)
    d, a, o = sea_mask.shape
    counts = sea_mask.reshape(d // 2, 2, a // 2, 2, o // 2, 2).sum(axis=(1, 3, 5))
    sea_c = jnp.minimum(counts, 1).astype(jnp.float32)[None]
    kap_c = coarsen(kap)
    diag = diag_of(sea, kap, coupling, 1.0)
    diag_c = diag_of(sea_c, kap_c, coupling, 0.25)
    sea_p, kap_p, diag_p = (sea, kap, diag)
    fine_set = (sea, kap, diag, sea_p, kap_p, diag_p)
    coarse_set = (sea_c, kap_c, diag_c)
    rhs = sea * source
    first_pass = vcycle(rhs, fine_set, coarse_set, coupling)
    second_pass = vcycle(first_pass, fine_set, coarse_set, coupling)
    return (first_pass, second_pass)


def solution(mesh):
    return jax.shard_map(
        per_device,
        mesh=mesh,
        in_specs=(
            P(None, "dep", "lat", "lon"),
            P("dep", "lat", "lon"),
            P("dep", "lat", "lon"),
            P(),
            P(),
        ),
        out_specs=(P(None, "dep", "lat", "lon"), P(None, "dep", "lat", "lon")),
        check_vma=False,
    )
```

profile of v0, /device:TPU:1, one launch (start us, length us, event | category | flops | bytes accessed | tf_op | source)
XLA Modules:
  0.0 523.1 jit_solution(16493940096580975271)
XLA Ops:
  1.7 7.5 %collective-permute-start.1 = (f32[4,8,8,1]{3,2,1,0:T(8,128)S(1)}, f32[4,8,8,1]{3,2,1,0:T(8,128)S(1)}, u32[]{:S(2)}, u32[]{:S(2)}) collective-permute-start(f32[4,8,8,1]{3,2,1,0:T(8,128)S(1)} %mul.791), channel_id=1, source_target_pairs={{16,0},{32,16},{48,32},{64,48},{80,64},{96,80},{112,96},{128,112},... | collective-permute-start | bytes 3080 | tf_op jit(solution)/shard_map/ppermute | solution.py:23
  9.4 6.3 %reshape.85 = s32[4,2,4,2,128,2]{5,4,3,2,1,0:T(8,128)} reshape(s32[8,8,256]{2,1,0:T(8,128)} %param.6) | data formatting | bytes 131072 | tf_op jit(solution)/shard_map/reshape | solution.py:123
  19.7 3.6 collective-permute-start.25
  41.2 3.1 collective-permute-start.7
  44.5 5.5 %broadcast_in_dim.303 = pred[4,2,4,2,128,2]{5,4,3,2,1,0:T(8,128)(4,1)} reshape(pred[8,8,256]{2,1,0:T(8,128)(4,1)S(1)} %get-tuple-element.230) | data formatting | bytes 32768 | tf_op jit(solution)/shard_map/jit(_where)/broadcast_in_dim | solution.py:31
  50.0 5.5 %broadcast_in_dim.300 = pred[4,2,4,2,128,2]{5,4,3,2,1,0:T(8,128)(4,1)} reshape(pred[8,8,256]{2,1,0:T(8,128)(4,1)S(1)} %get-tuple-element.231) | data formatting | bytes 32768 | tf_op jit(solution)/shard_map/jit(_where)/broadcast_in_dim | solution.py:31
  55.5 5.4 %broadcast_in_dim.297 = pred[4,2,4,2,128,2]{5,4,3,2,1,0:T(8,128)(4,1)} reshape(pred[8,8,256]{2,1,0:T(8,128)(4,1)S(1)} %get-tuple-element.225) | data formatting | bytes 32768 | tf_op jit(solution)/shard_map/jit(_where)/broadcast_in_dim | solution.py:31
  61.0 5.5 %broadcast_in_dim.294 = pred[4,2,4,2,128,2]{5,4,3,2,1,0:T(8,128)(4,1)} reshape(pred[8,8,256]{2,1,0:T(8,128)(4,1)S(1)} %get-tuple-element.226) | data formatting | bytes 32768 | tf_op jit(solution)/shard_map/jit(_where)/broadcast_in_dim | solution.py:31
  66.4 5.4 %broadcast_in_dim.291 = pred[4,2,4,2,128,2]{5,4,3,2,1,0:T(8,128)(4,1)} reshape(pred[8,8,256]{2,1,0:T(8,128)(4,1)S(1)} %get-tuple-element.227) | data formatting | bytes 32768 | tf_op jit(solution)/shard_map/jit(_where)/broadcast_in_dim | solution.py:31
  71.8 5.4 %broadcast_in_dim.288 = pred[4,2,4,2,128,2]{5,4,3,2,1,0:T(8,128)(4,1)} reshape(pred[8,8,256]{2,1,0:T(8,128)(4,1)S(1)} %get-tuple-element.228) | data formatting | bytes 32768 | tf_op jit(solution)/shard_map/jit(_where)/broadcast_in_dim | solution.py:31
  77.3 4.6 broadcast_in_dim.285
  82.0 4.7 broadcast_in_dim.281
  95.4 3.1 copy.1232
  122.0 3.3 collective-permute-start.13
  127.2 4.0 collective-permute-done.12
  131.5 6.5 %collective-permute-start.15 = (f32[4,8,1,258]{3,1,2,0:T(8,128)S(1)}, f32[4,8,1,258]{3,1,2,0:T(8,128)S(1)}, u32[]{:S(2)}, u32[]{:S(2)}) collective-permute-start(f32[4,8,1,258]{3,1,2,0:T(8,128)S(1)} %copy.1209), channel_id=1, source_target_pairs={{2,0},{4,2},{6,4},{8,6},{10,8},{12,10},{14,12},{0,14},{3,1},{5,3},... | collective-permute-start | bytes 99080 | tf_op jit(solution)/shard_map/ppermute | solution.py:23
  155.8 4.9 collective-permute-start.21
  169.1 4.7 copy.1226
  173.9 8.7 %reduce_sum.36 = f32[4,4,4,128]{0,3,2,1:T(8,128)S(1)} reduce(f32[4,4,2,4,2,128,2]{0,6,5,4,3,2,1:T(2,128)} %bitcast.155, f32[]{:T(128)} %constant.19.clone.1), dimensions={2,4,6}, to_apply=%region_0.1 | reduce | flops 57344 | bytes 294916 | tf_op jit(solution)/shard_map/reduce_sum | solution.py:94
  189.4 6.3 %collective-permute-start.33 = (f32[4,4,1,130]{3,2,1,0:T(1,128)S(1)}, f32[4,4,1,130]{3,2,1,0:T(1,128)S(1)}, u32[]{:S(2)}, u32[]{:S(2)}) collective-permute-start(f32[4,4,1,130]{3,2,1,0:T(1,128)S(1)} %get-tuple-element.218), channel_id=1, source_target_pairs={{2,0},{4,2},{6,4},{8,6},{10,8},{12,10},{14,12},{0,14},{3,1},{5,3},... | collective-permute-start | bytes 24968 | tf_op jit(solution)/shard_map/ppermute | solution.py:23
  197.0 3.4 collective-permute-start.35
  210.3 5.8 %collective-permute-start.39 = (f32[4,4,1,130]{3,2,1,0:T(1,128)S(1)}, f32[4,4,1,130]{3,2,1,0:T(1,128)S(1)}, u32[]{:S(2)}, u32[]{:S(2)}) collective-permute-start(f32[4,4,1,130]{3,2,1,0:T(1,128)S(1)} %get-tuple-element.216), channel_id=1, source_target_pairs={{2,0},{4,2},{6,4},{8,6},{10,8},{12,10},{14,12},{0,14},{3,1},{5,3},... | collective-permute-start | bytes 24968 | tf_op jit(solution)/shard_map/ppermute | solution.py:23
  227.7 5.8 %collective-permute-start.45 = (f32[4,4,1,130]{3,2,1,0:T(1,128)S(1)}, f32[4,4,1,130]{3,2,1,0:T(1,128)S(1)}, u32[]{:S(2)}, u32[]{:S(2)}) collective-permute-start(f32[4,4,1,130]{3,2,1,0:T(1,128)S(1)} %get-tuple-element.214), channel_id=1, source_target_pairs={{2,0},{4,2},{6,4},{8,6},{10,8},{12,10},{14,12},{0,14},{3,1},{5,3},... | collective-permute-start | bytes 24968 | tf_op jit(solution)/shard_map/ppermute | solution.py:23
  234.7 3.2 collective-permute-start.47
  255.0 5.8 %collective-permute-start.51 = (f32[4,8,1,258]{3,1,2,0:T(8,128)S(1)}, f32[4,8,1,258]{3,1,2,0:T(8,128)S(1)}, u32[]{:S(2)}, u32[]{:S(2)}) collective-permute-start(f32[4,8,1,258]{3,1,2,0:T(8,128)S(1)} %copy.1244), channel_id=1, source_target_pairs={{2,0},{4,2},{6,4},{8,6},{10,8},{12,10},{14,12},{0,14},{3,1},{5,3},... | collective-permute-start | bytes 99080 | tf_op jit(solution)/shard_map/ppermute | solution.py:23
  275.5 6.1 %collective-permute-start.57 = (f32[4,8,1,258]{3,1,2,0:T(8,128)S(1)}, f32[4,8,1,258]{3,1,2,0:T(8,128)S(1)}, u32[]{:S(2)}, u32[]{:S(2)}) collective-permute-start(f32[4,8,1,258]{3,1,2,0:T(8,128)S(1)} %copy.1253), channel_id=1, source_target_pairs={{2,0},{4,2},{6,4},{8,6},{10,8},{12,10},{14,12},{0,14},{3,1},{5,3},... | collective-permute-start | bytes 99080 | tf_op jit(solution)/shard_map/ppermute | solution.py:23
  283.1 3.2 collective-permute-start.59
  287.9 3.1 collective-permute-done.58
  298.7 6.1 %collective-permute-start.63 = (f32[4,8,1,258]{3,1,2,0:T(8,128)S(1)}, f32[4,8,1,258]{3,1,2,0:T(8,128)S(1)}, u32[]{:S(2)}, u32[]{:S(2)}) collective-permute-start(f32[4,8,1,258]{3,1,2,0:T(8,128)S(1)} %copy.1262), channel_id=1, source_target_pairs={{2,0},{4,2},{6,4},{8,6},{10,8},{12,10},{14,12},{0,14},{3,1},{5,3},... | collective-permute-start | bytes 99080 | tf_op jit(solution)/shard_map/ppermute | solution.py:23
  319.8 5.9 %collective-permute-start.69 = (f32[4,8,1,258]{3,1,2,0:T(8,128)S(1)}, f32[4,8,1,258]{3,1,2,0:T(8,128)S(1)}, u32[]{:S(2)}, u32[]{:S(2)}) collective-permute-start(f32[4,8,1,258]{3,1,2,0:T(8,128)S(1)} %copy.1271), channel_id=1, source_target_pairs={{2,0},{4,2},{6,4},{8,6},{10,8},{12,10},{14,12},{0,14},{3,1},{5,3},... | collective-permute-start | bytes 99080 | tf_op jit(solution)/shard_map/ppermute | solution.py:23
  327.2 3.1 collective-permute-start.71
  332.0 3.1 collective-permute-done.70
  342.8 6.1 %collective-permute-start.75 = (f32[4,8,1,258]{3,1,2,0:T(8,128)S(1)}, f32[4,8,1,258]{3,1,2,0:T(8,128)S(1)}, u32[]{:S(2)}, u32[]{:S(2)}) collective-permute-start(f32[4,8,1,258]{3,1,2,0:T(8,128)S(1)} %copy.1280), channel_id=1, source_target_pairs={{2,0},{4,2},{6,4},{8,6},{10,8},{12,10},{14,12},{0,14},{3,1},{5,3},... | collective-permute-start | bytes 99080 | tf_op jit(solution)/shard_map/ppermute | solution.py:23
  363.5 5.8 %collective-permute-start.81 = (f32[4,8,1,258]{3,1,2,0:T(8,128)S(1)}, f32[4,8,1,258]{3,1,2,0:T(8,128)S(1)}, u32[]{:S(2)}, u32[]{:S(2)}) collective-permute-start(f32[4,8,1,258]{3,1,2,0:T(8,128)S(1)} %copy.1289), channel_id=1, source_target_pairs={{2,0},{4,2},{6,4},{8,6},{10,8},{12,10},{14,12},{0,14},{3,1},{5,3},... | collective-permute-start | bytes 99080 | tf_op jit(solution)/shard_map/ppermute | solution.py:23
  370.8 3.2 collective-permute-start.83
  375.6 3.7 collective-permute-done.82
  380.5 4.7 copy.1297
  385.2 8.7 %reduce_sum.39 = f32[4,4,4,128]{0,3,2,1:T(8,128)S(1)} reduce(f32[4,4,2,4,2,128,2]{0,6,5,4,3,2,1:T(2,128)} %bitcast.154, f32[]{:T(128)} %constant.19.clone.1), dimensions={2,4,6}, to_apply=%region_3.4 | reduce | flops 57344 | bytes 294916 | tf_op jit(solution)/shard_map/reduce_sum | solution.py:94
  399.7 5.6 %collective-permute-start.87 = (f32[4,4,1,130]{3,2,1,0:T(1,128)S(1)}, f32[4,4,1,130]{3,2,1,0:T(1,128)S(1)}, u32[]{:S(2)}, u32[]{:S(2)}) collective-permute-start(f32[4,4,1,130]{3,2,1,0:T(1,128)S(1)} %get-tuple-element.212), channel_id=1, source_target_pairs={{2,0},{4,2},{6,4},{8,6},{10,8},{12,10},{14,12},{0,14},{3,1},{5,3},... | collective-permute-start | bytes 24968 | tf_op jit(solution)/shard_map/ppermute | solution.py:23
  417.1 5.7 %collective-permute-start.93 = (f32[4,4,1,130]{3,2,1,0:T(1,128)S(1)}, f32[4,4,1,130]{3,2,1,0:T(1,128)S(1)}, u32[]{:S(2)}, u32[]{:S(2)}) collective-permute-start(f32[4,4,1,130]{3,2,1,0:T(1,128)S(1)} %get-tuple-element.210), channel_id=1, source_target_pairs={{2,0},{4,2},{6,4},{8,6},{10,8},{12,10},{14,12},{0,14},{3,1},{5,3},... | collective-permute-start | bytes 24968 | tf_op jit(solution)/shard_map/ppermute | solution.py:23
  424.1 3.2 collective-permute-start.95
  437.2 5.8 %collective-permute-start.99 = (f32[4,4,1,130]{3,2,1,0:T(1,128)S(1)}, f32[4,4,1,130]{3,2,1,0:T(1,128)S(1)}, u32[]{:S(2)}, u32[]{:S(2)}) collective-permute-start(f32[4,4,1,130]{3,2,1,0:T(1,128)S(1)} %get-tuple-element.208), channel_id=1, source_target_pairs={{2,0},{4,2},{6,4},{8,6},{10,8},{12,10},{14,12},{0,14},{3,1},{5,3},... | collective-permute-start | bytes 24968 | tf_op jit(solution)/shard_map/ppermute | solution.py:23
  461.9 5.5 %collective-permute-start.105 = (f32[4,8,1,258]{3,1,2,0:T(8,128)S(1)}, f32[4,8,1,258]{3,1,2,0:T(8,128)S(1)}, u32[]{:S(2)}, u32[]{:S(2)}) collective-permute-start(f32[4,8,1,258]{3,1,2,0:T(8,128)S(1)} %copy.1306), channel_id=1, source_target_pairs={{2,0},{4,2},{6,4},{8,6},{10,8},{12,10},{14,12},{0,14},{3,1},{5,3},... | collective-permute-start | bytes 99080 | tf_op jit(solution)/shard_map/ppermute | solution.py:23
  468.9 3.4 collective-permute-start.107
  473.9 3.5 collective-permute-done.106
  485.4 5.7 %collective-permute-start.111 = (f32[4,8,1,258]{3,1,2,0:T(8,128)S(1)}, f32[4,8,1,258]{3,1,2,0:T(8,128)S(1)}, u32[]{:S(2)}, u32[]{:S(2)}) collective-permute-start(f32[4,8,1,258]{3,1,2,0:T(8,128)S(1)} %copy.1315), channel_id=1, source_target_pairs={{2,0},{4,2},{6,4},{8,6},{10,8},{12,10},{14,12},{0,14},{3,1},{5,3},... | collective-permute-start | bytes 99080 | tf_op jit(solution)/shard_map/ppermute | solution.py:23
  505.7 5.8 %collective-permute-start.117 = (f32[4,8,1,258]{3,1,2,0:T(8,128)S(1)}, f32[4,8,1,258]{3,1,2,0:T(8,128)S(1)}, u32[]{:S(2)}, u32[]{:S(2)}) collective-permute-start(f32[4,8,1,258]{3,1,2,0:T(8,128)S(1)} %copy.1324), channel_id=1, source_target_pairs={{2,0},{4,2},{6,4},{8,6},{10,8},{12,10},{14,12},{0,14},{3,1},{5,3},... | collective-permute-start | bytes 99080 | tf_op jit(solution)/shard_map/ppermute | solution.py:23
  517.7 3.0 collective-permute-done.118
  (573 shorter events, 281.7 us)
Async XLA Ops:
  1.7 23.0 %collective-permute-start.1 = (f32[4,8,8,1]{3,2,1,0:T(8,128)S(1)}, f32[4,8,8,1]{3,2,1,0:T(8,128)S(1)}, u32[]{:S(2)}, u32[]{:S(2)}) collective-permute-start(f32[4,8,8,1]{3,2,1,0:T(8,128)S(1)} %mul.791), channel_id=1, source_target_pairs={{16,0},{32,16},{48,32},{64,48},{80,64},{96,80},{112,96},{128,112},... | collective-permute-start | bytes 3080 | tf_op jit(solution)/shard_map/ppermute | solution.py:23
  9.3 15.4 %collective-permute-start = (f32[4,8,8,1]{3,2,1,0:T(8,128)S(1)}, f32[4,8,8,1]{3,2,1,0:T(8,128)S(1)}, u32[]{:S(2)}, u32[]{:S(2)}) collective-permute-start(f32[4,8,8,1]{3,2,1,0:T(8,128)S(1)} %mul.789), channel_id=1, source_target_pairs={{0,16},{16,32},{32,48},{48,64},{64,80},{80,96},{96,112},{112,128},... | collective-permute-start | bytes 3080 | tf_op jit(solution)/shard_map/ppermute | solution.py:20
  19.7 118.3 %collective-permute-start.25 = (f32[4,4,4,1]{3,2,1,0:T(4,128)}, f32[4,4,4,1]{3,2,1,0:T(4,128)S(1)}, u32[]{:S(2)}, u32[]{:S(2)}) collective-permute-start(f32[4,4,4,1]{3,2,1,0:T(4,128)} %mul.866), channel_id=1, source_target_pairs={{16,0},{32,16},{48,32},{64,48},{80,64},{96,80},{112,96},{128,112},... | collective-permute-start | bytes 776 | tf_op jit(solution)/shard_map/ppermute | solution.py:23
  24.0 114.0 %collective-permute-start.24 = (f32[4,4,4,1]{3,2,1,0:T(4,128)}, f32[4,4,4,1]{3,2,1,0:T(4,128)S(1)}, u32[]{:S(2)}, u32[]{:S(2)}) collective-permute-start(f32[4,4,4,1]{3,2,1,0:T(4,128)} %mul.864), channel_id=1, source_target_pairs={{0,16},{16,32},{32,48},{48,64},{64,80},{80,96},{96,112},{112,128},... | collective-permute-start | bytes 776 | tf_op jit(solution)/shard_map/ppermute | solution.py:20
  41.2 66.4 %collective-permute-start.7 = (f32[4,8,8,1]{3,2,1,0:T(8,128)}, f32[4,8,8,1]{3,2,1,0:T(8,128)S(1)}, u32[]{:S(2)}, u32[]{:S(2)}) collective-permute-start(f32[4,8,8,1]{3,2,1,0:T(8,128)} %get-tuple-element.192), channel_id=1, source_target_pairs={{16,0},{32,16},{48,32},{64,48},{80,64},{96,80},{112,96},{128,112},... | collective-permute-start | bytes 3080 | tf_op jit(solution)/shard_map/ppermute | solution.py:23
  44.4 63.3 %collective-permute-start.6 = (f32[4,8,8,1]{3,2,1,0:T(8,128)}, f32[4,8,8,1]{3,2,1,0:T(8,128)S(1)}, u32[]{:S(2)}, u32[]{:S(2)}) collective-permute-start(f32[4,8,8,1]{3,2,1,0:T(8,128)} %get-tuple-element.191), channel_id=1, source_target_pairs={{0,16},{16,32},{32,48},{48,64},{64,80},{80,96},{96,112},{112,128},... | collective-permute-start | bytes 3080 | tf_op jit(solution)/shard_map/ppermute | solution.py:20
  122.0 5.2 collective-permute-start.13
  125.2 5.9 %collective-permute-start.12 = (f32[4,8,8,1]{3,2,1,0:T(8,128)S(1)}, f32[4,8,8,1]{3,2,1,0:T(8,128)S(1)}, u32[]{:S(2)}, u32[]{:S(2)}) collective-permute-start(f32[4,8,8,1]{3,2,1,0:T(8,128)S(1)} %get-tuple-element.185), channel_id=1, source_target_pairs={{0,16},{16,32},{32,48},{48,64},{64,80},{80,96},{96,112},{112,128},... | collective-permute-start | bytes 3080 | tf_op jit(solution)/shard_map/ppermute | solution.py:20
  131.5 8.5 %collective-permute-start.15 = (f32[4,8,1,258]{3,1,2,0:T(8,128)S(1)}, f32[4,8,1,258]{3,1,2,0:T(8,128)S(1)}, u32[]{:S(2)}, u32[]{:S(2)}) collective-permute-start(f32[4,8,1,258]{3,1,2,0:T(8,128)S(1)} %copy.1209), channel_id=1, source_target_pairs={{2,0},{4,2},{6,4},{8,6},{10,8},{12,10},{14,12},{0,14},{3,1},{5,3},... | collective-permute-start | bytes 99080 | tf_op jit(solution)/shard_map/ppermute | solution.py:23
  138.2 12.7 %collective-permute-start.27 = (f32[4,4,1,130]{3,2,1,0:T(1,128)S(1)}, f32[4,4,1,130]{3,2,1,0:T(1,128)S(1)}, u32[]{:S(2)}, u32[]{:S(2)}) collective-permute-start(f32[4,4,1,130]{3,2,1,0:T(1,128)S(1)} %get-tuple-element.220), channel_id=1, source_target_pairs={{2,0},{4,2},{6,4},{8,6},{10,8},{12,10},{14,12},{0,14},{3,1},{5,3},... | collective-permute-start | bytes 24968 | tf_op jit(solution)/shard_map/ppermute | solution.py:23
  138.7 12.2 %collective-permute-start.26 = (f32[4,4,1,130]{3,2,1,0:T(1,128)S(1)}, f32[4,4,1,130]{3,2,1,0:T(1,128)S(1)}, u32[]{:S(2)}, u32[]{:S(2)}) collective-permute-start(f32[4,4,1,130]{3,2,1,0:T(1,128)S(1)} %get-tuple-element.219), channel_id=1, source_target_pairs={{0,2},{2,4},{4,6},{6,8},{8,10},{10,12},{12,14},{14,0},{1,3},{3,5},... | collective-permute-start | bytes 24968 | tf_op jit(solution)/shard_map/ppermute | solution.py:20
  142.9 5.1 collective-permute-start.16
  149.3 5.2 collective-permute-start.19
  149.4 6.1 %collective-permute-start.18 = (f32[4,8,8,1]{3,2,1,0:T(8,128)S(1)}, f32[4,8,8,1]{3,2,1,0:T(8,128)S(1)}, u32[]{:S(2)}, u32[]{:S(2)}) collective-permute-start(f32[4,8,8,1]{3,2,1,0:T(8,128)S(1)} %get-tuple-element.179), channel_id=1, source_target_pairs={{0,16},{16,32},{32,48},{48,64},{64,80},{80,96},{96,112},{112,128},... | collective-permute-start | bytes 3080 | tf_op jit(solution)/shard_map/ppermute | solution.py:20
  151.0 9.8 %collective-permute-start.29 = (f32[4,1,6,130]{3,2,1,0:T(8,128)S(1)}, f32[4,1,6,130]{3,2,1,0:T(8,128)S(1)}, u32[]{:S(2)}, u32[]{:S(2)}) collective-permute-start(f32[4,1,6,130]{3,2,1,0:T(8,128)S(1)} %get-tuple-element.206), channel_id=1, source_target_pairs={{1,0},{0,1},{3,2},{2,3},{5,4},{4,5},{7,6},{6,7},{9,8},{8,9},{11,10... | collective-permute-start | bytes 37448 | tf_op jit(solution)/shard_map/ppermute | solution.py:23
  151.7 9.1 %collective-permute-start.28 = (f32[4,1,6,130]{3,2,1,0:T(8,128)S(1)}, f32[4,1,6,130]{3,2,1,0:T(8,128)S(1)}, u32[]{:S(2)}, u32[]{:S(2)}) collective-permute-start(f32[4,1,6,130]{3,2,1,0:T(8,128)S(1)} %get-tuple-element.205), channel_id=1, source_target_pairs={{0,1},{1,0},{2,3},{3,2},{4,5},{5,4},{6,7},{7,6},{8,9},{9,8},{10,11... | collective-permute-start | bytes 37448 | tf_op jit(solution)/shard_map/ppermute | solution.py:20
  155.8 5.8 %collective-permute-start.21 = (f32[4,8,1,258]{3,1,2,0:T(8,128)S(1)}, f32[4,8,1,258]{3,1,2,0:T(8,128)S(1)}, u32[]{:S(2)}, u32[]{:S(2)}) collective-permute-start(f32[4,8,1,258]{3,1,2,0:T(8,128)S(1)} %copy.1218), channel_id=1, source_target_pairs={{2,0},{4,2},{6,4},{8,6},{10,8},{12,10},{14,12},{0,14},{3,1},{5,3},... | collective-permute-start | bytes 99080 | tf_op jit(solution)/shard_map/ppermute | solution.py:23
  189.4 7.1 %collective-permute-start.33 = (f32[4,4,1,130]{3,2,1,0:T(1,128)S(1)}, f32[4,4,1,130]{3,2,1,0:T(1,128)S(1)}, u32[]{:S(2)}, u32[]{:S(2)}) collective-permute-start(f32[4,4,1,130]{3,2,1,0:T(1,128)S(1)} %get-tuple-element.218), channel_id=1, source_target_pairs={{2,0},{4,2},{6,4},{8,6},{10,8},{12,10},{14,12},{0,14},{3,1},{5,3},... | collective-permute-start | bytes 24968 | tf_op jit(solution)/shard_map/ppermute | solution.py:23
  205.1 5.0 collective-permute-start.36
  210.3 6.6 %collective-permute-start.39 = (f32[4,4,1,130]{3,2,1,0:T(1,128)S(1)}, f32[4,4,1,130]{3,2,1,0:T(1,128)S(1)}, u32[]{:S(2)}, u32[]{:S(2)}) collective-permute-start(f32[4,4,1,130]{3,2,1,0:T(1,128)S(1)} %get-tuple-element.216), channel_id=1, source_target_pairs={{2,0},{4,2},{6,4},{8,6},{10,8},{12,10},{14,12},{0,14},{3,1},{5,3},... | collective-permute-start | bytes 24968 | tf_op jit(solution)/shard_map/ppermute | solution.py:23
  222.5 5.0 collective-permute-start.42
  227.7 6.6 %collective-permute-start.45 = (f32[4,4,1,130]{3,2,1,0:T(1,128)S(1)}, f32[4,4,1,130]{3,2,1,0:T(1,128)S(1)}, u32[]{:S(2)}, u32[]{:S(2)}) collective-permute-start(f32[4,4,1,130]{3,2,1,0:T(1,128)S(1)} %get-tuple-element.214), channel_id=1, source_target_pairs={{2,0},{4,2},{6,4},{8,6},{10,8},{12,10},{14,12},{0,14},{3,1},{5,3},... | collective-permute-start | bytes 24968 | tf_op jit(solution)/shard_map/ppermute | solution.py:23
  248.7 6.0 %collective-permute-start.48 = (f32[4,8,8,1]{3,2,1,0:T(8,128)S(1)}, f32[4,8,8,1]{3,2,1,0:T(8,128)S(1)}, u32[]{:S(2)}, u32[]{:S(2)}) collective-permute-start(f32[4,8,8,1]{3,2,1,0:T(8,128)S(1)} %get-tuple-element.173), channel_id=1, source_target_pairs={{0,16},{16,32},{32,48},{48,64},{64,80},{80,96},{96,112},{112,128},... | collective-permute-start | bytes 3080 | tf_op jit(solution)/shard_map/ppermute | solution.py:20
  255.0 6.7 %collective-permute-start.51 = (f32[4,8,1,258]{3,1,2,0:T(8,128)S(1)}, f32[4,8,1,258]{3,1,2,0:T(8,128)S(1)}, u32[]{:S(2)}, u32[]{:S(2)}) collective-permute-start(f32[4,8,1,258]{3,1,2,0:T(8,128)S(1)} %copy.1244), channel_id=1, source_target_pairs={{2,0},{4,2},{6,4},{8,6},{10,8},{12,10},{14,12},{0,14},{3,1},{5,3},... | collective-permute-start | bytes 99080 | tf_op jit(solution)/shard_map/ppermute | solution.py:23
  269.1 6.0 %collective-permute-start.54 = (f32[4,8,8,1]{3,2,1,0:T(8,128)S(1)}, f32[4,8,8,1]{3,2,1,0:T(8,128)S(1)}, u32[]{:S(2)}, u32[]{:S(2)}) collective-permute-start(f32[4,8,8,1]{3,2,1,0:T(8,128)S(1)} %get-tuple-element.167), channel_id=1, source_target_pairs={{0,16},{16,32},{32,48},{48,64},{64,80},{80,96},{96,112},{112,128},... | collective-permute-start | bytes 3080 | tf_op jit(solution)/shard_map/ppermute | solution.py:20
  275.5 7.0 %collective-permute-start.57 = (f32[4,8,1,258]{3,1,2,0:T(8,128)S(1)}, f32[4,8,1,258]{3,1,2,0:T(8,128)S(1)}, u32[]{:S(2)}, u32[]{:S(2)}) collective-permute-start(f32[4,8,1,258]{3,1,2,0:T(8,128)S(1)} %copy.1253), channel_id=1, source_target_pairs={{2,0},{4,2},{6,4},{8,6},{10,8},{12,10},{14,12},{0,14},{3,1},{5,3},... | collective-permute-start | bytes 99080 | tf_op jit(solution)/shard_map/ppermute | solution.py:23
  292.4 6.0 %collective-permute-start.60 = (f32[4,8,8,1]{3,2,1,0:T(8,128)S(1)}, f32[4,8,8,1]{3,2,1,0:T(8,128)S(1)}, u32[]{:S(2)}, u32[]{:S(2)}) collective-permute-start(f32[4,8,8,1]{3,2,1,0:T(8,128)S(1)} %get-tuple-element.161), channel_id=1, source_target_pairs={{0,16},{16,32},{32,48},{48,64},{64,80},{80,96},{96,112},{112,128},... | collective-permute-start | bytes 3080 | tf_op jit(solution)/shard_map/ppermute | solution.py:20
  298.7 7.0 %collective-permute-start.63 = (f32[4,8,1,258]{3,1,2,0:T(8,128)S(1)}, f32[4,8,1,258]{3,1,2,0:T(8,128)S(1)}, u32[]{:S(2)}, u32[]{:S(2)}) collective-permute-start(f32[4,8,1,258]{3,1,2,0:T(8,128)S(1)} %copy.1262), channel_id=1, source_target_pairs={{2,0},{4,2},{6,4},{8,6},{10,8},{12,10},{14,12},{0,14},{3,1},{5,3},... | collective-permute-start | bytes 99080 | tf_op jit(solution)/shard_map/ppermute | solution.py:23
  313.1 6.4 %collective-permute-start.66 = (f32[4,8,8,1]{3,2,1,0:T(8,128)S(1)}, f32[4,8,8,1]{3,2,1,0:T(8,128)S(1)}, u32[]{:S(2)}, u32[]{:S(2)}) collective-permute-start(f32[4,8,8,1]{3,2,1,0:T(8,128)S(1)} %get-tuple-element.155), channel_id=1, source_target_pairs={{0,16},{16,32},{32,48},{48,64},{64,80},{80,96},{96,112},{112,128},... | collective-permute-start | bytes 3080 | tf_op jit(solution)/shard_map/ppermute | solution.py:20
  319.8 6.8 %collective-permute-start.69 = (f32[4,8,1,258]{3,1,2,0:T(8,128)S(1)}, f32[4,8,1,258]{3,1,2,0:T(8,128)S(1)}, u32[]{:S(2)}, u32[]{:S(2)}) collective-permute-start(f32[4,8,1,258]{3,1,2,0:T(8,128)S(1)} %copy.1271), channel_id=1, source_target_pairs={{2,0},{4,2},{6,4},{8,6},{10,8},{12,10},{14,12},{0,14},{3,1},{5,3},... | collective-permute-start | bytes 99080 | tf_op jit(solution)/shard_map/ppermute | solution.py:23
  336.4 6.0 %collective-permute-start.72 = (f32[4,8,8,1]{3,2,1,0:T(8,128)S(1)}, f32[4,8,8,1]{3,2,1,0:T(8,128)S(1)}, u32[]{:S(2)}, u32[]{:S(2)}) collective-permute-start(f32[4,8,8,1]{3,2,1,0:T(8,128)S(1)} %get-tuple-element.149), channel_id=1, source_target_pairs={{0,16},{16,32},{32,48},{48,64},{64,80},{80,96},{96,112},{112,128},... | collective-permute-start | bytes 3080 | tf_op jit(solution)/shard_map/ppermute | solution.py:20
  342.8 7.0 %collective-permute-start.75 = (f32[4,8,1,258]{3,1,2,0:T(8,128)S(1)}, f32[4,8,1,258]{3,1,2,0:T(8,128)S(1)}, u32[]{:S(2)}, u32[]{:S(2)}) collective-permute-start(f32[4,8,1,258]{3,1,2,0:T(8,128)S(1)} %copy.1280), channel_id=1, source_target_pairs={{2,0},{4,2},{6,4},{8,6},{10,8},{12,10},{14,12},{0,14},{3,1},{5,3},... | collective-permute-start | bytes 99080 | tf_op jit(solution)/shard_map/ppermute | solution.py:23
  357.1 6.0 %collective-permute-start.78 = (f32[4,8,8,1]{3,2,1,0:T(8,128)S(1)}, f32[4,8,8,1]{3,2,1,0:T(8,128)S(1)}, u32[]{:S(2)}, u32[]{:S(2)}) collective-permute-start(f32[4,8,8,1]{3,2,1,0:T(8,128)S(1)} %get-tuple-element.143), channel_id=1, source_target_pairs={{0,16},{16,32},{32,48},{48,64},{64,80},{80,96},{96,112},{112,128},... | collective-permute-start | bytes 3080 | tf_op jit(solution)/shard_map/ppermute | solution.py:20
  363.5 6.7 %collective-permute-start.81 = (f32[4,8,1,258]{3,1,2,0:T(8,128)S(1)}, f32[4,8,1,258]{3,1,2,0:T(8,128)S(1)}, u32[]{:S(2)}, u32[]{:S(2)}) collective-permute-start(f32[4,8,1,258]{3,1,2,0:T(8,128)S(1)} %copy.1289), channel_id=1, source_target_pairs={{2,0},{4,2},{6,4},{8,6},{10,8},{12,10},{14,12},{0,14},{3,1},{5,3},... | collective-permute-start | bytes 99080 | tf_op jit(solution)/shard_map/ppermute | solution.py:23
  374.0 5.3 %collective-permute-start.82 = (f32[4,1,10,258]{3,0,2,1:T(4,128)S(1)}, f32[4,1,10,258]{3,0,2,1:T(4,128)S(1)}, u32[]{:S(2)}, u32[]{:S(2)}) collective-permute-start(f32[4,1,10,258]{3,0,2,1:T(4,128)S(1)} %copy.1292), channel_id=1, source_target_pairs={{0,1},{1,0},{2,3},{3,2},{4,5},{5,4},{6,7},{7,6},{8,9},{9,8},{10,11... | collective-permute-start | bytes 123848 | tf_op jit(solution)/shard_map/ppermute | solution.py:20
  394.6 5.0 collective-permute-start.84
  399.7 6.5 %collective-permute-start.87 = (f32[4,4,1,130]{3,2,1,0:T(1,128)S(1)}, f32[4,4,1,130]{3,2,1,0:T(1,128)S(1)}, u32[]{:S(2)}, u32[]{:S(2)}) collective-permute-start(f32[4,4,1,130]{3,2,1,0:T(1,128)S(1)} %get-tuple-element.212), channel_id=1, source_target_pairs={{2,0},{4,2},{6,4},{8,6},{10,8},{12,10},{14,12},{0,14},{3,1},{5,3},... | collective-permute-start | bytes 24968 | tf_op jit(solution)/shard_map/ppermute | solution.py:23
  411.8 5.2 collective-permute-start.90
  417.1 6.6 %collective-permute-start.93 = (f32[4,4,1,130]{3,2,1,0:T(1,128)S(1)}, f32[4,4,1,130]{3,2,1,0:T(1,128)S(1)}, u32[]{:S(2)}, u32[]{:S(2)}) collective-permute-start(f32[4,4,1,130]{3,2,1,0:T(1,128)S(1)} %get-tuple-element.210), channel_id=1, source_target_pairs={{2,0},{4,2},{6,4},{8,6},{10,8},{12,10},{14,12},{0,14},{3,1},{5,3},... | collective-permute-start | bytes 24968 | tf_op jit(solution)/shard_map/ppermute | solution.py:23
  437.2 6.6 %collective-permute-start.99 = (f32[4,4,1,130]{3,2,1,0:T(1,128)S(1)}, f32[4,4,1,130]{3,2,1,0:T(1,128)S(1)}, u32[]{:S(2)}, u32[]{:S(2)}) collective-permute-start(f32[4,4,1,130]{3,2,1,0:T(1,128)S(1)} %get-tuple-element.208), channel_id=1, source_target_pairs={{2,0},{4,2},{6,4},{8,6},{10,8},{12,10},{14,12},{0,14},{3,1},{5,3},... | collective-permute-start | bytes 24968 | tf_op jit(solution)/shard_map/ppermute | solution.py:23
  455.5 6.0 %collective-permute-start.102 = (f32[4,8,8,1]{3,2,1,0:T(8,128)S(1)}, f32[4,8,8,1]{3,2,1,0:T(8,128)S(1)}, u32[]{:S(2)}, u32[]{:S(2)}) collective-permute-start(f32[4,8,8,1]{3,2,1,0:T(8,128)S(1)} %get-tuple-element.137), channel_id=1, source_target_pairs={{0,16},{16,32},{32,48},{48,64},{64,80},{80,96},{96,112},{112,128},... | collective-permute-start | bytes 3080 | tf_op jit(solution)/shard_map/ppermute | solution.py:20
  461.9 6.4 %collective-permute-start.105 = (f32[4,8,1,258]{3,1,2,0:T(8,128)S(1)}, f32[4,8,1,258]{3,1,2,0:T(8,128)S(1)}, u32[]{:S(2)}, u32[]{:S(2)}) collective-permute-start(f32[4,8,1,258]{3,1,2,0:T(8,128)S(1)} %copy.1306), channel_id=1, source_target_pairs={{2,0},{4,2},{6,4},{8,6},{10,8},{12,10},{14,12},{0,14},{3,1},{5,3},... | collective-permute-start | bytes 99080 | tf_op jit(solution)/shard_map/ppermute | solution.py:23
  468.9 5.0 collective-permute-start.107
  472.3 5.1 collective-permute-start.106
  478.8 6.3 %collective-permute-start.108 = (f32[4,8,8,1]{3,2,1,0:T(8,128)S(1)}, f32[4,8,8,1]{3,2,1,0:T(8,128)S(1)}, u32[]{:S(2)}, u32[]{:S(2)}) collective-permute-start(f32[4,8,8,1]{3,2,1,0:T(8,128)S(1)} %get-tuple-element.131), channel_id=1, source_target_pairs={{0,16},{16,32},{32,48},{48,64},{64,80},{80,96},{96,112},{112,128},... | collective-permute-start | bytes 3080 | tf_op jit(solution)/shard_map/ppermute | solution.py:20
  485.4 6.6 %collective-permute-start.111 = (f32[4,8,1,258]{3,1,2,0:T(8,128)S(1)}, f32[4,8,1,258]{3,1,2,0:T(8,128)S(1)}, u32[]{:S(2)}, u32[]{:S(2)}) collective-permute-start(f32[4,8,1,258]{3,1,2,0:T(8,128)S(1)} %copy.1315), channel_id=1, source_target_pairs={{2,0},{4,2},{6,4},{8,6},{10,8},{12,10},{14,12},{0,14},{3,1},{5,3},... | collective-permute-start | bytes 99080 | tf_op jit(solution)/shard_map/ppermute | solution.py:23
  499.3 6.0 %collective-permute-start.114 = (f32[4,8,8,1]{3,2,1,0:T(8,128)S(1)}, f32[4,8,8,1]{3,2,1,0:T(8,128)S(1)}, u32[]{:S(2)}, u32[]{:S(2)}) collective-permute-start(f32[4,8,8,1]{3,2,1,0:T(8,128)S(1)} %get-tuple-element.125), channel_id=1, source_target_pairs={{0,16},{16,32},{32,48},{48,64},{64,80},{80,96},{96,112},{112,128},... | collective-permute-start | bytes 3080 | tf_op jit(solution)/shard_map/ppermute | solution.py:20
  505.7 6.7 %collective-permute-start.117 = (f32[4,8,1,258]{3,1,2,0:T(8,128)S(1)}, f32[4,8,1,258]{3,1,2,0:T(8,128)S(1)}, u32[]{:S(2)}, u32[]{:S(2)}) collective-permute-start(f32[4,8,1,258]{3,1,2,0:T(8,128)S(1)} %copy.1324), channel_id=1, source_target_pairs={{2,0},{4,2},{6,4},{8,6},{10,8},{12,10},{14,12},{0,14},{3,1},{5,3},... | collective-permute-start | bytes 99080 | tf_op jit(solution)/shard_map/ppermute | solution.py:23
  (123 other events, 1672.4 us)
where the time goes:
time: 532 us; the launch traced here: 523 us
  starting transfers between devices  214 us (40%)
  waiting for transfers between devices  155 us (29%)
  local copies, waits for them, and re-layouts  99.4 us (19%)
  other arithmetic  51.9 us (10%)
    ppermute x60, starting transfers between devices, padded_2(): lax.ppermute(lax.slice_in_dim(block, 0, width, axis=dim), axis, backward)  158 us
    ppermute x60, waiting for transfers between devices, padded_2(): lax.ppermute(lax.slice_in_dim(block, block.shape[dim] - width, None, axis...  81.5 us
    ppermute x60, waiting for transfers between devices, padded_2(): lax.ppermute(lax.slice_in_dim(block, 0, width, axis=dim), axis, backward)  73.1 us
    broadcast_in_dim x16, local copies, waits for them, and re-layouts, lookup(): jnp.where(classes[None] == c, table[c][:, None, None, None], jnp.float32(...  63.1 us
    ppermute x60, starting transfers between devices, padded_2(): lax.ppermute(lax.slice_in_dim(block, block.shape[dim] - width, None, axis...  56.1 us
    reduce_sum x3, other arithmetic, coarsen(): return x.reshape(f, d // 2, 2, a // 2, 2, o // 2, 2).mean(axis=(2, 4, 6))  18.7 us
    mul x20, other arithmetic, apply_op(): near = near_fn(sea * u)  12.7 us
  transfers between devices with their start and end apart: 120, of which 106 were waited for; matrix products, arithmetic and copies ran while one was open for 17% of the time, Pallas kernels for 0%

commit v1 on v0

v1 whole, which is shorter than its diff:
```python
import functools

import jax
import jax.numpy as jnp
from jax import lax
from jax.experimental import pallas as pl
from jax.experimental.pallas import tpu as pltpu
from jax.sharding import PartitionSpec as P


FIELDS = 4
CLASSES = 8
OMEGA = 0.8
OWN = 16
HALO = 13
BASE = 14
WIDE = OWN + 2 * BASE
COARSE_WIDE = WIDE // 2
AXES = ("lon", "lat", "dep")
F32 = jnp.float32
VMEM_LIMIT = 48 * 1024 * 1024


def spot(rank):
    return (rank, 0) if rank < 8 else (15 - rank, 1)


def rank_of(lat, dep):
    return lat if dep == 0 else 15 - lat


def device_of(slab):
    block, rank = divmod(slab % 256, 16)
    lat, dep = spot(rank if block % 2 == 0 else 15 - rank)
    return (block * 8 + lat) * 2 + dep


def params():
    return pltpu.CompilerParams(vmem_limit_bytes=VMEM_LIMIT)


def vmem(count):
    return [pl.BlockSpec(memory_space=pltpu.VMEM)] * count


def smem(count):
    return [pl.BlockSpec(memory_space=pltpu.SMEM)] * count


def block_rank(odd, chunk):
    rank = rank_of(chunk // 2, chunk % 2)
    return rank + odd * (15 - 2 * rank)


def pack_kernel(odd_ref, source_ref, sea_ref, classes_ref, out_ref, turned):
    odd = odd_ref[0]
    rows = [source_ref[f].reshape(64, 256) for f in range(FIELDS)]
    rows.append(sea_ref[...].astype(F32).reshape(64, 256))
    rows.append(classes_ref[...].astype(F32).reshape(64, 256))
    for q in range(3):
        pair = jnp.concatenate([rows[2 * q], rows[2 * q + 1]], axis=0)
        for half in range(2):
            turned[q, half * 128 : half * 128 + 128, :] = pair[:, half * 128 : half * 128 + 128].T
    for chunk in range(16):
        at = pl.multiple_of(block_rank(odd, chunk) * 16, 16)
        for q in range(3):
            out_ref[chunk, q * 16 : q * 16 + 16, :] = turned[q, pl.ds(at, 16), :]


def lanes():
    return lax.broadcasted_iota(jnp.int32, (8, 128), 1)


def pick(value, index):
    return jnp.take_along_axis(value, index, axis=1, mode="promise_in_bounds")


def unpack_kernel(in_ref, own_ref, low_ref, high_ref):
    lane = lanes()
    row, depth = lane // 16, lane % 16
    place = (depth % 8) * 8 + row
    upper = depth >= 8
    for o in range(OWN):
        for q in range(3):
            parts = [in_ref[pl.ds(d * 48 + q * 16 + o, 8, stride=96), :] for d in range(2)]
            for half in range(2):
                index = place + 64 * half
                plane = jnp.where(upper, pick(parts[1], index), pick(parts[0], index))
                at = 2 * q + half
                own_ref[o, at] = plane
                if o < HALO:
                    low_ref[o, at] = plane
                if o >= OWN - HALO:
                    high_ref[o - (OWN - HALO), at] = plane


def plane_masks(step):
    lane = lanes()
    row = lax.broadcasted_iota(jnp.int32, (8, 128), 0)
    depth = lane % 16
    return (
        lane < 16 * step,
        row == 7,
        lane >= 128 - 16 * step,
        row == 0,
        jnp.where(depth >= 16 - step, 0.0, 1.0).astype(F32),
        jnp.where(depth < step, 0.0, 1.0).astype(F32),
    )


def plane_near(v, masks, step):
    first, top, last, bottom, keep_up, keep_down = masks
    zero = jnp.zeros_like(v)
    above = jnp.where(first, jnp.where(top, zero, pltpu.roll(v, 7, 0)), v)
    below = jnp.where(last, jnp.where(bottom, zero, pltpu.roll(v, 1, 0)), v)
    total = pltpu.roll(above, 128 - 16 * step, 1) + pltpu.roll(below, 16 * step, 1)
    return total + (pltpu.roll(v, 128 - step, 1) * keep_up + pltpu.roll(v, step, 1) * keep_down)


def stencil(start, stop, u_ref, sea, coupling, masks, step, emit, unroll):
    def load(w):
        u = [u_ref[w, f] for f in range(FIELDS)]
        s = sea(w)
        return u, [s * x for x in u]

    def body(w, carry):
        before, u, v = carry
        u_next, after = load(w + 1)
        for f in range(FIELDS):
            near = (before[f] + after[f]) + plane_near(v[f], masks, step)
            others = [coupling[f][g] * u[g] for g in range(FIELDS) if g != f]
            emit(w, f, u[f], near, others[0] + others[1] + others[2])
        return v, u_next, after

    _, before = load(start - 1)
    u, v = load(start)
    lax.fori_loop(start, stop, body, (before, u, v), unroll=unroll)


def halves(t):
    lane = lanes()
    t = t + jnp.where(lane % 2 == 0, pltpu.roll(t, 127, 1), pltpu.roll(t, 1, 1))
    return t + jnp.where((lane // 16) % 2 == 0, pltpu.roll(t, 112, 1), pltpu.roll(t, 16, 1))


def solve(coupling, fine, coarse, b_sum, u_a, u_b, e_a, e_b, rhs_c):
    gain, size = fine
    gain_c = coarse
    masks, masks_c = plane_masks(1), plane_masks(2)

    def sea(w):
        return gain[w, FIELDS]

    def sea_c(c):
        return gain_c[c, FIELDS]

    def sweep_into(target):
        def emit(w, f, u, near, off):
            target[w, f] = (0.2 * u + b_sum[w, f]) + gain[w, f] * (near - off)

        return emit

    def residual(w, f, u, near, off):
        u_a[w, f] = ((b_sum[w, f] - OMEGA * u) + gain[w, f] * (near - off)) * size[w, f]

    def coarse_into(target):
        def emit(c, f, e, near, off):
            target[c, f] = (0.2 * e + rhs_c[c, f]) + gain_c[c, f] * (0.25 * near - off)

        return emit

    stencil(2, 42, u_a, sea, coupling, masks, 1, sweep_into(u_b), 2)
    stencil(3, 41, u_b, sea, coupling, masks, 1, sweep_into(u_a), 2)

    def residual_b(w, f, u, near, off):
        u_b[w, f] = ((b_sum[w, f] - OMEGA * u) + gain[w, f] * (near - off)) * size[w, f]

    stencil(4, 40, u_a, sea, coupling, masks, 1, residual_b, 2)

    def restrict(c, carry):
        s = sea_c(c)
        for f in range(FIELDS):
            mean = halves(u_b[2 * c, f] + u_b[2 * c + 1, f]) * 0.125
            first = (gain_c[c, f] + (1.0 - s) * OMEGA) * (s * mean)
            rhs_c[c, f] = first
            e_a[c, f] = first
        return carry

    lax.fori_loop(2, 20, restrict, 0, unroll=2)
    stencil(3, 19, e_a, sea_c, coupling, masks_c, 2, coarse_into(e_b), 2)
    stencil(4, 18, e_b, sea_c, coupling, masks_c, 2, coarse_into(e_a), 2)
    stencil(5, 17, e_a, sea_c, coupling, masks_c, 2, coarse_into(e_b), 2)

    def correct(c, carry):
        for f in range(FIELDS):
            e = e_b[c, f]
            for w in (2 * c, 2 * c + 1):
                u_a[w, f] = u_a[w, f] + sea(w) * e
        return carry

    lax.fori_loop(5, 17, correct, 0, unroll=2)
    stencil(12, 32, u_a, sea, coupling, masks, 1, sweep_into(u_b), 2)
    stencil(13, 31, u_b, sea, coupling, masks, 1, sweep_into(u_a), 2)
    stencil(14, 30, u_a, sea, coupling, masks, 1, sweep_into(u_b), 2)


def window(own_ref, low_ref, high_ref, visit):
    for ref, count, first in ((low_ref, HALO, BASE - HALO), (own_ref, OWN, BASE), (high_ref, HALO, BASE + OWN)):

        def body(i, carry, ref=ref, first=first):
            visit(first + i, ref, i)
            return carry

        lax.fori_loop(0, count, body, 0)


def read_coupling(coupling_ref):
    return [[coupling_ref[f, g] for g in range(FIELDS)] for f in range(FIELDS)]


def first_kernel(table_ref, coupling_ref, own_ref, low_ref, high_ref, out_ref, to_low, to_high, gain, size, gain_c,
                 u_a, u_b, e_a, e_b, rhs_c, b_sum):
    coupling = read_coupling(coupling_ref)
    table = [[table_ref[c, f] for f in range(FIELDS)] for c in range(CLASSES)]

    def fine(w, ref, at):
        s = ref[at, 4]
        kind = ref[at, 5]
        gain[w, FIELDS] = s
        hits = [kind == float(c) for c in range(CLASSES)]
        for f in range(FIELDS):
            kappa = jnp.zeros_like(s)
            for c in range(CLASSES):
                kappa = jnp.where(hits[c], table[c][f], kappa)
            diag = s * (kappa + (coupling[f][f] + 6.0)) + (1.0 - s)
            rate = OMEGA / diag
            first = rate * (s * ref[at, f])
            gain[w, f] = s * rate
            size[w, f] = diag * (1.0 / OMEGA)
            b_sum[w, f] = first
            u_a[w, f] = first
            u_b[w, f] = kappa

    window(own_ref, low_ref, high_ref, fine)

    def coarse(c, carry):
        s = jnp.minimum(halves(gain[2 * c, FIELDS] + gain[2 * c + 1, FIELDS]), 1.0)
        gain_c[c, FIELDS] = s
        for f in range(FIELDS):
            kappa = halves(u_b[2 * c, f] + u_b[2 * c + 1, f]) * 0.125
            diag = s * (kappa + (coupling[f][f] + 1.5)) + (1.0 - s)
            gain_c[c, f] = s * (OMEGA / diag)
        return carry

    lax.fori_loop(2, 20, coarse, 0)
    solve(coupling, (gain, size), gain_c, b_sum, u_a, u_b, e_a, e_b, rhs_c)
    for o in range(OWN):
        for f in range(FIELDS):
            plane = u_b[BASE + o, f]
            out_ref[o, f] = plane
            if o < HALO:
                to_low[o, f] = plane
            if o >= OWN - HALO:
                to_high[o - (OWN - HALO), f] = plane


def second_kernel(coupling_ref, own_ref, low_ref, high_ref, gain, size, gain_c, out_ref, u_a, u_b, e_a, e_b, rhs_c, b_sum):
    coupling = read_coupling(coupling_ref)

    def fine(w, ref, at):
        land = (1.0 - gain[w, FIELDS]) * OMEGA
        for f in range(FIELDS):
            first = (gain[w, f] + land) * ref[at, f]
            b_sum[w, f] = first
            u_a[w, f] = first

    window(own_ref, low_ref, high_ref, fine)
    solve(coupling, (gain, size), gain_c, b_sum, u_a, u_b, e_a, e_b, rhs_c)

    lane = lanes()
    place = (lane % 8) * 16 + (lane // 8) % 8
    lower = lane < 64
    for o in range(OWN):
        for k in range(2):
            for q in range(2):
                planes = [own_ref[o, 2 * q + h] if k == 0 else u_b[BASE + o, 2 * q + h] for h in range(2)]
                for d in range(2):
                    index = place + 8 * d
                    rows = jnp.where(lower, pick(planes[0], index), pick(planes[1], index))
                    out_ref[pl.ds(d * 64 + k * 32 + q * 16 + o, 8, stride=128), :] = rows


def finish_kernel(odd_ref, in_ref, first_ref, second_ref, turned):
    odd = odd_ref[0]
    for k, out_ref in enumerate((first_ref, second_ref)):
        for q in range(2):
            for chunk in range(16):
                at = pl.multiple_of(block_rank(odd, chunk) * 16, 16)
                turned[2 * k + q, pl.ds(at, 16), :] = in_ref[chunk, k * 32 + q * 16 : k * 32 + q * 16 + 16, :]
            for half in range(2):
                pair = turned[2 * k + q, half * 128 : half * 128 + 128, :].T
                for h in range(2):
                    out_ref[2 * q + h, :, :, half * 128 : half * 128 + 128] = pair[64 * h : 64 * h + 64].reshape(8, 8, 128)


def planes(count, kinds=FIELDS):
    return jax.ShapeDtypeStruct((count, kinds, 8, 128), F32)


def scratch(count, kinds=FIELDS):
    return pltpu.VMEM((count, kinds, 8, 128), F32)


def per_device(source, sea_mask, classes, kappa_table, coupling):
    odd = (lax.axis_index("lon") % 2).astype(jnp.int32).reshape(1)
    upward = [(device_of(g), device_of(g + 1)) for g in range(256)]
    downward = [(b, a) for a, b in upward]

    sent = pl.pallas_call(
        pack_kernel,
        out_shape=jax.ShapeDtypeStruct((16, 48, 128), F32),
        in_specs=smem(1) + vmem(3),
        out_specs=vmem(1)[0],
        scratch_shapes=[pltpu.VMEM((3, 256, 128), F32)],
        compiler_params=params(),
        name="pack",
    )(odd, source, sea_mask, classes)
    got = lax.all_to_all(sent, ("lat", "dep"), 0, 0, tiled=False)
    own, to_low, to_high = pl.pallas_call(
        unpack_kernel,
        out_shape=(planes(OWN, 6), planes(HALO, 6), planes(HALO, 6)),
        in_specs=vmem(1),
        out_specs=tuple(vmem(3)),
        compiler_params=params(),
        name="unpack",
    )(got.reshape(768, 128))
    low = lax.ppermute(to_high, AXES, upward)
    high = lax.ppermute(to_low, AXES, downward)

    work = [scratch(WIDE), scratch(WIDE), scratch(COARSE_WIDE), scratch(COARSE_WIDE), scratch(COARSE_WIDE), scratch(WIDE)]
    first, to_low, to_high, gain, size, gain_c = pl.pallas_call(
        first_kernel,
        out_shape=(planes(OWN), planes(HALO), planes(HALO), planes(WIDE, 5), planes(WIDE), planes(COARSE_WIDE, 5)),
        in_specs=smem(2) + vmem(3),
        out_specs=tuple(vmem(6)),
        scratch_shapes=work,
        compiler_params=params(),
        name="first",
    )(kappa_table, coupling, own, low, high)
    low = lax.ppermute(to_high, AXES, upward)
    high = lax.ppermute(to_low, AXES, downward)
    sent = pl.pallas_call(
        second_kernel,
        out_shape=jax.ShapeDtypeStruct((1024, 128), F32),
        in_specs=smem(1) + vmem(6),
        out_specs=vmem(1)[0],
        scratch_shapes=work,
        compiler_params=params(),
        name="second",
    )(coupling, first, low, high, gain, size, gain_c)
    got = lax.all_to_all(sent.reshape(16, 64, 128), ("lat", "dep"), 0, 0, tiled=False)
    block = jax.ShapeDtypeStruct((FIELDS, 8, 8, 256), F32)
    return pl.pallas_call(
        finish_kernel,
        out_shape=(block, block),
        in_specs=smem(1) + vmem(1),
        out_specs=tuple(vmem(2)),
        scratch_shapes=[pltpu.VMEM((4, 256, 128), F32)],
        compiler_params=params(),
        name="finish",
    )(odd, got)


def solution(mesh):
    return jax.shard_map(
        per_device,
        mesh=mesh,
        in_specs=(
            P(None, "dep", "lat", "lon"),
            P("dep", "lat", "lon"),
            P("dep", "lat", "lon"),
            P(),
            P(),
        ),
        out_specs=(P(None, "dep", "lat", "lon"), P(None, "dep", "lat", "lon")),
        check_vma=False,
    )
```

time: 532 us -> 90.7 us (0.17); the launches traced: 523 us -> 90.4 us
  starting transfers between devices: 214 us -> 5.63 us
  waiting for transfers between devices: 155 us -> 6.92 us
  local copies, waits for them, and re-layouts: 99.4 us -> 2.78 us
  other arithmetic: 51.9 us -> 0 us
  blocking collectives: 0 us -> 40.8 us
  Pallas kernels: 0 us -> 33.5 us
    ppermute x120 -> x4, starting transfers between devices: 214 us -> 5.63 us  [the longest x2 5.45 us: per_device(): high = lax.ppermute(to_low, AXES, downward)]
    ppermute x120 -> x4, waiting for transfers between devices: 155 us -> 6.92 us  [the longest x2 4.12 us: per_device(): low = lax.ppermute(to_high, AXES, upward)]
    broadcast_in_dim x22 -> x0, local copies, waits for them, and re-layouts: 67.7 us -> none  [the longest x16 63.1 us: lookup(): jnp.where(classes[None] == c, table[c][:, None, None, None], jnp.float32(...]
    all_to_all x0 -> x2, blocking collectives: none -> 40.8 us  [the longest x1 21.9 us: per_device(): lax.all_to_all(sent.reshape(16, 64, 128), ('lat', 'dep'), 0, 0, tiled=False)]
    pallas_call x0 -> x5, Pallas kernels: none -> 33.5 us  [the longest x1 17.4 us: per_device(): pl.pallas_call(first_kernel, out_shape=(planes(OWN), planes(HALO), planes...]
    reduce_sum x4 -> x0, other arithmetic: 21.3 us -> none  [the longest x3 18.7 us: coarsen(): return x.reshape(f, d // 2, 2, a // 2, 2, o // 2, 2).mean(axis=(2, 4, 6))]
    reshape x5 -> x0, local copies, waits for them, and re-layouts: 13.3 us -> none  [the longest x4 7.01 us: prolong(): return jnp.repeat(jnp.repeat(jnp.repeat(e, 2, 1), 2, 2), 2, 3)]
    mul x20 -> x0, other arithmetic: 12.7 us -> none  [apply_op(): near = near_fn(sea * u)]
  transfers between devices with their start and end apart: 120 -> 4, of which waited for: 106 -> 4; matrix products, arithmetic and copies ran while one was open for 17% -> 0% of each run, Pallas kernels for 0% -> 0%
where the time goes in v1:
time: 90.7 us; the launch traced here: 90.4 us
  blocking collectives  40.8 us (45%)
  Pallas kernels  33.5 us (37%)
  waiting for transfers between devices  6.92 us (8%)
  starting transfers between devices  5.63 us (6%)
  local copies, waits for them, and re-layouts  2.78 us (3%)
    all_to_all x1, blocking collectives, per_device(): lax.all_to_all(sent.reshape(16, 64, 128), ('lat', 'dep'), 0, 0, tiled=False)  21.9 us
    all_to_all x1, blocking collectives, per_device(): got = lax.all_to_all(sent, ('lat', 'dep'), 0, 0, tiled=False)  18.9 us
    pallas_call x1, Pallas kernels, per_device(): pl.pallas_call(first_kernel, out_shape=(planes(OWN), planes(HALO), planes...  17.4 us
    pallas_call x1, Pallas kernels, per_device(): pl.pallas_call(second_kernel, out_shape=jax.ShapeDtypeStruct((1024, 128),...  14.5 us
    ppermute x2, starting transfers between devices, per_device(): high = lax.ppermute(to_low, AXES, downward)  5.45 us
    ppermute x2, waiting for transfers between devices, per_device(): low = lax.ppermute(to_high, AXES, upward)  4.12 us
    ppermute x2, waiting for transfers between devices, per_device(): high = lax.ppermute(to_low, AXES, downward)  2.8 us
    unnamed x11, local copies, waits for them, and re-layouts  2.78 us
  transfers between devices with their start and end apart: 4, of which 4 were waited for; matrix products, arithmetic and copies ran while one was open for 0% of the time, Pallas kernels for 0%

profile of v1, /device:TPU:1, one launch (start us, length us, event | category | flops | bytes accessed | tf_op | source)
XLA Modules:
  0.0 90.4 jit_solution(5552456518981180058)
XLA Ops:
  0.6 0.0 copy-start
  0.7 0.9 %copy-done = f32[4,8,8,256]{3,2,1,0:T(8,128)S(1)} copy-done((f32[4,8,8,256]{3,2,1,0:T(8,128)S(1)}, f32[4,8,8,256]{3,2,1,0:T(8,128)}, u32[]{:S(2)}) %copy-start) | copy-done | bytes 262168
  1.6 0.0 copy-start.1
  1.6 0.8 copy-done.1
  2.4 0.0 copy-start.2
  2.4 0.8 copy-done.2
  3.3 0.2 pack.1
  3.5 18.9 %all_to_all.10 = f32[16,48,128]{2,1,0:T(8,128)S(1)} all-to-all(f32[16,48,128]{2,1,0:T(8,128)S(1)} %pack.1), channel_id=1, replica_groups=mesh['lon'=16,'lat'=8,'dep'=2] {'lat','dep'}, dimensions={0} | all-to-all | bytes 786432 | tf_op jit(solution)/shard_map/all_to_all | solution.py:328
  22.4 0.5 unpack.1
  22.9 0.0 copy-start.4
  23.0 0.1 collective-permute-start
  23.1 0.5 collective-permute-start.1
  23.6 0.1 copy-done.4
  23.6 0.0 copy-start.3
  23.6 0.1 copy.7.table_ref
  23.7 3.3 %collective-permute-done.low_ref = f32[13,6,8,128]{3,2,1,0:T(8,128)S(1)} collective-permute-done((f32[13,6,8,128]{3,2,1,0:T(8,128)S(1)}, f32[13,6,8,128]{3,2,1,0:T(8,128)S(1)}, u32[]{:S(2)}, u32[]{:S(2)}) %collective-permute-start) | collective-permute-done | bytes 319520 | tf_op jit(solution)/shard_map/ppermute | solution.py:337
  27.0 2.6 %collective-permute-done.1.high_ref = f32[13,6,8,128]{3,2,1,0:T(8,128)S(1)} collective-permute-done((f32[13,6,8,128]{3,2,1,0:T(8,128)S(1)}, f32[13,6,8,128]{3,2,1,0:T(8,128)S(1)}, u32[]{:S(2)}, u32[]{:S(2)}) %collective-permute-start.1) | collective-permute-done | bytes 319520 | tf_op jit(solution)/shard_map/ppermute | solution.py:338
  29.6 0.0 copy-done.3
  29.6 17.4 %first.1 = (f32[16,4,8,128]{3,2,1,0:T(8,128)S(1)}, f32[13,4,8,128]{3,2,1,0:T(8,128)S(1)}, f32[13,4,8,128]{3,2,1,0:T(8,128)S(1)}, f32[44,5,8,128]{3,2,1,0:T(8,128...) custom-call(f32[8,4]{1,0:T(8,128)S(1)} %copy.7.table_ref, f32[4,4]{1,0:T(4,128)S(1)} %copy-done.3, ...), custom_call_target="tpu_custom_call" | custom-call | tf_op jit(solution)/shard_map/first/pallas_call | solution.py:341
  47.0 0.1 collective-permute-start.2
  47.1 4.9 %collective-permute-start.3 = (f32[13,4,8,128]{3,2,1,0:T(8,128)S(1)}, f32[13,4,8,128]{3,2,1,0:T(8,128)S(1)}, u32[]{:S(2)}, u32[]{:S(2)}) collective-permute-start(f32[13,4,8,128]{3,2,1,0:T(8,128)S(1)} %get-tuple-element.16), channel_id=1, source_target_pairs={{2,0},{4,2},{6,4},{8,6},{10,8},{12,10},{14,12},{15,14},{13,15},{11... | collective-permute-start | bytes 638984 | tf_op jit(solution)/shard_map/ppermute | solution.py:351
  52.0 0.9 collective-permute-done.2.low_ref
  52.9 0.2 collective-permute-done.3.high_ref
  53.1 14.5 %second.1 = f32[1024,128]{1,0:T(8,128)S(1)} custom-call(f32[4,4]{1,0:T(4,128)S(1)} %copy-done.3, f32[16,4,8,128]{3,2,1,0:T(8,128)S(1)} %get-tuple-element.14.own_ref, f32[13,4,8,128]{3,2,1,0:T(8,128)S(1)} %collective-permute-done.2.low_ref, f32[13,4,8,128]{3,2,1,0:T(8,128)S(1)} %collective-permute-done.3.high_ref, ...), custom_call_target="tpu_custom_call" | custom-call | tf_op jit(solution)/shard_map/second/pallas_call | solution.py:352
  67.6 21.9 %all_to_all.11.in_ref = f32[16,64,128]{2,1,0:T(8,128)S(1)} all-to-all(f32[16,64,128]{2,1,0:T(8,128)S(1)} %bitcast.3), channel_id=1, replica_groups=mesh['lon'=16,'lat'=8,'dep'=2] {'lat','dep'}, dimensions={0} | all-to-all | bytes 1048576 | tf_op jit(solution)/shard_map/all_to_all | solution.py:361
  89.4 0.9 %finish.1 = (f32[4,8,8,256]{3,2,1,0:T(8,128)}, f32[4,8,8,256]{3,2,1,0:T(8,128)}) custom-call(s32[1]{0:T(128)} %bitcast.odd_ref, f32[16,64,128]{2,1,0:T(8,128)S(1)} %all_to_all.11.in_ref), custom_call_target="tpu_custom_call" | custom-call | tf_op jit(solution)/shard_map/finish/pallas_call | solution.py:363
Async XLA Ops:
  0.6 1.0 %copy-start = (f32[4,8,8,256]{3,2,1,0:T(8,128)S(1)}, f32[4,8,8,256]{3,2,1,0:T(8,128)}, u32[]{:S(2)}) copy-start(f32[4,8,8,256]{3,2,1,0:T(8,128)} %source_ref.1) | copy-start | bytes 786436
  1.6 0.8 copy-start.1
  2.4 0.8 copy-start.2
  22.9 0.7 copy-start.4
  23.0 4.0 %collective-permute-start = (f32[13,6,8,128]{3,2,1,0:T(8,128)S(1)}, f32[13,6,8,128]{3,2,1,0:T(8,128)S(1)}, u32[]{:S(2)}, u32[]{:S(2)}) collective-permute-start(f32[13,6,8,128]{3,2,1,0:T(8,128)S(1)} %get-tuple-element.12), channel_id=1, source_target_pairs={{0,2},{2,4},{4,6},{6,8},{8,10},{10,12},{12,14},{14,15},{15,13},{13... | collective-permute-start | bytes 958472 | tf_op jit(solution)/shard_map/ppermute | solution.py:337
  23.1 6.5 %collective-permute-start.1 = (f32[13,6,8,128]{3,2,1,0:T(8,128)S(1)}, f32[13,6,8,128]{3,2,1,0:T(8,128)S(1)}, u32[]{:S(2)}, u32[]{:S(2)}) collective-permute-start(f32[13,6,8,128]{3,2,1,0:T(8,128)S(1)} %get-tuple-element.13), channel_id=1, source_target_pairs={{2,0},{4,2},{6,4},{8,6},{10,8},{12,10},{14,12},{15,14},{13,15},{11... | collective-permute-start | bytes 958472 | tf_op jit(solution)/shard_map/ppermute | solution.py:338
  23.6 5.9 %copy-start.3 = (f32[4,4]{1,0:T(4,128)S(1)}, f32[4,4]{1,0:T(4,128)}, u32[]{:S(2)}) copy-start(f32[4,4]{1,0:T(4,128)} %coupling_ref.3) | copy-start | bytes 196
  47.0 5.9 %collective-permute-start.2 = (f32[13,4,8,128]{3,2,1,0:T(8,128)S(1)}, f32[13,4,8,128]{3,2,1,0:T(8,128)S(1)}, u32[]{:S(2)}, u32[]{:S(2)}) collective-permute-start(f32[13,4,8,128]{3,2,1,0:T(8,128)S(1)} %get-tuple-element.15), channel_id=1, source_target_pairs={{0,2},{2,4},{4,6},{6,8},{8,10},{10,12},{12,14},{14,15},{15,13},{13... | collective-permute-start | bytes 638984 | tf_op jit(solution)/shard_map/ppermute | solution.py:350
  47.1 6.0 %collective-permute-start.3 = (f32[13,4,8,128]{3,2,1,0:T(8,128)S(1)}, f32[13,4,8,128]{3,2,1,0:T(8,128)S(1)}, u32[]{:S(2)}, u32[]{:S(2)}) collective-permute-start(f32[13,4,8,128]{3,2,1,0:T(8,128)S(1)} %get-tuple-element.16), channel_id=1, source_target_pairs={{2,0},{4,2},{6,4},{8,6},{10,8},{12,10},{14,12},{15,14},{13,15},{11... | collective-permute-start | bytes 638984 | tf_op jit(solution)/shard_map/ppermute | solution.py:351

commit v2 on v1

--- a/solution.py
+++ b/solution.py
@@ -16,6 +16,7 @@
 BASE = 14
 WIDE = OWN + 2 * BASE
 COARSE_WIDE = WIDE // 2
+UNROLL = (6, 2, 4, 6)
 AXES = ("lon", "lat", "dep")
 F32 = jnp.float32
 VMEM_LIMIT = 48 * 1024 * 1024
@@ -117,24 +118,21 @@
     return total + (pltpu.roll(v, 128 - step, 1) * keep_up + pltpu.roll(v, step, 1) * keep_down)
 
 
-def stencil(start, stop, u_ref, sea, coupling, masks, step, emit, unroll):
+def stencil(start, stop, u_ref, sea, coupling, masks, step, emit):
     def load(w):
         u = [u_ref[w, f] for f in range(FIELDS)]
         s = sea(w)
         return u, [s * x for x in u]
 
-    def body(w, carry):
-        before, u, v = carry
+    _, before = load(start - 1)
+    u, v = load(start)
+    for w in range(start, stop):
         u_next, after = load(w + 1)
         for f in range(FIELDS):
             near = (before[f] + after[f]) + plane_near(v[f], masks, step)
             others = [coupling[f][g] * u[g] for g in range(FIELDS) if g != f]
             emit(w, f, u[f], near, others[0] + others[1] + others[2])
-        return v, u_next, after
-
-    _, before = load(start - 1)
-    u, v = load(start)
-    lax.fori_loop(start, stop, body, (before, u, v), unroll=unroll)
+        before, u, v = v, u_next, after
 
 
 def halves(t):
@@ -160,22 +158,19 @@
 
         return emit
 
-    def residual(w, f, u, near, off):
-        u_a[w, f] = ((b_sum[w, f] - OMEGA * u) + gain[w, f] * (near - off)) * size[w, f]
-
     def coarse_into(target):
         def emit(c, f, e, near, off):
             target[c, f] = (0.2 * e + rhs_c[c, f]) + gain_c[c, f] * (0.25 * near - off)
 
         return emit
 
-    stencil(2, 42, u_a, sea, coupling, masks, 1, sweep_into(u_b), 2)
-    stencil(3, 41, u_b, sea, coupling, masks, 1, sweep_into(u_a), 2)
-
-    def residual_b(w, f, u, near, off):
+    stencil(2, 42, u_a, sea, coupling, masks, 1, sweep_into(u_b))
+    stencil(3, 41, u_b, sea, coupling, masks, 1, sweep_into(u_a))
+
+    def residual(w, f, u, near, off):
         u_b[w, f] = ((b_sum[w, f] - OMEGA * u) + gain[w, f] * (near - off)) * size[w, f]
 
-    stencil(4, 40, u_a, sea, coupling, masks, 1, residual_b, 2)
+    stencil(4, 40, u_a, sea, coupling, masks, 1, residual)
 
     def restrict(c, carry):
         s = sea_c(c)
@@ -186,10 +181,10 @@
             e_a[c, f] = first
         return carry
 
-    lax.fori_loop(2, 20, restrict, 0, unroll=2)
-    stencil(3, 19, e_a, sea_c, coupling, masks_c, 2, coarse_into(e_b), 2)
-    stencil(4, 18, e_b, sea_c, coupling, masks_c, 2, coarse_into(e_a), 2)
-    stencil(5, 17, e_a, sea_c, coupling, masks_c, 2, coarse_into(e_b), 2)
+    lax.fori_loop(2, 20, restrict, 0, unroll=UNROLL[0])
+    stencil(3, 19, e_a, sea_c, coupling, masks_c, 2, coarse_into(e_b))
+    stencil(4, 18, e_b, sea_c, coupling, masks_c, 2, coarse_into(e_a))
+    stencil(5, 17, e_a, sea_c, coupling, masks_c, 2, coarse_into(e_b))
 
     def correct(c, carry):
         for f in range(FIELDS):
@@ -198,10 +193,10 @@
                 u_a[w, f] = u_a[w, f] + sea(w) * e
         return carry
 
-    lax.fori_loop(5, 17, correct, 0, unroll=2)
-    stencil(12, 32, u_a, sea, coupling, masks, 1, sweep_into(u_b), 2)
-    stencil(13, 31, u_b, sea, coupling, masks, 1, sweep_into(u_a), 2)
-    stencil(14, 30, u_a, sea, coupling, masks, 1, sweep_into(u_b), 2)
+    lax.fori_loop(5, 17, correct, 0, unroll=UNROLL[1])
+    stencil(12, 32, u_a, sea, coupling, masks, 1, sweep_into(u_b))
+    stencil(13, 31, u_b, sea, coupling, masks, 1, sweep_into(u_a))
+    stencil(14, 30, u_a, sea, coupling, masks, 1, sweep_into(u_b))
 
 
 def window(own_ref, low_ref, high_ref, visit):
@@ -211,7 +206,7 @@
             visit(first + i, ref, i)
             return carry
 
-        lax.fori_loop(0, count, body, 0)
+        lax.fori_loop(0, count, body, 0, unroll=UNROLL[2])
 
 
 def read_coupling(coupling_ref):
@@ -252,7 +247,7 @@
             gain_c[c, f] = s * (OMEGA / diag)
         return carry
 
-    lax.fori_loop(2, 20, coarse, 0)
+    lax.fori_loop(2, 20, coarse, 0, unroll=UNROLL[3])
     solve(coupling, (gain, size), gain_c, b_sum, u_a, u_b, e_a, e_b, rhs_c)
     for o in range(OWN):
         for f in range(FIELDS):

time: 90.7 us -> 71.1 us (0.78)
  Pallas kernels: 33.5 us -> 14 us
    pallas_call x1, Pallas kernels: 17.4 us -> 6.45 us  [per_device(): pl.pallas_call(first_kernel, out_shape=(planes(OWN), planes(HALO), planes...]
    pallas_call x1, Pallas kernels: 14.5 us -> 5.84 us  [per_device(): pl.pallas_call(second_kernel, out_shape=jax.ShapeDtypeStruct((1024, 128),...]
where the time goes in v2:
time: 71.1 us; the launch traced here: 70.8 us
  blocking collectives  40.6 us (57%)
  Pallas kernels  14 us (20%)
  waiting for transfers between devices  6.92 us (10%)
  starting transfers between devices  5.81 us (8%)
  local copies, waits for them, and re-layouts  2.78 us (4%)
    all_to_all x1, blocking collectives, per_device(): lax.all_to_all(sent.reshape(16, 64, 128), ('lat', 'dep'), 0, 0, tiled=False)  21.7 us
    all_to_all x1, blocking collectives, per_device(): got = lax.all_to_all(sent, ('lat', 'dep'), 0, 0, tiled=False)  18.9 us
    pallas_call x1, Pallas kernels, per_device(): pl.pallas_call(first_kernel, out_shape=(planes(OWN), planes(HALO), planes...  6.45 us
    pallas_call x1, Pallas kernels, per_device(): pl.pallas_call(second_kernel, out_shape=jax.ShapeDtypeStruct((1024, 128),...  5.84 us
    ppermute x2, starting transfers between devices, per_device(): high = lax.ppermute(to_low, AXES, downward)  5.63 us
    ppermute x2, waiting for transfers between devices, per_device(): low = lax.ppermute(to_high, AXES, upward)  3.94 us
    ppermute x2, waiting for transfers between devices, per_device(): high = lax.ppermute(to_low, AXES, downward)  2.98 us
    unnamed x11, local copies, waits for them, and re-layouts  2.78 us
  transfers between devices with their start and end apart: 4, of which 4 were waited for; matrix products, arithmetic and copies ran while one was open for 0% of the time, Pallas kernels for 0%

profile of v2, /device:TPU:1, one launch (start us, length us, event | category | flops | bytes accessed | tf_op | source)
XLA Modules:
  0.0 70.8 jit_solution(1682590438178305363)
XLA Ops:
  0.6 0.0 copy-start
  0.7 0.9 %copy-done = f32[4,8,8,256]{3,2,1,0:T(8,128)S(1)} copy-done((f32[4,8,8,256]{3,2,1,0:T(8,128)S(1)}, f32[4,8,8,256]{3,2,1,0:T(8,128)}, u32[]{:S(2)}) %copy-start) | copy-done | bytes 262168
  1.6 0.0 copy-start.1
  1.6 0.8 %copy-done.1 = s32[8,8,256]{2,1,0:T(8,128)S(1)} copy-done((s32[8,8,256]{2,1,0:T(8,128)S(1)}, s32[8,8,256]{2,1,0:T(8,128)}, u32[]{:S(2)}) %copy-start.1) | copy-done | bytes 65560
  2.4 0.0 copy-start.2
  2.4 0.8 %copy-done.2 = s32[8,8,256]{2,1,0:T(8,128)S(1)} copy-done((s32[8,8,256]{2,1,0:T(8,128)S(1)}, s32[8,8,256]{2,1,0:T(8,128)}, u32[]{:S(2)}) %copy-start.2) | copy-done | bytes 65560
  3.3 0.2 pack.1
  3.5 18.9 %all_to_all.10 = f32[16,48,128]{2,1,0:T(8,128)S(1)} all-to-all(f32[16,48,128]{2,1,0:T(8,128)S(1)} %pack.1), channel_id=1, replica_groups=mesh['lon'=16,'lat'=8,'dep'=2] {'lat','dep'}, dimensions={0} | all-to-all | bytes 786432 | tf_op jit(solution)/shard_map/all_to_all | solution.py:323
  22.4 0.5 unpack.1
  22.9 0.0 copy-start.4
  23.0 0.1 collective-permute-start
  23.1 0.5 collective-permute-start.1
  23.6 0.1 copy-done.4
  23.6 0.0 copy-start.3
  23.6 0.1 copy.7.table_ref
  23.7 3.3 %collective-permute-done.low_ref = f32[13,6,8,128]{3,2,1,0:T(8,128)S(1)} collective-permute-done((f32[13,6,8,128]{3,2,1,0:T(8,128)S(1)}, f32[13,6,8,128]{3,2,1,0:T(8,128)S(1)}, u32[]{:S(2)}, u32[]{:S(2)}) %collective-permute-start) | collective-permute-done | bytes 319520 | tf_op jit(solution)/shard_map/ppermute | solution.py:332
  27.0 2.6 %collective-permute-done.1.high_ref = f32[13,6,8,128]{3,2,1,0:T(8,128)S(1)} collective-permute-done((f32[13,6,8,128]{3,2,1,0:T(8,128)S(1)}, f32[13,6,8,128]{3,2,1,0:T(8,128)S(1)}, u32[]{:S(2)}, u32[]{:S(2)}) %collective-permute-start.1) | collective-permute-done | bytes 319520 | tf_op jit(solution)/shard_map/ppermute | solution.py:333
  29.6 0.0 copy-done.3
  29.6 6.5 %first.1 = (f32[16,4,8,128]{3,2,1,0:T(8,128)S(1)}, f32[13,4,8,128]{3,2,1,0:T(8,128)S(1)}, f32[13,4,8,128]{3,2,1,0:T(8,128)S(1)}, f32[44,5,8,128]{3,2,1,0:T(8,128...) custom-call(f32[8,4]{1,0:T(8,128)S(1)} %copy.7.table_ref, f32[4,4]{1,0:T(4,128)S(1)} %copy-done.3, ...), custom_call_target="tpu_custom_call" | custom-call | tf_op jit(solution)/shard_map/first/pallas_call | solution.py:336
  36.0 0.1 collective-permute-start.2
  36.1 5.1 %collective-permute-start.3 = (f32[13,4,8,128]{3,2,1,0:T(8,128)S(1)}, f32[13,4,8,128]{3,2,1,0:T(8,128)S(1)}, u32[]{:S(2)}, u32[]{:S(2)}) collective-permute-start(f32[13,4,8,128]{3,2,1,0:T(8,128)S(1)} %get-tuple-element.16), channel_id=1, source_target_pairs={{2,0},{4,2},{6,4},{8,6},{10,8},{12,10},{14,12},{15,14},{13,15},{11... | collective-permute-start | bytes 638984 | tf_op jit(solution)/shard_map/ppermute | solution.py:346
  41.2 0.7 collective-permute-done.2.low_ref
  41.9 0.4 collective-permute-done.3.high_ref
  42.3 5.8 %second.1 = f32[1024,128]{1,0:T(8,128)S(1)} custom-call(f32[4,4]{1,0:T(4,128)S(1)} %copy-done.3, f32[16,4,8,128]{3,2,1,0:T(8,128)S(1)} %get-tuple-element.14.own_ref, f32[13,4,8,128]{3,2,1,0:T(8,128)S(1)} %collective-permute-done.2.low_ref, f32[13,4,8,128]{3,2,1,0:T(8,128)S(1)} %collective-permute-done.3.high_ref, ...), custom_call_target="tpu_custom_call" | custom-call | tf_op jit(solution)/shard_map/second/pallas_call | solution.py:347
  48.2 21.7 %all_to_all.11.in_ref = f32[16,64,128]{2,1,0:T(8,128)S(1)} all-to-all(f32[16,64,128]{2,1,0:T(8,128)S(1)} %bitcast.3), channel_id=1, replica_groups=mesh['lon'=16,'lat'=8,'dep'=2] {'lat','dep'}, dimensions={0} | all-to-all | bytes 1048576 | tf_op jit(solution)/shard_map/all_to_all | solution.py:356
  69.9 0.9 %finish.1 = (f32[4,8,8,256]{3,2,1,0:T(8,128)}, f32[4,8,8,256]{3,2,1,0:T(8,128)}) custom-call(s32[1]{0:T(128)} %bitcast.odd_ref, f32[16,64,128]{2,1,0:T(8,128)S(1)} %all_to_all.11.in_ref), custom_call_target="tpu_custom_call" | custom-call | tf_op jit(solution)/shard_map/finish/pallas_call | solution.py:358
Async XLA Ops:
  0.6 1.0 %copy-start = (f32[4,8,8,256]{3,2,1,0:T(8,128)S(1)}, f32[4,8,8,256]{3,2,1,0:T(8,128)}, u32[]{:S(2)}) copy-start(f32[4,8,8,256]{3,2,1,0:T(8,128)} %source_ref.1) | copy-start | bytes 786436
  1.6 0.8 %copy-start.1 = (s32[8,8,256]{2,1,0:T(8,128)S(1)}, s32[8,8,256]{2,1,0:T(8,128)}, u32[]{:S(2)}) copy-start(s32[8,8,256]{2,1,0:T(8,128)} %sea_ref.1) | copy-start | bytes 196612
  2.4 0.8 %copy-start.2 = (s32[8,8,256]{2,1,0:T(8,128)S(1)}, s32[8,8,256]{2,1,0:T(8,128)}, u32[]{:S(2)}) copy-start(s32[8,8,256]{2,1,0:T(8,128)} %classes_ref.1) | copy-start | bytes 196612
  22.9 0.7 copy-start.4
  23.0 4.0 %collective-permute-start = (f32[13,6,8,128]{3,2,1,0:T(8,128)S(1)}, f32[13,6,8,128]{3,2,1,0:T(8,128)S(1)}, u32[]{:S(2)}, u32[]{:S(2)}) collective-permute-start(f32[13,6,8,128]{3,2,1,0:T(8,128)S(1)} %get-tuple-element.12), channel_id=1, source_target_pairs={{0,2},{2,4},{4,6},{6,8},{8,10},{10,12},{12,14},{14,15},{15,13},{13... | collective-permute-start | bytes 958472 | tf_op jit(solution)/shard_map/ppermute | solution.py:332
  23.1 6.5 %collective-permute-start.1 = (f32[13,6,8,128]{3,2,1,0:T(8,128)S(1)}, f32[13,6,8,128]{3,2,1,0:T(8,128)S(1)}, u32[]{:S(2)}, u32[]{:S(2)}) collective-permute-start(f32[13,6,8,128]{3,2,1,0:T(8,128)S(1)} %get-tuple-element.13), channel_id=1, source_target_pairs={{2,0},{4,2},{6,4},{8,6},{10,8},{12,10},{14,12},{15,14},{13,15},{11... | collective-permute-start | bytes 958472 | tf_op jit(solution)/shard_map/ppermute | solution.py:333
  23.6 5.9 %copy-start.3 = (f32[4,4]{1,0:T(4,128)S(1)}, f32[4,4]{1,0:T(4,128)}, u32[]{:S(2)}) copy-start(f32[4,4]{1,0:T(4,128)} %coupling_ref.3) | copy-start | bytes 196
  36.0 5.9 %collective-permute-start.2 = (f32[13,4,8,128]{3,2,1,0:T(8,128)S(1)}, f32[13,4,8,128]{3,2,1,0:T(8,128)S(1)}, u32[]{:S(2)}, u32[]{:S(2)}) collective-permute-start(f32[13,4,8,128]{3,2,1,0:T(8,128)S(1)} %get-tuple-element.15), channel_id=1, source_target_pairs={{0,2},{2,4},{4,6},{6,8},{8,10},{10,12},{12,14},{14,15},{15,13},{13... | collective-permute-start | bytes 638984 | tf_op jit(solution)/shard_map/ppermute | solution.py:345
  36.1 6.2 %collective-permute-start.3 = (f32[13,4,8,128]{3,2,1,0:T(8,128)S(1)}, f32[13,4,8,128]{3,2,1,0:T(8,128)S(1)}, u32[]{:S(2)}, u32[]{:S(2)}) collective-permute-start(f32[13,4,8,128]{3,2,1,0:T(8,128)S(1)} %get-tuple-element.16), channel_id=1, source_target_pairs={{2,0},{4,2},{6,4},{8,6},{10,8},{12,10},{14,12},{15,14},{13,15},{11... | collective-permute-start | bytes 638984 | tf_op jit(solution)/shard_map/ppermute | solution.py:346

commit v3 on v2

--- a/solution.py
+++ b/solution.py
@@ -16,23 +16,28 @@
 BASE = 14
 WIDE = OWN + 2 * BASE
 COARSE_WIDE = WIDE // 2
-UNROLL = (6, 2, 4, 6)
+UNROLL = (6, 2, 4, 5, 4)
 AXES = ("lon", "lat", "dep")
 F32 = jnp.float32
 VMEM_LIMIT = 48 * 1024 * 1024
 
 
-def spot(rank):
-    return (rank, 0) if rank < 8 else (15 - rank, 1)
-
-
-def rank_of(lat, dep):
-    return lat if dep == 0 else 15 - lat
+PATHS = (
+    ((3, 1), (2, 1), (1, 1), (0, 1), (0, 0), (1, 0), (2, 0), (3, 0)),
+    ((3, 1), (2, 1), (1, 1), (0, 1), (0, 0), (1, 0), (2, 0), (3, 0)),
+)
+
+
+def spots(path):
+    return [(2 * x + core, dep) for x, dep in path for core in ((0, 1) if dep else (1, 0))]
+
+
+PLACES = [spots(path) for path in PATHS]
 
 
 def device_of(slab):
     block, rank = divmod(slab % 256, 16)
-    lat, dep = spot(rank if block % 2 == 0 else 15 - rank)
+    lat, dep = PLACES[block // 8][rank if block % 2 == 0 else 15 - rank]
     return (block * 8 + lat) * 2 + dep
 
 
@@ -48,22 +53,21 @@
     return [pl.BlockSpec(memory_space=pltpu.SMEM)] * count
 
 
-def block_rank(odd, chunk):
-    rank = rank_of(chunk // 2, chunk % 2)
+def block_rank(block, chunk):
+    low, high = (places.index((chunk // 2, chunk % 2)) for places in PLACES)
+    rank = low if low == high else jnp.where(block < 8, low, high)
+    odd = lax.rem(block, 2)
     return rank + odd * (15 - 2 * rank)
 
 
-def pack_kernel(odd_ref, source_ref, sea_ref, classes_ref, out_ref, turned):
-    odd = odd_ref[0]
-    rows = [source_ref[f].reshape(64, 256) for f in range(FIELDS)]
-    rows.append(sea_ref[...].astype(F32).reshape(64, 256))
-    rows.append(classes_ref[...].astype(F32).reshape(64, 256))
+def pack_kernel(block_ref, rows_ref, out_ref, turned):
+    block = block_ref[0]
     for q in range(3):
-        pair = jnp.concatenate([rows[2 * q], rows[2 * q + 1]], axis=0)
         for half in range(2):
-            turned[q, half * 128 : half * 128 + 128, :] = pair[:, half * 128 : half * 128 + 128].T
+            tile = rows_ref[128 * q : 128 * q + 128, half * 128 : half * 128 + 128]
+            turned[q, half * 128 : half * 128 + 128, :] = tile.T
     for chunk in range(16):
-        at = pl.multiple_of(block_rank(odd, chunk) * 16, 16)
+        at = pl.multiple_of(block_rank(block, chunk) * 16, 16)
         for q in range(3):
             out_ref[chunk, q * 16 : q * 16 + 16, :] = turned[q, pl.ds(at, 16), :]
 
@@ -141,16 +145,12 @@
     return t + jnp.where((lane // 16) % 2 == 0, pltpu.roll(t, 112, 1), pltpu.roll(t, 16, 1))
 
 
-def solve(coupling, fine, coarse, b_sum, u_a, u_b, e_a, e_b, rhs_c):
-    gain, size = fine
-    gain_c = coarse
-    masks, masks_c = plane_masks(1), plane_masks(2)
+def fine_passes(coupling, coeffs, u_a, u_b):
+    gain, size, b_sum = coeffs
+    masks = plane_masks(1)
 
     def sea(w):
         return gain[w, FIELDS]
-
-    def sea_c(c):
-        return gain_c[c, FIELDS]
 
     def sweep_into(target):
         def emit(w, f, u, near, off):
@@ -158,19 +158,43 @@
 
         return emit
 
+    def residual(w, f, u, near, off):
+        u_b[w, f] = ((b_sum[w, f] - OMEGA * u) + gain[w, f] * (near - off)) * size[w, f]
+
+    def a_to_b(start, stop):
+        stencil(start, stop, u_a, sea, coupling, masks, 1, sweep_into(u_b))
+
+    def b_to_a(start, stop):
+        stencil(start, stop, u_b, sea, coupling, masks, 1, sweep_into(u_a))
+
+    def rest(start, stop):
+        stencil(start, stop, u_a, sea, coupling, masks, 1, residual)
+
+    return a_to_b, b_to_a, rest
+
+
+def inner_passes(coupling, coeffs, u_a, u_b):
+    for turn, one in enumerate(fine_passes(coupling, coeffs, u_a, u_b)):
+        one(BASE + 1 + turn, BASE + OWN - 1 - turn)
+
+
+def solve(coupling, coeffs, gain_c, u_a, u_b, e_a, e_b, rhs_c):
+    gain = coeffs[0]
+    passes = fine_passes(coupling, coeffs, u_a, u_b)
+    for turn, one in enumerate(passes):
+        one(BASE - HALO + 1 + turn, BASE + 1 + turn)
+        one(BASE + OWN - 1 - turn, BASE + OWN + HALO - 1 - turn)
+
+    masks_c = plane_masks(2)
+
+    def sea_c(c):
+        return gain_c[c, FIELDS]
+
     def coarse_into(target):
         def emit(c, f, e, near, off):
             target[c, f] = (0.2 * e + rhs_c[c, f]) + gain_c[c, f] * (0.25 * near - off)
 
         return emit
-
-    stencil(2, 42, u_a, sea, coupling, masks, 1, sweep_into(u_b))
-    stencil(3, 41, u_b, sea, coupling, masks, 1, sweep_into(u_a))
-
-    def residual(w, f, u, near, off):
-        u_b[w, f] = ((b_sum[w, f] - OMEGA * u) + gain[w, f] * (near - off)) * size[w, f]
-
-    stencil(4, 40, u_a, sea, coupling, masks, 1, residual)
 
     def restrict(c, carry):
         s = sea_c(c)
@@ -190,35 +214,31 @@
         for f in range(FIELDS):
             e = e_b[c, f]
             for w in (2 * c, 2 * c + 1):
-                u_a[w, f] = u_a[w, f] + sea(w) * e
+                u_a[w, f] = u_a[w, f] + gain[w, FIELDS] * e
         return carry
 
     lax.fori_loop(5, 17, correct, 0, unroll=UNROLL[1])
-    stencil(12, 32, u_a, sea, coupling, masks, 1, sweep_into(u_b))
-    stencil(13, 31, u_b, sea, coupling, masks, 1, sweep_into(u_a))
-    stencil(14, 30, u_a, sea, coupling, masks, 1, sweep_into(u_b))
-
-
-def window(own_ref, low_ref, high_ref, visit):
-    for ref, count, first in ((low_ref, HALO, BASE - HALO), (own_ref, OWN, BASE), (high_ref, HALO, BASE + OWN)):
-
-        def body(i, carry, ref=ref, first=first):
-            visit(first + i, ref, i)
-            return carry
-
-        lax.fori_loop(0, count, body, 0, unroll=UNROLL[2])
+    passes[0](12, 32)
+    passes[1](13, 31)
+    passes[0](14, 30)
+
+
+def each_plane(ref, count, first, visit, unroll):
+    def body(i, carry):
+        visit(first + i, ref, i)
+        return carry
+
+    lax.fori_loop(0, count, body, 0, unroll=unroll)
 
 
 def read_coupling(coupling_ref):
     return [[coupling_ref[f, g] for g in range(FIELDS)] for f in range(FIELDS)]
 
 
-def first_kernel(table_ref, coupling_ref, own_ref, low_ref, high_ref, out_ref, to_low, to_high, gain, size, gain_c,
-                 u_a, u_b, e_a, e_b, rhs_c, b_sum):
-    coupling = read_coupling(coupling_ref)
-    table = [[table_ref[c, f] for f in range(FIELDS)] for c in range(CLASSES)]
-
-    def fine(w, ref, at):
+def fine_coefficients(table, coupling, coeffs, u_a, kappas):
+    gain, size, b_sum = coeffs
+
+    def visit(w, ref, at):
         s = ref[at, 4]
         kind = ref[at, 5]
         gain[w, FIELDS] = s
@@ -234,43 +254,75 @@
             size[w, f] = diag * (1.0 / OMEGA)
             b_sum[w, f] = first
             u_a[w, f] = first
-            u_b[w, f] = kappa
-
-    window(own_ref, low_ref, high_ref, fine)
-
-    def coarse(c, carry):
+            kappas[w, f] = kappa
+
+    return visit
+
+
+def coarse_coefficients(coupling, gain, gain_c, kappas):
+    def visit(c, carry):
         s = jnp.minimum(halves(gain[2 * c, FIELDS] + gain[2 * c + 1, FIELDS]), 1.0)
         gain_c[c, FIELDS] = s
         for f in range(FIELDS):
-            kappa = halves(u_b[2 * c, f] + u_b[2 * c + 1, f]) * 0.125
+            kappa = halves(kappas[2 * c, f] + kappas[2 * c + 1, f]) * 0.125
             diag = s * (kappa + (coupling[f][f] + 1.5)) + (1.0 - s)
             gain_c[c, f] = s * (OMEGA / diag)
         return carry
 
-    lax.fori_loop(2, 20, coarse, 0, unroll=UNROLL[3])
-    solve(coupling, (gain, size), gain_c, b_sum, u_a, u_b, e_a, e_b, rhs_c)
-    for o in range(OWN):
-        for f in range(FIELDS):
-            plane = u_b[BASE + o, f]
-            out_ref[o, f] = plane
-            if o < HALO:
-                to_low[o, f] = plane
-            if o >= OWN - HALO:
-                to_high[o - (OWN - HALO), f] = plane
-
-
-def second_kernel(coupling_ref, own_ref, low_ref, high_ref, gain, size, gain_c, out_ref, u_a, u_b, e_a, e_b, rhs_c, b_sum):
+    return visit
+
+
+def inner_first_kernel(table_ref, coupling_ref, own_ref, gain, size, b_sum, gain_c, u_a, u_b):
     coupling = read_coupling(coupling_ref)
-
-    def fine(w, ref, at):
+    table = [[table_ref[c, f] for f in range(FIELDS)] for c in range(CLASSES)]
+    coeffs = (gain, size, b_sum)
+    each_plane(own_ref, OWN, BASE, fine_coefficients(table, coupling, coeffs, u_a, u_b), UNROLL[2])
+    lax.fori_loop(7, 15, coarse_coefficients(coupling, gain, gain_c, u_b), 0, unroll=UNROLL[4])
+    inner_passes(coupling, coeffs, u_a, u_b)
+
+
+def first_kernel(table_ref, coupling_ref, low_ref, high_ref, *refs):
+    gain, size, b_sum, gain_c, u_a, u_b, out_ref, to_low, to_high, e_a, e_b, rhs_c, kappas = refs[6:]
+    coupling = read_coupling(coupling_ref)
+    table = [[table_ref[c, f] for f in range(FIELDS)] for c in range(CLASSES)]
+    coeffs = (gain, size, b_sum)
+    visit = fine_coefficients(table, coupling, coeffs, u_a, kappas)
+    each_plane(low_ref, HALO, BASE - HALO, visit, UNROLL[2])
+    each_plane(high_ref, HALO, BASE + OWN, visit, UNROLL[2])
+    visit = coarse_coefficients(coupling, gain, gain_c, kappas)
+    lax.fori_loop(0, 10, lambda i, carry: visit(i + jnp.where(i < 5, 2, 10), carry), 0, unroll=UNROLL[3])
+    solve(coupling, coeffs, gain_c, u_a, u_b, e_a, e_b, rhs_c)
+    out_ref[...] = u_b[BASE : BASE + OWN]
+    to_low[...] = u_b[BASE : BASE + HALO]
+    to_high[...] = u_b[BASE + OWN - HALO : BASE + OWN]
+
+
+def second_start(coeffs, u_a):
+    gain, _, b_sum = coeffs
+
+    def visit(w, ref, at):
         land = (1.0 - gain[w, FIELDS]) * OMEGA
         for f in range(FIELDS):
             first = (gain[w, f] + land) * ref[at, f]
             b_sum[w, f] = first
             u_a[w, f] = first
 
-    window(own_ref, low_ref, high_ref, fine)
-    solve(coupling, (gain, size), gain_c, b_sum, u_a, u_b, e_a, e_b, rhs_c)
+    return visit
+
+
+def inner_second_kernel(coupling_ref, own_ref, gain, size, b_sum, u_a, u_b):
+    coeffs = (gain, size, b_sum)
+    each_plane(own_ref, OWN, BASE, second_start(coeffs, u_a), UNROLL[2])
+    inner_passes(read_coupling(coupling_ref), coeffs, u_a, u_b)
+
+
+def second_kernel(coupling_ref, own_ref, low_ref, high_ref, gain, size, gain_c, *refs):
+    b_sum, u_a, u_b, out_ref, e_a, e_b, rhs_c = refs[3:]
+    coupling = read_coupling(coupling_ref)
+    coeffs = (gain, size, b_sum)
+    each_plane(low_ref, HALO, BASE - HALO, second_start(coeffs, u_a), UNROLL[2])
+    each_plane(high_ref, HALO, BASE + OWN, second_start(coeffs, u_a), UNROLL[2])
+    solve(coupling, coeffs, gain_c, u_a, u_b, e_a, e_b, rhs_c)
 
     lane = lanes()
     place = (lane % 8) * 16 + (lane // 8) % 8
@@ -285,12 +337,12 @@
                     out_ref[pl.ds(d * 64 + k * 32 + q * 16 + o, 8, stride=128), :] = rows
 
 
-def finish_kernel(odd_ref, in_ref, first_ref, second_ref, turned):
-    odd = odd_ref[0]
+def finish_kernel(block_ref, in_ref, first_ref, second_ref, turned):
+    block = block_ref[0]
     for k, out_ref in enumerate((first_ref, second_ref)):
         for q in range(2):
             for chunk in range(16):
-                at = pl.multiple_of(block_rank(odd, chunk) * 16, 16)
+                at = pl.multiple_of(block_rank(block, chunk) * 16, 16)
                 turned[2 * k + q, pl.ds(at, 16), :] = in_ref[chunk, k * 32 + q * 16 : k * 32 + q * 16 + 16, :]
             for half in range(2):
                 pair = turned[2 * k + q, half * 128 : half * 128 + 128, :].T
@@ -307,19 +359,19 @@
 
 
 def per_device(source, sea_mask, classes, kappa_table, coupling):
-    odd = (lax.axis_index("lon") % 2).astype(jnp.int32).reshape(1)
+    block = lax.axis_index("lon").astype(jnp.int32).reshape(1)
     upward = [(device_of(g), device_of(g + 1)) for g in range(256)]
     downward = [(b, a) for a, b in upward]
 
     sent = pl.pallas_call(
         pack_kernel,
         out_shape=jax.ShapeDtypeStruct((16, 48, 128), F32),
-        in_specs=smem(1) + vmem(3),
+        in_specs=smem(1) + vmem(1),
         out_specs=vmem(1)[0],
         scratch_shapes=[pltpu.VMEM((3, 256, 128), F32)],
         compiler_params=params(),
         name="pack",
-    )(odd, source, sea_mask, classes)
+    )(block, jnp.concatenate([x.astype(F32).reshape(-1, 256) for x in (source, sea_mask, classes)]))
     got = lax.all_to_all(sent, ("lat", "dep"), 0, 0, tiled=False)
     own, to_low, to_high = pl.pallas_call(
         unpack_kernel,
@@ -332,38 +384,62 @@
     low = lax.ppermute(to_high, AXES, upward)
     high = lax.ppermute(to_low, AXES, downward)
 
-    work = [scratch(WIDE), scratch(WIDE), scratch(COARSE_WIDE), scratch(COARSE_WIDE), scratch(COARSE_WIDE), scratch(WIDE)]
-    first, to_low, to_high, gain, size, gain_c = pl.pallas_call(
+    cost = pl.CostEstimate(flops=40_000_000, bytes_accessed=8_000_000, transcendentals=0)
+    coarse = [scratch(COARSE_WIDE)] * 3
+    state = (planes(WIDE, 5), planes(WIDE), planes(WIDE), planes(COARSE_WIDE, 5), planes(WIDE), planes(WIDE))
+    state = pl.pallas_call(
+        inner_first_kernel,
+        out_shape=state,
+        in_specs=smem(2) + vmem(1),
+        out_specs=tuple(vmem(6)),
+        compiler_params=params(),
+        cost_estimate=cost,
+        name="inner_first",
+    )(kappa_table, coupling, own)
+    gain, size, _, gain_c, _, _, first, to_low, to_high = pl.pallas_call(
         first_kernel,
-        out_shape=(planes(OWN), planes(HALO), planes(HALO), planes(WIDE, 5), planes(WIDE), planes(COARSE_WIDE, 5)),
-        in_specs=smem(2) + vmem(3),
-        out_specs=tuple(vmem(6)),
-        scratch_shapes=work,
-        compiler_params=params(),
+        out_shape=tuple(state) + (planes(OWN), planes(HALO), planes(HALO)),
+        in_specs=smem(2) + vmem(8),
+        out_specs=tuple(vmem(9)),
+        scratch_shapes=coarse + [scratch(WIDE)],
+        input_output_aliases={4 + i: i for i in range(6)},
+        compiler_params=params(),
+        cost_estimate=cost,
         name="first",
-    )(kappa_table, coupling, own, low, high)
+    )(kappa_table, coupling, low, high, *state)
     low = lax.ppermute(to_high, AXES, upward)
     high = lax.ppermute(to_low, AXES, downward)
-    sent = pl.pallas_call(
+    state = pl.pallas_call(
+        inner_second_kernel,
+        out_shape=(planes(WIDE), planes(WIDE), planes(WIDE)),
+        in_specs=smem(1) + vmem(3),
+        out_specs=tuple(vmem(3)),
+        compiler_params=params(),
+        cost_estimate=cost,
+        name="inner_second",
+    )(coupling, first, gain, size)
+    _, _, _, sent = pl.pallas_call(
         second_kernel,
-        out_shape=jax.ShapeDtypeStruct((1024, 128), F32),
-        in_specs=smem(1) + vmem(6),
-        out_specs=vmem(1)[0],
-        scratch_shapes=work,
-        compiler_params=params(),
+        out_shape=tuple(state) + (jax.ShapeDtypeStruct((1024, 128), F32),),
+        in_specs=smem(1) + vmem(9),
+        out_specs=tuple(vmem(4)),
+        scratch_shapes=coarse,
+        input_output_aliases={7 + i: i for i in range(3)},
+        compiler_params=params(),
+        cost_estimate=cost,
         name="second",
-    )(coupling, first, low, high, gain, size, gain_c)
+    )(coupling, first, low, high, gain, size, gain_c, *state)
     got = lax.all_to_all(sent.reshape(16, 64, 128), ("lat", "dep"), 0, 0, tiled=False)
-    block = jax.ShapeDtypeStruct((FIELDS, 8, 8, 256), F32)
+    out = jax.ShapeDtypeStruct((FIELDS, 8, 8, 256), F32)
     return pl.pallas_call(
         finish_kernel,
-        out_shape=(block, block),
+        out_shape=(out, out),
         in_specs=smem(1) + vmem(1),
         out_specs=tuple(vmem(2)),
         scratch_shapes=[pltpu.VMEM((4, 256, 128), F32)],
         compiler_params=params(),
         name="finish",
-    )(odd, got)
+    )(block, got)
 
 
 def solution(mesh):

time: 71.1 us -> 67.4 us (0.948)
  waiting for transfers between devices: 6.92 us -> 3.85 us
  local copies, waits for them, and re-layouts: 2.78 us -> 0.16 us
  Pallas kernels: 14 us -> 15.6 us
  blocking collectives: 40.6 us -> 39.6 us
  other arithmetic: 0 us -> 0.95 us
    ppermute x2, waiting for transfers between devices: 2.98 us -> 0.01 us  [per_device(): high = lax.ppermute(to_low, AXES, downward)]
    unnamed x11 -> x7, local copies, waits for them, and re-layouts: 2.78 us -> 0.16 us
    pallas_call x3 -> x5, Pallas kernels: 13.2 us -> 14.8 us  [the longest x1 5.27 us: per_device(): pl.pallas_call(first_kernel, out_shape=tuple(state) + (planes(OWN), plane...]
    all_to_all x1, blocking collectives: 21.7 us -> 20.6 us  [per_device(): lax.all_to_all(sent.reshape(16, 64, 128), ('lat', 'dep'), 0, 0, tiled=False)]
    reshape x0 -> x1, other arithmetic: none -> 0.92 us  [per_device(): x.astype(F32).reshape(-1, 256)]
  transfers between devices with their start and end apart: 4 -> 4, of which waited for: 4 -> 2; matrix products, arithmetic and copies ran while one was open for 0% -> 0% of each run, Pallas kernels for 0% -> 5%
where the time goes in v3:
time: 67.4 us; the launch traced here: 67.2 us
  blocking collectives  39.6 us (59%)
  Pallas kernels  15.6 us (23%)
  starting transfers between devices  6.37 us (9%)
  waiting for transfers between devices  3.85 us (6%)
  other arithmetic  0.95 us (1%)
  between operations  0.7 us (1%)
    all_to_all x1, blocking collectives, per_device(): lax.all_to_all(sent.reshape(16, 64, 128), ('lat', 'dep'), 0, 0, tiled=False)  20.6 us
    all_to_all x1, blocking collectives, per_device(): got = lax.all_to_all(sent, ('lat', 'dep'), 0, 0, tiled=False)  18.9 us
    ppermute x2, starting transfers between devices, per_device(): high = lax.ppermute(to_low, AXES, downward)  5.77 us
    pallas_call x1, Pallas kernels, per_device(): pl.pallas_call(first_kernel, out_shape=tuple(state) + (planes(OWN), plane...  5.27 us
    pallas_call x1, Pallas kernels, per_device(): pl.pallas_call(second_kernel, out_shape=tuple(state) + (jax.ShapeDtypeStr...  5.18 us
    ppermute x2, waiting for transfers between devices, per_device(): low = lax.ppermute(to_high, AXES, upward)  3.84 us
    pallas_call x1, Pallas kernels, per_device(): pl.pallas_call(inner_first_kernel, out_shape=state, in_specs=smem(2) + vm...  2.03 us
    pallas_call x1, Pallas kernels, per_device(): pl.pallas_call(inner_second_kernel, out_shape=(planes(WIDE), planes(WIDE)...  1.37 us
  transfers between devices with their start and end apart: 4, of which 2 were waited for; matrix products, arithmetic and copies ran while one was open for 0% of the time, Pallas kernels for 5%

profile of v3, /device:TPU:1, one launch (start us, length us, event | category | flops | bytes accessed | tf_op | source)
XLA Modules:
  0.0 67.2 jit_solution(1358053279155704197)
XLA Ops:
  0.6 0.0 copy-start.1
  0.6 0.9 %convert_bitcast_fusion = (f32[64,256]{1,0:T(8,128)S(1)}, f32[64,256]{1,0:T(8,128)S(1)}) fusion(s32[8,8,256]{2,1,0:T(8,128)} %param.7, s32[8,8,256]{2,1,0:T(8,128)} %param.6), kind=kLoop, calls=%fused_computation.1 | loop fusion | flops 32768 | bytes 262144 | tf_op jit(solution)/shard_map/reshape | solution.py:374
  1.6 0.1 copy-done.1
  1.7 0.2 pack.1
  1.9 18.9 %all_to_all.10 = f32[16,48,128]{2,1,0:T(8,128)S(1)} all-to-all(f32[16,48,128]{2,1,0:T(8,128)S(1)} %pack.1), channel_id=1, replica_groups=mesh['lon'=16,'lat'=8,'dep'=2] {'lat','dep'}, dimensions={0} | all-to-all | bytes 786432 | tf_op jit(solution)/shard_map/all_to_all | solution.py:375
  20.8 0.0 copy-start
  20.8 0.5 unpack.1
  21.4 0.0 copy-start.2
  21.4 0.5 collective-permute-start
  21.9 2.5 %collective-permute-start.1 = (f32[13,6,8,128]{3,2,1,0:T(8,128)S(1)}, f32[13,6,8,128]{3,2,1,0:T(8,128)S(1)}, u32[]{:S(2)}, u32[]{:S(2)}) collective-permute-start(f32[13,6,8,128]{3,2,1,0:T(8,128)S(1)} %get-tuple-element.22), channel_id=1, source_target_pairs={{15,13},{9,15},{11,9},{5,11},{7,5},{1,7},{3,1},{2,3},{0,2},{6,0},{... | collective-permute-start | bytes 958472 | tf_op jit(solution)/shard_map/ppermute | solution.py:385
  24.4 0.0 copy-done.2
  24.4 0.1 copy.17.table_ref
  24.5 0.0 copy-done
  24.5 2.0 %inner_first.1 = (f32[44,5,8,128]{3,2,1,0:T(8,128)S(1)}, f32[44,4,8,128]{3,2,1,0:T(8,128)S(1)}, f32[44,4,8,128]{3,2,1,0:T(8,128)S(1)}, f32[22,5,8,128]{3,2,1,0:T...) custom-call(f32[8,4]{1,0:T(8,128)S(1)} %copy.17.table_ref, f32[4,4]{1,0:T(4,128)S(1)} %copy-done, ...), custom_call_target="tpu_custom_call" | custom-call | flops 40000000 | bytes 8000000 | tf_op jit(solution)/shard_map/inner_first/pallas_call | solution.py:390
  26.6 2.3 %collective-permute-done.low_ref = f32[13,6,8,128]{3,2,1,0:T(8,128)S(1)} collective-permute-done((f32[13,6,8,128]{3,2,1,0:T(8,128)S(1)}, f32[13,6,8,128]{3,2,1,0:T(8,128)S(1)}, u32[]{:S(2)}, u32[]{:S(2)}) %collective-permute-start) | collective-permute-done | bytes 319520 | tf_op jit(solution)/shard_map/ppermute | solution.py:384
  28.8 0.0 collective-permute-done.1.high_ref
  28.8 5.3 %first.1 = (f32[44,5,8,128]{3,2,1,0:T(8,128)S(1)}, f32[44,4,8,128]{3,2,1,0:T(8,128)S(1)}, f32[44,4,8,128]{3,2,1,0:T(8,128)S(1)}, f32[22,5,8,128]{3,2,1,0:T(8,128...) custom-call(f32[8,4]{1,0:T(8,128)S(1)} %copy.17.table_ref, ...), custom_call_target="tpu_custom_call", output_to_operand_aliasing={{0}: (4, {}), {1}: (5, {}), {2}: (6, {}), {3}: (7, {}), {4}... | custom-call | flops 40000000 | bytes 8000000 | tf_op jit(solution)/shard_map/first/pallas_call | solution.py:399
  34.1 0.1 collective-permute-start.2
  34.2 3.2 %collective-permute-start.3 = (f32[13,4,8,128]{3,2,1,0:T(8,128)S(1)}, f32[13,4,8,128]{3,2,1,0:T(8,128)S(1)}, u32[]{:S(2)}, u32[]{:S(2)}) collective-permute-start(f32[13,4,8,128]{3,2,1,0:T(8,128)S(1)} %get-tuple-element.32), channel_id=1, source_target_pairs={{15,13},{9,15},{11,9},{5,11},{7,5},{1,7},{3,1},{2,3},{0,2},{6,0},{... | collective-permute-start | bytes 638984 | tf_op jit(solution)/shard_map/ppermute | solution.py:411
  37.4 1.4 %inner_second.1 = (f32[44,4,8,128]{3,2,1,0:T(8,128)S(1)}, f32[44,4,8,128]{3,2,1,0:T(8,128)S(1)}, f32[44,4,8,128]{3,2,1,0:T(8,128)S(1)}) custom-call(f32[4,4]{1,0:T(4,128)S(1)} %copy-done, f32[16,4,8,128]{3,2,1,0:T(8,128)S(1)} %get-tuple-element.30.own_ref, f32[44,5,8,128]{3,2,1,0:T(8,128)S(1)} %get-tuple-element.33.gain, ...), custom_call_target="tpu_custom_call" | custom-call | flops 40000000 | bytes 8000000 | tf_op jit(solution)/shard_map/inner_second/pallas_call | solution.py:412
  38.8 1.6 %collective-permute-done.2.low_ref = f32[13,4,8,128]{3,2,1,0:T(8,128)S(1)} collective-permute-done((f32[13,4,8,128]{3,2,1,0:T(8,128)S(1)}, f32[13,4,8,128]{3,2,1,0:T(8,128)S(1)}, u32[]{:S(2)}, u32[]{:S(2)}) %collective-permute-start.2) | collective-permute-done | bytes 213024 | tf_op jit(solution)/shard_map/ppermute | solution.py:410
  40.4 0.0 collective-permute-done.3.high_ref
  40.4 5.2 %second.1 = (f32[44,4,8,128]{3,2,1,0:T(8,128)S(1)}, f32[44,4,8,128]{3,2,1,0:T(8,128)S(1)}, f32[44,4,8,128]{3,2,1,0:T(8,128)S(1)}, f32[1024,128]{1,0:T(8,128)S(1)}) custom-call(f32[4,4]{1,0:T(4,128)S(1)} %copy-done, f32[16,4,8,128]{3,2,1,0:T(8,128)S(1)} %get-tuple-element.30.own_ref, ...), custom_call_target="tpu_custom_call", output_to_operand_aliasing={{0}: (7, {}), {1}: (8, {}), {2}: (9, {})} | custom-call | flops 40000000 | bytes 8000000 | tf_op jit(solution)/shard_map/second/pallas_call | solution.py:421
  45.6 20.6 %all_to_all.11.in_ref = f32[16,64,128]{2,1,0:T(8,128)S(1)} all-to-all(f32[16,64,128]{2,1,0:T(8,128)S(1)} %bitcast.9), channel_id=1, replica_groups=mesh['lon'=16,'lat'=8,'dep'=2] {'lat','dep'}, dimensions={0} | all-to-all | bytes 1048576 | tf_op jit(solution)/shard_map/all_to_all | solution.py:432
  66.2 1.0 %finish.1 = (f32[4,8,8,256]{3,2,1,0:T(8,128)}, f32[4,8,8,256]{3,2,1,0:T(8,128)}) custom-call(s32[1]{0:T(128)} %bitcast.block_ref, f32[16,64,128]{2,1,0:T(8,128)S(1)} %all_to_all.11.in_ref), custom_call_target="tpu_custom_call" | custom-call | tf_op jit(solution)/shard_map/finish/pallas_call | solution.py:434
  (1 shorter events, 0.0 us)
Async XLA Ops:
  0.6 1.0 %copy-start.1 = (f32[4,8,8,256]{3,2,1,0:T(8,128)S(1)}, f32[4,8,8,256]{3,2,1,0:T(8,128)}, u32[]{:S(2)}) copy-start(f32[4,8,8,256]{3,2,1,0:T(8,128)} %param.5) | copy-start | bytes 786436
  20.8 3.7 %copy-start = (f32[4,4]{1,0:T(4,128)S(1)}, f32[4,4]{1,0:T(4,128)}, u32[]{:S(2)}) copy-start(f32[4,4]{1,0:T(4,128)} %coupling_ref.7) | copy-start | bytes 196
  21.4 3.1 %copy-start.2 = (f32[8,4]{0,1:T(4,128)S(1)}, f32[8,4]{0,1:T(4,128)}, u32[]{:S(2)}) copy-start(f32[8,4]{0,1:T(4,128)} %param.8) | copy-start | bytes 388
  21.4 7.4 %collective-permute-start = (f32[13,6,8,128]{3,2,1,0:T(8,128)S(1)}, f32[13,6,8,128]{3,2,1,0:T(8,128)S(1)}, u32[]{:S(2)}, u32[]{:S(2)}) collective-permute-start(f32[13,6,8,128]{3,2,1,0:T(8,128)S(1)} %get-tuple-element.21), channel_id=1, source_target_pairs={{13,15},{15,9},{9,11},{11,5},{5,7},{7,1},{1,3},{3,2},{2,0},{0,6},{... | collective-permute-start | bytes 958472 | tf_op jit(solution)/shard_map/ppermute | solution.py:384
  21.9 6.9 %collective-permute-start.1 = (f32[13,6,8,128]{3,2,1,0:T(8,128)S(1)}, f32[13,6,8,128]{3,2,1,0:T(8,128)S(1)}, u32[]{:S(2)}, u32[]{:S(2)}) collective-permute-start(f32[13,6,8,128]{3,2,1,0:T(8,128)S(1)} %get-tuple-element.22), channel_id=1, source_target_pairs={{15,13},{9,15},{11,9},{5,11},{7,5},{1,7},{3,1},{2,3},{0,2},{6,0},{... | collective-permute-start | bytes 958472 | tf_op jit(solution)/shard_map/ppermute | solution.py:385
  34.1 6.3 %collective-permute-start.2 = (f32[13,4,8,128]{3,2,1,0:T(8,128)S(1)}, f32[13,4,8,128]{3,2,1,0:T(8,128)S(1)}, u32[]{:S(2)}, u32[]{:S(2)}) collective-permute-start(f32[13,4,8,128]{3,2,1,0:T(8,128)S(1)} %get-tuple-element.31), channel_id=1, source_target_pairs={{13,15},{15,9},{9,11},{11,5},{5,7},{7,1},{1,3},{3,2},{2,0},{0,6},{... | collective-permute-start | bytes 638984 | tf_op jit(solution)/shard_map/ppermute | solution.py:410
  34.2 6.2 %collective-permute-start.3 = (f32[13,4,8,128]{3,2,1,0:T(8,128)S(1)}, f32[13,4,8,128]{3,2,1,0:T(8,128)S(1)}, u32[]{:S(2)}, u32[]{:S(2)}) collective-permute-start(f32[13,4,8,128]{3,2,1,0:T(8,128)S(1)} %get-tuple-element.32), channel_id=1, source_target_pairs={{15,13},{9,15},{11,9},{5,11},{7,5},{1,7},{3,1},{2,3},{0,2},{6,0},{... | collective-permute-start | bytes 638984 | tf_op jit(solution)/shard_map/ppermute | solution.py:411

commit v4 on v3

--- a/solution.py
+++ b/solution.py
@@ -16,7 +16,7 @@
 BASE = 14
 WIDE = OWN + 2 * BASE
 COARSE_WIDE = WIDE // 2
-UNROLL = (6, 2, 4, 5, 4)
+UNROLL = (6, 2, 4, 4)
 AXES = ("lon", "lat", "dep")
 F32 = jnp.float32
 VMEM_LIMIT = 48 * 1024 * 1024
@@ -51,6 +51,11 @@
 
 def smem(count):
     return [pl.BlockSpec(memory_space=pltpu.SMEM)] * count
+
+
+def is_odd(me):
+    block, lat, dep = lax.div(me, 16), lax.rem(lax.div(me, 2), 8), lax.rem(me, 2)
+    return lax.rem(block + lat + dep + 1, 2)
 
 
 def block_rank(block, chunk):
@@ -60,8 +65,8 @@
     return rank + odd * (15 - 2 * rank)
 
 
-def pack_kernel(block_ref, rows_ref, out_ref, turned):
-    block = block_ref[0]
+def pack_kernel(me_ref, rows_ref, out_ref, turned):
+    block = lax.div(me_ref[0], 16)
     for q in range(3):
         for half in range(2):
             tile = rows_ref[128 * q : 128 * q + 128, half * 128 : half * 128 + 128]
@@ -80,23 +85,29 @@
     return jnp.take_along_axis(value, index, axis=1, mode="promise_in_bounds")
 
 
-def unpack_kernel(in_ref, own_ref, low_ref, high_ref):
+def share(own_ref, to_chip, to_next):
+    for i in range(HALO):
+        to_chip[i] = own_ref[OWN - 1 - i]
+        to_next[i] = own_ref[i]
+
+
+def local(odd, o):
+    return o + odd * (OWN - 1 - 2 * o)
+
+
+def unpack_kernel(me_ref, in_ref, own_ref, to_chip, to_next):
     lane = lanes()
     row, depth = lane // 16, lane % 16
     place = (depth % 8) * 8 + row
     upper = depth >= 8
+    odd = is_odd(me_ref[0])
     for o in range(OWN):
         for q in range(3):
             parts = [in_ref[pl.ds(d * 48 + q * 16 + o, 8, stride=96), :] for d in range(2)]
             for half in range(2):
                 index = place + 64 * half
-                plane = jnp.where(upper, pick(parts[1], index), pick(parts[0], index))
-                at = 2 * q + half
-                own_ref[o, at] = plane
-                if o < HALO:
-                    low_ref[o, at] = plane
-                if o >= OWN - HALO:
-                    high_ref[o - (OWN - HALO), at] = plane
+                own_ref[local(odd, o), 2 * q + half] = jnp.where(upper, pick(parts[1], index), pick(parts[0], index))
+    share(own_ref, to_chip, to_next)
 
 
 def plane_masks(step):
@@ -178,12 +189,16 @@
         one(BASE + 1 + turn, BASE + OWN - 1 - turn)
 
 
+def chip_passes(coupling, coeffs, u_a, u_b):
+    for turn, one in enumerate(fine_passes(coupling, coeffs, u_a, u_b)):
+        one(BASE + OWN - 1 - turn, BASE + OWN + HALO - 1 - turn)
+
+
 def solve(coupling, coeffs, gain_c, u_a, u_b, e_a, e_b, rhs_c):
     gain = coeffs[0]
     passes = fine_passes(coupling, coeffs, u_a, u_b)
     for turn, one in enumerate(passes):
         one(BASE - HALO + 1 + turn, BASE + 1 + turn)
-        one(BASE + OWN - 1 - turn, BASE + OWN + HALO - 1 - turn)
 
     masks_c = plane_masks(2)
 
@@ -223,12 +238,24 @@
     passes[0](14, 30)
 
 
-def each_plane(ref, count, first, visit, unroll):
+def each_plane(ref, count, place, visit):
     def body(i, carry):
-        visit(first + i, ref, i)
+        visit(place(i), ref, i)
         return carry
 
-    lax.fori_loop(0, count, body, 0, unroll=unroll)
+    lax.fori_loop(0, count, body, 0, unroll=UNROLL[2])
+
+
+def own_place(i):
+    return BASE + i
+
+
+def chip_place(i):
+    return BASE + OWN + i
+
+
+def next_place(i):
+    return BASE - 1 - i
 
 
 def read_coupling(coupling_ref):
@@ -272,29 +299,39 @@
     return visit
 
 
+def read_table(table_ref):
+    return [[table_ref[c, f] for f in range(FIELDS)] for c in range(CLASSES)]
+
+
+def first_part(table_ref, coupling_ref, ref, place, cells, coeffs, gain_c, u_a, kappas):
+    coupling = read_coupling(coupling_ref)
+    each_plane(ref, ref.shape[0], place, fine_coefficients(read_table(table_ref), coupling, coeffs, u_a, kappas))
+    visit = coarse_coefficients(coupling, coeffs[0], gain_c, kappas)
+    start, stop = cells
+    lax.fori_loop(start, stop, visit, 0, unroll=UNROLL[3])
+    return coupling
+
+
 def inner_first_kernel(table_ref, coupling_ref, own_ref, gain, size, b_sum, gain_c, u_a, u_b):
-    coupling = read_coupling(coupling_ref)
-    table = [[table_ref[c, f] for f in range(FIELDS)] for c in range(CLASSES)]
-    coeffs = (gain, size, b_sum)
-    each_plane(own_ref, OWN, BASE, fine_coefficients(table, coupling, coeffs, u_a, u_b), UNROLL[2])
-    lax.fori_loop(7, 15, coarse_coefficients(coupling, gain, gain_c, u_b), 0, unroll=UNROLL[4])
+    coeffs = (gain, size, b_sum)
+    coupling = first_part(table_ref, coupling_ref, own_ref, own_place, (7, 15), coeffs, gain_c, u_a, u_b)
     inner_passes(coupling, coeffs, u_a, u_b)
 
 
-def first_kernel(table_ref, coupling_ref, low_ref, high_ref, *refs):
-    gain, size, b_sum, gain_c, u_a, u_b, out_ref, to_low, to_high, e_a, e_b, rhs_c, kappas = refs[6:]
-    coupling = read_coupling(coupling_ref)
-    table = [[table_ref[c, f] for f in range(FIELDS)] for c in range(CLASSES)]
-    coeffs = (gain, size, b_sum)
-    visit = fine_coefficients(table, coupling, coeffs, u_a, kappas)
-    each_plane(low_ref, HALO, BASE - HALO, visit, UNROLL[2])
-    each_plane(high_ref, HALO, BASE + OWN, visit, UNROLL[2])
-    visit = coarse_coefficients(coupling, gain, gain_c, kappas)
-    lax.fori_loop(0, 10, lambda i, carry: visit(i + jnp.where(i < 5, 2, 10), carry), 0, unroll=UNROLL[3])
+def chip_first_kernel(table_ref, coupling_ref, chip_ref, *refs):
+    gain, size, b_sum, gain_c, u_a, u_b, kappas = refs[6:]
+    coeffs = (gain, size, b_sum)
+    coupling = first_part(table_ref, coupling_ref, chip_ref, chip_place, (15, 20), coeffs, gain_c, u_a, kappas)
+    chip_passes(coupling, coeffs, u_a, u_b)
+
+
+def first_kernel(table_ref, coupling_ref, next_ref, *refs):
+    gain, size, b_sum, gain_c, u_a, u_b, out_ref, to_chip, to_next, e_a, e_b, rhs_c, kappas = refs[6:]
+    coeffs = (gain, size, b_sum)
+    coupling = first_part(table_ref, coupling_ref, next_ref, next_place, (2, 7), coeffs, gain_c, u_a, kappas)
     solve(coupling, coeffs, gain_c, u_a, u_b, e_a, e_b, rhs_c)
     out_ref[...] = u_b[BASE : BASE + OWN]
-    to_low[...] = u_b[BASE : BASE + HALO]
-    to_high[...] = u_b[BASE + OWN - HALO : BASE + OWN]
+    share(out_ref, to_chip, to_next)
 
 
 def second_start(coeffs, u_a):
@@ -310,35 +347,43 @@
     return visit
 
 
-def inner_second_kernel(coupling_ref, own_ref, gain, size, b_sum, u_a, u_b):
-    coeffs = (gain, size, b_sum)
-    each_plane(own_ref, OWN, BASE, second_start(coeffs, u_a), UNROLL[2])
-    inner_passes(read_coupling(coupling_ref), coeffs, u_a, u_b)
-
-
-def second_kernel(coupling_ref, own_ref, low_ref, high_ref, gain, size, gain_c, *refs):
-    b_sum, u_a, u_b, out_ref, e_a, e_b, rhs_c = refs[3:]
-    coupling = read_coupling(coupling_ref)
-    coeffs = (gain, size, b_sum)
-    each_plane(low_ref, HALO, BASE - HALO, second_start(coeffs, u_a), UNROLL[2])
-    each_plane(high_ref, HALO, BASE + OWN, second_start(coeffs, u_a), UNROLL[2])
-    solve(coupling, coeffs, gain_c, u_a, u_b, e_a, e_b, rhs_c)
-
+def send_rows(odd, kind, plane_of, out_ref):
     lane = lanes()
     place = (lane % 8) * 16 + (lane // 8) % 8
     lower = lane < 64
     for o in range(OWN):
-        for k in range(2):
-            for q in range(2):
-                planes = [own_ref[o, 2 * q + h] if k == 0 else u_b[BASE + o, 2 * q + h] for h in range(2)]
-                for d in range(2):
-                    index = place + 8 * d
-                    rows = jnp.where(lower, pick(planes[0], index), pick(planes[1], index))
-                    out_ref[pl.ds(d * 64 + k * 32 + q * 16 + o, 8, stride=128), :] = rows
-
-
-def finish_kernel(block_ref, in_ref, first_ref, second_ref, turned):
-    block = block_ref[0]
+        for q in range(2):
+            pair = [plane_of(local(odd, o), 2 * q + h) for h in range(2)]
+            for d in range(2):
+                index = place + 8 * d
+                rows = jnp.where(lower, pick(pair[0], index), pick(pair[1], index))
+                out_ref[pl.ds(d * 64 + kind * 32 + q * 16 + o, 8, stride=128), :] = rows
+
+
+def inner_second_kernel(me_ref, coupling_ref, own_ref, gain, size, b_sum, u_a, u_b, out_ref):
+    coeffs = (gain, size, b_sum)
+    each_plane(own_ref, OWN, own_place, second_start(coeffs, u_a))
+    inner_passes(read_coupling(coupling_ref), coeffs, u_a, u_b)
+    send_rows(is_odd(me_ref[0]), 0, lambda at, f: own_ref[at, f], out_ref)
+
+
+def chip_second_kernel(coupling_ref, chip_ref, gain, size, *refs):
+    b_sum, u_a, u_b = refs[3:]
+    coeffs = (gain, size, b_sum)
+    each_plane(chip_ref, HALO, chip_place, second_start(coeffs, u_a))
+    chip_passes(read_coupling(coupling_ref), coeffs, u_a, u_b)
+
+
+def second_kernel(me_ref, coupling_ref, next_ref, gain, size, gain_c, *refs):
+    b_sum, u_a, u_b, out_ref, e_a, e_b, rhs_c = refs[4:]
+    coeffs = (gain, size, b_sum)
+    each_plane(next_ref, HALO, next_place, second_start(coeffs, u_a))
+    solve(read_coupling(coupling_ref), coeffs, gain_c, u_a, u_b, e_a, e_b, rhs_c)
+    send_rows(is_odd(me_ref[0]), 1, lambda at, f: u_b[BASE + at, f], out_ref)
+
+
+def finish_kernel(me_ref, in_ref, first_ref, second_ref, turned):
+    block = lax.div(me_ref[0], 16)
     for k, out_ref in enumerate((first_ref, second_ref)):
         for q in range(2):
             for chunk in range(16):
@@ -359,9 +404,13 @@
 
 
 def per_device(source, sea_mask, classes, kappa_table, coupling):
-    block = lax.axis_index("lon").astype(jnp.int32).reshape(1)
-    upward = [(device_of(g), device_of(g + 1)) for g in range(256)]
-    downward = [(b, a) for a, b in upward]
+    me = lax.axis_index(AXES).astype(jnp.int32).reshape(1)
+    chips = [(device_of(g ^ 1), device_of(g)) for g in range(256)]
+    nexts = [(device_of(((g + 1) ^ 1) - 1), device_of(g)) for g in range(256)]
+
+    def trade(to_chip, to_next):
+        from_next = lax.ppermute(to_next, AXES, nexts)
+        return lax.ppermute(to_chip, AXES, chips), from_next
 
     sent = pl.pallas_call(
         pack_kernel,
@@ -371,64 +420,43 @@
         scratch_shapes=[pltpu.VMEM((3, 256, 128), F32)],
         compiler_params=params(),
         name="pack",
-    )(block, jnp.concatenate([x.astype(F32).reshape(-1, 256) for x in (source, sea_mask, classes)]))
+    )(me, jnp.concatenate([x.astype(F32).reshape(-1, 256) for x in (source, sea_mask, classes)]))
     got = lax.all_to_all(sent, ("lat", "dep"), 0, 0, tiled=False)
-    own, to_low, to_high = pl.pallas_call(
-        unpack_kernel,
-        out_shape=(planes(OWN, 6), planes(HALO, 6), planes(HALO, 6)),
-        in_specs=vmem(1),
-        out_specs=tuple(vmem(3)),
-        compiler_params=params(),
-        name="unpack",
-    )(got.reshape(768, 128))
-    low = lax.ppermute(to_high, AXES, upward)
-    high = lax.ppermute(to_low, AXES, downward)
-
-    cost = pl.CostEstimate(flops=40_000_000, bytes_accessed=8_000_000, transcendentals=0)
+    def call(kernel, given, numbers, state, more, work, name):
+        return pl.pallas_call(
+            kernel,
+            out_shape=tuple(state) + tuple(more),
+            in_specs=smem(numbers) + vmem(len(given) - numbers + len(state)),
+            out_specs=tuple(vmem(len(state) + len(more))),
+            scratch_shapes=work,
+            input_output_aliases={len(given) + i: i for i in range(len(state))},
+            compiler_params=params(),
+            cost_estimate=pl.CostEstimate(flops=40_000_000, bytes_accessed=8_000_000, transcendentals=0),
+            name=name,
+        )(*given, *state)
+
+    halo = [planes(HALO), planes(HALO)]
     coarse = [scratch(COARSE_WIDE)] * 3
-    state = (planes(WIDE, 5), planes(WIDE), planes(WIDE), planes(COARSE_WIDE, 5), planes(WIDE), planes(WIDE))
-    state = pl.pallas_call(
-        inner_first_kernel,
-        out_shape=state,
-        in_specs=smem(2) + vmem(1),
-        out_specs=tuple(vmem(6)),
-        compiler_params=params(),
-        cost_estimate=cost,
-        name="inner_first",
-    )(kappa_table, coupling, own)
-    gain, size, _, gain_c, _, _, first, to_low, to_high = pl.pallas_call(
-        first_kernel,
-        out_shape=tuple(state) + (planes(OWN), planes(HALO), planes(HALO)),
-        in_specs=smem(2) + vmem(8),
-        out_specs=tuple(vmem(9)),
-        scratch_shapes=coarse + [scratch(WIDE)],
-        input_output_aliases={4 + i: i for i in range(6)},
-        compiler_params=params(),
-        cost_estimate=cost,
-        name="first",
-    )(kappa_table, coupling, low, high, *state)
-    low = lax.ppermute(to_high, AXES, upward)
-    high = lax.ppermute(to_low, AXES, downward)
-    state = pl.pallas_call(
-        inner_second_kernel,
-        out_shape=(planes(WIDE), planes(WIDE), planes(WIDE)),
-        in_specs=smem(1) + vmem(3),
-        out_specs=tuple(vmem(3)),
-        compiler_params=params(),
-        cost_estimate=cost,
-        name="inner_second",
-    )(coupling, first, gain, size)
-    _, _, _, sent = pl.pallas_call(
-        second_kernel,
-        out_shape=tuple(state) + (jax.ShapeDtypeStruct((1024, 128), F32),),
-        in_specs=smem(1) + vmem(9),
-        out_specs=tuple(vmem(4)),
-        scratch_shapes=coarse,
-        input_output_aliases={7 + i: i for i in range(3)},
-        compiler_params=params(),
-        cost_estimate=cost,
-        name="second",
-    )(coupling, first, low, high, gain, size, gain_c, *state)
+    rows = jax.ShapeDtypeStruct((1024, 128), F32)
+    given = [me, got.reshape(768, 128)]
+    own, to_chip, to_next = call(unpack_kernel, given, 1, [], [planes(OWN, 6), planes(HALO, 6), planes(HALO, 6)], [], "unpack")
+    mate, beyond = trade(to_chip, to_next)
+
+    fresh = [planes(WIDE, 5), planes(WIDE), planes(WIDE), planes(COARSE_WIDE, 5), planes(WIDE), planes(WIDE)]
+    numbers = [kappa_table, coupling]
+    state = call(inner_first_kernel, numbers + [own], 2, [], fresh, [], "inner_first")
+    state = call(chip_first_kernel, numbers + [mate], 2, state, [], [scratch(WIDE)], "chip_first")
+    more = [planes(OWN)] + halo
+    state = call(first_kernel, numbers + [beyond], 2, state, more, coarse + [scratch(WIDE)], "first")
+    gain, size, _, gain_c, _, _, first, to_chip, to_next = state
+    mate, beyond = trade(to_chip, to_next)
+
+    fresh = [planes(WIDE), planes(WIDE), planes(WIDE), rows]
+    state = call(inner_second_kernel, [me, coupling, first, gain, size], 2, [], fresh, [], "inner_second")
+    sent = state[3]
+    state = call(chip_second_kernel, [coupling, mate, gain, size], 1, state[:3], [], [], "chip_second")
+    state = call(second_kernel, [me, coupling, beyond, gain, size, gain_c], 2, list(state) + [sent], [], coarse, "second")
+    sent = state[3]
     got = lax.all_to_all(sent.reshape(16, 64, 128), ("lat", "dep"), 0, 0, tiled=False)
     out = jax.ShapeDtypeStruct((FIELDS, 8, 8, 256), F32)
     return pl.pallas_call(
@@ -439,7 +467,7 @@
         scratch_shapes=[pltpu.VMEM((4, 256, 128), F32)],
         compiler_params=params(),
         name="finish",
-    )(block, got)
+    )(me, got)
 
 
 def solution(mesh):

time: 67.4 us -> 66.4 us (0.985)
  starting transfers between devices: 6.37 us -> 1.44 us
  Pallas kernels: 15.6 us -> 18.3 us
  waiting for transfers between devices: 3.85 us -> 5.5 us
    ppermute x4, starting transfers between devices: 6.37 us -> 1.44 us  [the longest x2 0.83 us: trade(): from_next = lax.ppermute(to_next, AXES, nexts)]
    pallas_call x5 -> x7, Pallas kernels: 14.4 us -> 17.1 us  [call(): pl.pallas_call(kernel, out_shape=tuple(state) + tuple(more), in_specs=sme...]
    ppermute x4, waiting for transfers between devices: 3.85 us -> 5.5 us  [the longest x2 5.49 us: trade(): from_next = lax.ppermute(to_next, AXES, nexts)]
  transfers between devices with their start and end apart: 4 -> 4, of which waited for: 2 -> 2; matrix products, arithmetic and copies ran while one was open for 0% -> 0% of each run, Pallas kernels for 5% -> 11%
where the time goes in v4:
time: 66.4 us; the launch traced here: 66.2 us
  blocking collectives  39.2 us (59%)
  Pallas kernels  18.3 us (28%)
  waiting for transfers between devices  5.5 us (8%)
  starting transfers between devices  1.44 us (2%)
  other arithmetic  0.95 us (1%)
  between operations  0.73 us (1%)
    all_to_all x1, blocking collectives, per_device(): lax.all_to_all(sent.reshape(16, 64, 128), ('lat', 'dep'), 0, 0, tiled=False)  20.2 us
    all_to_all x1, blocking collectives, per_device(): got = lax.all_to_all(sent, ('lat', 'dep'), 0, 0, tiled=False)  18.9 us
    pallas_call x7, Pallas kernels, call(): pl.pallas_call(kernel, out_shape=tuple(state) + tuple(more), in_specs=sme...  17.1 us
    ppermute x2, waiting for transfers between devices, trade(): from_next = lax.ppermute(to_next, AXES, nexts)  5.49 us
  transfers between devices with their start and end apart: 4, of which 2 were waited for; matrix products, arithmetic and copies ran while one was open for 0% of the time, Pallas kernels for 11%

profile of v4, /device:TPU:1, one launch (start us, length us, event | category | flops | bytes accessed | tf_op | source)
XLA Modules:
  0.0 66.2 jit_solution(11532045936373816981)
XLA Ops:
  0.6 0.0 copy-start.1
  0.6 0.9 %convert_bitcast_fusion = (f32[64,256]{1,0:T(8,128)S(1)}, f32[64,256]{1,0:T(8,128)S(1)}) fusion(s32[8,8,256]{2,1,0:T(8,128)} %param.7, s32[8,8,256]{2,1,0:T(8,128)} %param.6), kind=kLoop, calls=%fused_computation.1 | loop fusion | flops 32768 | bytes 262144 | tf_op jit(solution)/shard_map/reshape | solution.py:423
  1.6 0.1 copy-done.1
  1.7 0.2 pack.1
  1.9 18.9 %all_to_all.10 = f32[16,48,128]{2,1,0:T(8,128)S(1)} all-to-all(f32[16,48,128]{2,1,0:T(8,128)S(1)} %pack.1), channel_id=1, replica_groups=mesh['lon'=16,'lat'=8,'dep'=2] {'lat','dep'}, dimensions={0} | all-to-all | bytes 786432 | tf_op jit(solution)/shard_map/all_to_all | solution.py:424
  20.8 0.0 copy-start
  20.8 0.6 unpack.1
  21.5 0.0 copy-start.2
  21.5 0.5 collective-permute-start.1
  22.0 0.3 collective-permute-start
  22.3 0.0 copy-done.2
  22.3 0.1 copy.28.table_ref
  22.4 0.0 copy-done
  22.4 2.0 %inner_first.1 = (f32[44,5,8,128]{3,2,1,0:T(8,128)S(1)}, f32[44,4,8,128]{3,2,1,0:T(8,128)S(1)}, f32[44,4,8,128]{3,2,1,0:T(8,128)S(1)}, f32[22,5,8,128]{3,2,1,0:T...) custom-call(f32[8,4]{1,0:T(8,128)S(1)} %copy.28.table_ref, f32[4,4]{1,0:T(4,128)S(1)} %copy-done, ...), custom_call_target="tpu_custom_call" | custom-call | flops 40000000 | bytes 8000000 | tf_op jit(solution)/shard_map/inner_first/pallas_call | solution.py:426
  24.4 0.0 collective-permute-done.1.chip_ref
  24.4 2.3 %chip_first.1 = (f32[44,5,8,128]{3,2,1,0:T(8,128)S(1)}, f32[44,4,8,128]{3,2,1,0:T(8,128)S(1)}, f32[44,4,8,128]{3,2,1,0:T(8,128)S(1)}, f32[22,5,8,128]{3,2,1,0:T(...) custom-call(f32[8,4]{1,0:T(8,128)S(1)} %copy.28.table_ref, ...), custom_call_target="tpu_custom_call", output_to_operand_aliasing={{0}: (3, {}), {1}: (4, {}), {2}: (5, {}), {3}: (6, {}), {4}... | custom-call | flops 40000000 | bytes 8000000 | tf_op jit(solution)/shard_map/chip_first/pallas_call | solution.py:426
  26.7 2.7 %collective-permute-done.next_ref = f32[13,6,8,128]{3,2,1,0:T(8,128)S(1)} collective-permute-done((f32[13,6,8,128]{3,2,1,0:T(8,128)S(1)}, f32[13,6,8,128]{3,2,1,0:T(8,128)S(1)}, u32[]{:S(2)}, u32[]{:S(2)}) %collective-permute-start) | collective-permute-done | bytes 319520 | tf_op jit(solution)/shard_map/ppermute | solution.py:412
  29.3 4.8 %first.1 = (f32[44,5,8,128]{3,2,1,0:T(8,128)S(1)}, f32[44,4,8,128]{3,2,1,0:T(8,128)S(1)}, f32[44,4,8,128]{3,2,1,0:T(8,128)S(1)}, f32[22,5,8,128]{3,2,1,0:T(8,128...) custom-call(f32[8,4]{1,0:T(8,128)S(1)} %copy.28.table_ref, ...), custom_call_target="tpu_custom_call", output_to_operand_aliasing={{0}: (3, {}), {1}: (4, {}), {2}: (5, {}), {3}: (6, {}), {4}... | custom-call | flops 40000000 | bytes 8000000 | tf_op jit(solution)/shard_map/first/pallas_call | solution.py:426
  34.1 0.1 collective-permute-start.3
  34.2 0.6 collective-permute-start.2
  34.8 1.7 %inner_second.1 = (f32[44,4,8,128]{3,2,1,0:T(8,128)S(1)}, f32[44,4,8,128]{3,2,1,0:T(8,128)S(1)}, f32[44,4,8,128]{3,2,1,0:T(8,128)S(1)}, f32[1024,128]{1,0:T(8,128)S(1)}) custom-call(s32[1]{0:T(128)} %bitcast.me_ref, f32[4,4]{1,0:T(4,128)S(1)} %copy-done, f32[16,4,8,128]{3,2,1,0:T(8,128)S(1)} %get-tuple-element.51.own_ref, ...), custom_call_target="tpu_custom_call" | custom-call | flops 40000000 | bytes 8000000 | tf_op jit(solution)/shard_map/inner_second/pallas_call | solution.py:426
  36.5 0.0 collective-permute-done.3.chip_ref
  36.5 1.4 %chip_second.1 = (f32[44,4,8,128]{3,2,1,0:T(8,128)S(1)}, f32[44,4,8,128]{3,2,1,0:T(8,128)S(1)}, f32[44,4,8,128]{3,2,1,0:T(8,128)S(1)}) custom-call(f32[4,4]{1,0:T(4,128)S(1)} %copy-done, f32[13,4,8,128]{3,2,1,0:T(8,128)S(1)} %collective-permute-done.3.chip_ref, ...), custom_call_target="tpu_custom_call", output_to_operand_aliasing={{0}: (4, {}), {1}: (5, {}), {2}: (6, {})} | custom-call | flops 40000000 | bytes 8000000 | tf_op jit(solution)/shard_map/chip_second/pallas_call | solution.py:426
  37.9 2.8 %collective-permute-done.2.next_ref = f32[13,4,8,128]{3,2,1,0:T(8,128)S(1)} collective-permute-done((f32[13,4,8,128]{3,2,1,0:T(8,128)S(1)}, f32[13,4,8,128]{3,2,1,0:T(8,128)S(1)}, u32[]{:S(2)}, u32[]{:S(2)}) %collective-permute-start.2) | collective-permute-done | bytes 213024 | tf_op jit(solution)/shard_map/ppermute | solution.py:412
  40.7 4.3 %second.1 = (f32[44,4,8,128]{3,2,1,0:T(8,128)S(1)}, f32[44,4,8,128]{3,2,1,0:T(8,128)S(1)}, f32[44,4,8,128]{3,2,1,0:T(8,128)S(1)}, f32[1024,128]{1,0:T(8,128)S(1)}) custom-call(s32[1]{0:T(128)} %bitcast.me_ref, f32[4,4]{1,0:T(4,128)S(1)} %copy-done, ...), custom_call_target="tpu_custom_call", output_to_operand_aliasing={{0}: (6, {}), {1}: (7, {}), {2}: (8, {}), {3}: (9, {})} | custom-call | flops 40000000 | bytes 8000000 | tf_op jit(solution)/shard_map/second/pallas_call | solution.py:426
  45.0 20.2 %all_to_all.11.in_ref = f32[16,64,128]{2,1,0:T(8,128)S(1)} all-to-all(f32[16,64,128]{2,1,0:T(8,128)S(1)} %bitcast.8), channel_id=1, replica_groups=mesh['lon'=16,'lat'=8,'dep'=2] {'lat','dep'}, dimensions={0} | all-to-all | bytes 1048576 | tf_op jit(solution)/shard_map/all_to_all | solution.py:460
  65.2 1.0 %finish.1 = (f32[4,8,8,256]{3,2,1,0:T(8,128)}, f32[4,8,8,256]{3,2,1,0:T(8,128)}) custom-call(s32[1]{0:T(128)} %bitcast.me_ref, f32[16,64,128]{2,1,0:T(8,128)S(1)} %all_to_all.11.in_ref), custom_call_target="tpu_custom_call" | custom-call | tf_op jit(solution)/shard_map/finish/pallas_call | solution.py:462
  (1 shorter events, 0.0 us)
Async XLA Ops:
  0.6 1.0 %copy-start.1 = (f32[4,8,8,256]{3,2,1,0:T(8,128)S(1)}, f32[4,8,8,256]{3,2,1,0:T(8,128)}, u32[]{:S(2)}) copy-start(f32[4,8,8,256]{3,2,1,0:T(8,128)} %param.5) | copy-start | bytes 786436
  20.8 1.5 %copy-start = (f32[4,4]{1,0:T(4,128)S(1)}, f32[4,4]{1,0:T(4,128)}, u32[]{:S(2)}) copy-start(f32[4,4]{1,0:T(4,128)} %coupling_ref.11) | copy-start | bytes 196
  21.5 0.8 %copy-start.2 = (f32[8,4]{0,1:T(4,128)S(1)}, f32[8,4]{0,1:T(4,128)}, u32[]{:S(2)}) copy-start(f32[8,4]{0,1:T(4,128)} %param.8) | copy-start | bytes 388
  21.5 2.9 %collective-permute-start.1 = (f32[13,6,8,128]{3,2,1,0:T(8,128)S(1)}, f32[13,6,8,128]{3,2,1,0:T(8,128)S(1)}, u32[]{:S(2)}, u32[]{:S(2)}) collective-permute-start(f32[13,6,8,128]{3,2,1,0:T(8,128)S(1)} %get-tuple-element.32), channel_id=1, source_target_pairs={{15,13},{13,15},{11,9},{9,11},{7,5},{5,7},{3,1},{1,3},{0,2},{2,0},... | collective-permute-start | bytes 958472 | tf_op jit(solution)/shard_map/ppermute | solution.py:413
  22.0 7.3 %collective-permute-start = (f32[13,6,8,128]{3,2,1,0:T(8,128)S(1)}, f32[13,6,8,128]{3,2,1,0:T(8,128)S(1)}, u32[]{:S(2)}, u32[]{:S(2)}) collective-permute-start(f32[13,6,8,128]{3,2,1,0:T(8,128)S(1)} %get-tuple-element.31), channel_id=1, source_target_pairs={{253,13},{9,15},{15,9},{5,11},{11,5},{1,7},{7,1},{2,3},{3,2},{6,0}... | collective-permute-start | bytes 958472 | tf_op jit(solution)/shard_map/ppermute | solution.py:412
  34.1 2.4 %collective-permute-start.3 = (f32[13,4,8,128]{3,2,1,0:T(8,128)S(1)}, f32[13,4,8,128]{3,2,1,0:T(8,128)S(1)}, u32[]{:S(2)}, u32[]{:S(2)}) collective-permute-start(f32[13,4,8,128]{3,2,1,0:T(8,128)S(1)} %get-tuple-element.50), channel_id=1, source_target_pairs={{15,13},{13,15},{11,9},{9,11},{7,5},{5,7},{3,1},{1,3},{0,2},{2,0},... | collective-permute-start | bytes 638984 | tf_op jit(solution)/shard_map/ppermute | solution.py:413
  34.2 6.5 %collective-permute-start.2 = (f32[13,4,8,128]{3,2,1,0:T(8,128)S(1)}, f32[13,4,8,128]{3,2,1,0:T(8,128)S(1)}, u32[]{:S(2)}, u32[]{:S(2)}) collective-permute-start(f32[13,4,8,128]{3,2,1,0:T(8,128)S(1)} %get-tuple-element.46), channel_id=1, source_target_pairs={{253,13},{9,15},{15,9},{5,11},{11,5},{1,7},{7,1},{2,3},{3,2},{6,0}... | collective-permute-start | bytes 638984 | tf_op jit(solution)/shard_map/ppermute | solution.py:412

commit v5 on v4

--- a/solution.py
+++ b/solution.py
@@ -16,7 +16,7 @@
 BASE = 14
 WIDE = OWN + 2 * BASE
 COARSE_WIDE = WIDE // 2
-UNROLL = (6, 2, 4, 4)
+UNROLL = (9, 12, 13, 4)
 AXES = ("lon", "lat", "dep")
 F32 = jnp.float32
 VMEM_LIMIT = 48 * 1024 * 1024
@@ -150,10 +150,52 @@
         before, u, v = v, u_next, after
 
 
-def halves(t):
-    lane = lanes()
-    t = t + jnp.where(lane % 2 == 0, pltpu.roll(t, 127, 1), pltpu.roll(t, 1, 1))
-    return t + jnp.where((lane // 16) % 2 == 0, pltpu.roll(t, 112, 1), pltpu.roll(t, 16, 1))
+class Places:
+    def __init__(self):
+        lane = lanes()
+        self.swaps = [jnp.bitwise_xor(lane, x) for x in (1, 16, 17)]
+        self.even_depth = lane % 2 == 0
+        self.even_lat = (lane // 16) % 2 == 0
+
+    def turn(self, value, x):
+        return pick(value, self.swaps[x - 1]) if x else value
+
+    def choose(self, values):
+        low = jnp.where(self.even_depth, values[0], values[1])
+        return jnp.where(self.even_lat, low, jnp.where(self.even_depth, values[2], values[3]))
+
+    def gather(self, t):
+        pairs = []
+        for x, y in ((t[0], t[1]), (t[2], t[3])):
+            pairs.append(jnp.where(self.even_depth, x, y) + self.turn(jnp.where(self.even_depth, y, x), 1))
+        x, y = pairs
+        return jnp.where(self.even_lat, x, y) + self.turn(jnp.where(self.even_lat, y, x), 2)
+
+    def total(self, t):
+        t = t + self.turn(t, 1)
+        return t + self.turn(t, 2)
+
+    def spread(self, packed):
+        turned = [self.turn(packed, x) for x in range(4)]
+        return [self.choose([turned[p ^ f] for p in range(4)]) for f in range(FIELDS)]
+
+
+def coarse_stencil(start, stop, e_ref, target, gain_c, rhs_c, coupling, places):
+    masks = plane_masks(2)
+    mix = [places.choose([jnp.full((8, 128), coupling[f][f ^ x], F32) for f in range(FIELDS)]) for x in range(1, 4)]
+
+    def load(c):
+        e = e_ref[c, 0]
+        return e, gain_c[c, 1] * e
+
+    _, before = load(start - 1)
+    e, v = load(start)
+    for c in range(start, stop):
+        e_next, after = load(c + 1)
+        near = (before + after) + plane_near(v, masks, 2)
+        off = mix[0] * places.turn(e, 1) + mix[1] * places.turn(e, 2) + mix[2] * places.turn(e, 3)
+        target[c, 0] = (0.2 * e + rhs_c[c, 0]) + gain_c[c, 0] * (0.25 * near - off)
+        before, e, v = v, e_next, after
 
 
 def fine_passes(coupling, coeffs, u_a, u_b):
@@ -200,36 +242,26 @@
     for turn, one in enumerate(passes):
         one(BASE - HALO + 1 + turn, BASE + 1 + turn)
 
-    masks_c = plane_masks(2)
-
-    def sea_c(c):
-        return gain_c[c, FIELDS]
-
-    def coarse_into(target):
-        def emit(c, f, e, near, off):
-            target[c, f] = (0.2 * e + rhs_c[c, f]) + gain_c[c, f] * (0.25 * near - off)
-
-        return emit
+    places = Places()
 
     def restrict(c, carry):
-        s = sea_c(c)
-        for f in range(FIELDS):
-            mean = halves(u_b[2 * c, f] + u_b[2 * c + 1, f]) * 0.125
-            first = (gain_c[c, f] + (1.0 - s) * OMEGA) * (s * mean)
-            rhs_c[c, f] = first
-            e_a[c, f] = first
+        s = gain_c[c, 1]
+        mean = places.gather([u_b[2 * c, f] + u_b[2 * c + 1, f] for f in range(FIELDS)]) * 0.125
+        first = (gain_c[c, 0] + (1.0 - s) * OMEGA) * (s * mean)
+        rhs_c[c, 0] = first
+        e_a[c, 0] = first
         return carry
 
     lax.fori_loop(2, 20, restrict, 0, unroll=UNROLL[0])
-    stencil(3, 19, e_a, sea_c, coupling, masks_c, 2, coarse_into(e_b))
-    stencil(4, 18, e_b, sea_c, coupling, masks_c, 2, coarse_into(e_a))
-    stencil(5, 17, e_a, sea_c, coupling, masks_c, 2, coarse_into(e_b))
+    coarse_stencil(3, 19, e_a, e_b, gain_c, rhs_c, coupling, places)
+    coarse_stencil(4, 18, e_b, e_a, gain_c, rhs_c, coupling, places)
+    coarse_stencil(5, 17, e_a, e_b, gain_c, rhs_c, coupling, places)
 
     def correct(c, carry):
-        for f in range(FIELDS):
-            e = e_b[c, f]
-            for w in (2 * c, 2 * c + 1):
-                u_a[w, f] = u_a[w, f] + gain[w, FIELDS] * e
+        e = places.spread(e_b[c, 0])
+        for w in (2 * c, 2 * c + 1):
+            for f in range(FIELDS):
+                u_a[w, f] = u_a[w, f] + gain[w, FIELDS] * e[f]
         return carry
 
     lax.fori_loop(5, 17, correct, 0, unroll=UNROLL[1])
@@ -287,13 +319,15 @@
 
 
 def coarse_coefficients(coupling, gain, gain_c, kappas):
+    places = Places()
+    own = places.choose([jnp.full((8, 128), coupling[f][f] + 1.5, F32) for f in range(FIELDS)])
+
     def visit(c, carry):
-        s = jnp.minimum(halves(gain[2 * c, FIELDS] + gain[2 * c + 1, FIELDS]), 1.0)
-        gain_c[c, FIELDS] = s
-        for f in range(FIELDS):
-            kappa = halves(kappas[2 * c, f] + kappas[2 * c + 1, f]) * 0.125
-            diag = s * (kappa + (coupling[f][f] + 1.5)) + (1.0 - s)
-            gain_c[c, f] = s * (OMEGA / diag)
+        s = jnp.minimum(places.total(gain[2 * c, FIELDS] + gain[2 * c + 1, FIELDS]), 1.0)
+        kappa = places.gather([kappas[2 * c, f] + kappas[2 * c + 1, f] for f in range(FIELDS)]) * 0.125
+        diag = s * (kappa + own) + (1.0 - s)
+        gain_c[c, 0] = s * (OMEGA / diag)
+        gain_c[c, 1] = s
         return carry
 
     return visit
@@ -436,13 +470,13 @@
         )(*given, *state)
 
     halo = [planes(HALO), planes(HALO)]
-    coarse = [scratch(COARSE_WIDE)] * 3
+    coarse = [scratch(COARSE_WIDE, 1)] * 3
     rows = jax.ShapeDtypeStruct((1024, 128), F32)
     given = [me, got.reshape(768, 128)]
     own, to_chip, to_next = call(unpack_kernel, given, 1, [], [planes(OWN, 6), planes(HALO, 6), planes(HALO, 6)], [], "unpack")
     mate, beyond = trade(to_chip, to_next)
 
-    fresh = [planes(WIDE, 5), planes(WIDE), planes(WIDE), planes(COARSE_WIDE, 5), planes(WIDE), planes(WIDE)]
+    fresh = [planes(WIDE, 5), planes(WIDE), planes(WIDE), planes(COARSE_WIDE, 2), planes(WIDE), planes(WIDE)]
     numbers = [kappa_table, coupling]
     state = call(inner_first_kernel, numbers + [own], 2, [], fresh, [], "inner_first")
     state = call(chip_first_kernel, numbers + [mate], 2, state, [], [scratch(WIDE)], "chip_first")

time: 66.4 us -> 64.3 us (0.968)
  Pallas kernels: 18.3 us -> 15.5 us
  waiting for transfers between devices: 5.5 us -> 6.4 us
    pallas_call x7, Pallas kernels: 17.1 us -> 14.3 us  [call(): pl.pallas_call(kernel, out_shape=tuple(state) + tuple(more), in_specs=sme...]
    ppermute x2, waiting for transfers between devices: 5.49 us -> 6.39 us  [trade(): from_next = lax.ppermute(to_next, AXES, nexts)]
  transfers between devices with their start and end apart: 4 -> 4, of which waited for: 2 -> 2; matrix products, arithmetic and copies ran while one was open for 0% -> 0% of each run, Pallas kernels for 11% -> 10%
where the time goes in v5:
time: 64.3 us; the launch traced here: 64.1 us
  blocking collectives  39.2 us (61%)
  Pallas kernels  15.5 us (24%)
  waiting for transfers between devices  6.4 us (10%)
  starting transfers between devices  1.26 us (2%)
  other arithmetic  0.95 us (1%)
  between operations  0.72 us (1%)
    all_to_all x1, blocking collectives, per_device(): lax.all_to_all(sent.reshape(16, 64, 128), ('lat', 'dep'), 0, 0, tiled=False)  20.2 us
    all_to_all x1, blocking collectives, per_device(): got = lax.all_to_all(sent, ('lat', 'dep'), 0, 0, tiled=False)  18.9 us
    pallas_call x7, Pallas kernels, call(): pl.pallas_call(kernel, out_shape=tuple(state) + tuple(more), in_specs=sme...  14.3 us
    ppermute x2, waiting for transfers between devices, trade(): from_next = lax.ppermute(to_next, AXES, nexts)  6.39 us
  transfers between devices with their start and end apart: 4, of which 2 were waited for; matrix products, arithmetic and copies ran while one was open for 0% of the time, Pallas kernels for 10%

profile of v5, /device:TPU:1, one launch (start us, length us, event | category | flops | bytes accessed | tf_op | source)
XLA Modules:
  0.0 64.1 jit_solution(15786611655485894751)
XLA Ops:
  0.6 0.0 copy-start.1
  0.6 0.9 %convert_bitcast_fusion = (f32[64,256]{1,0:T(8,128)S(1)}, f32[64,256]{1,0:T(8,128)S(1)}) fusion(s32[8,8,256]{2,1,0:T(8,128)} %param.7, s32[8,8,256]{2,1,0:T(8,128)} %param.6), kind=kLoop, calls=%fused_computation.1 | loop fusion | flops 32768 | bytes 262144 | tf_op jit(solution)/shard_map/reshape | solution.py:457
  1.6 0.1 copy-done.1
  1.7 0.2 pack.1
  1.9 18.9 %all_to_all.10 = f32[16,48,128]{2,1,0:T(8,128)S(1)} all-to-all(f32[16,48,128]{2,1,0:T(8,128)S(1)} %pack.1), channel_id=1, replica_groups=mesh['lon'=16,'lat'=8,'dep'=2] {'lat','dep'}, dimensions={0} | all-to-all | bytes 786432 | tf_op jit(solution)/shard_map/all_to_all | solution.py:458
  20.8 0.0 copy-start
  20.8 0.6 unpack.1
  21.5 0.0 copy-start.2
  21.5 0.5 collective-permute-start.1
  22.0 0.3 collective-permute-start
  22.3 0.0 copy-done.2
  22.3 0.1 copy.28.table_ref
  22.4 0.0 copy-done
  22.4 1.9 %inner_first.1 = (f32[44,5,8,128]{3,2,1,0:T(8,128)S(1)}, f32[44,4,8,128]{3,2,1,0:T(8,128)S(1)}, f32[44,4,8,128]{3,2,1,0:T(8,128)S(1)}, f32[22,2,8,128]{3,2,1,0:T...) custom-call(f32[8,4]{1,0:T(8,128)S(1)} %copy.28.table_ref, f32[4,4]{1,0:T(4,128)S(1)} %copy-done, ...), custom_call_target="tpu_custom_call" | custom-call | flops 40000000 | bytes 8000000 | tf_op jit(solution)/shard_map/inner_first/pallas_call | solution.py:460
  24.3 0.0 collective-permute-done.1.chip_ref
  24.3 1.5 %chip_first.1 = (f32[44,5,8,128]{3,2,1,0:T(8,128)S(1)}, f32[44,4,8,128]{3,2,1,0:T(8,128)S(1)}, f32[44,4,8,128]{3,2,1,0:T(8,128)S(1)}, f32[22,2,8,128]{3,2,1,0:T(...) custom-call(f32[8,4]{1,0:T(8,128)S(1)} %copy.28.table_ref, ...), custom_call_target="tpu_custom_call", output_to_operand_aliasing={{0}: (3, {}), {1}: (4, {}), {2}: (5, {}), {3}: (6, {}), {4}... | custom-call | flops 40000000 | bytes 8000000 | tf_op jit(solution)/shard_map/chip_first/pallas_call | solution.py:460
  25.8 3.5 %collective-permute-done.next_ref = f32[13,6,8,128]{3,2,1,0:T(8,128)S(1)} collective-permute-done((f32[13,6,8,128]{3,2,1,0:T(8,128)S(1)}, f32[13,6,8,128]{3,2,1,0:T(8,128)S(1)}, u32[]{:S(2)}, u32[]{:S(2)}) %collective-permute-start) | collective-permute-done | bytes 319520 | tf_op jit(solution)/shard_map/ppermute | solution.py:446
  29.3 3.5 %first.1 = (f32[44,5,8,128]{3,2,1,0:T(8,128)S(1)}, f32[44,4,8,128]{3,2,1,0:T(8,128)S(1)}, f32[44,4,8,128]{3,2,1,0:T(8,128)S(1)}, f32[22,2,8,128]{3,2,1,0:T(8,128...) custom-call(f32[8,4]{1,0:T(8,128)S(1)} %copy.28.table_ref, ...), custom_call_target="tpu_custom_call", output_to_operand_aliasing={{0}: (3, {}), {1}: (4, {}), {2}: (5, {}), {3}: (6, {}), {4}... | custom-call | flops 40000000 | bytes 8000000 | tf_op jit(solution)/shard_map/first/pallas_call | solution.py:460
  32.9 0.1 collective-permute-start.3
  33.0 0.4 collective-permute-start.2
  33.3 1.7 %inner_second.1 = (f32[44,4,8,128]{3,2,1,0:T(8,128)S(1)}, f32[44,4,8,128]{3,2,1,0:T(8,128)S(1)}, f32[44,4,8,128]{3,2,1,0:T(8,128)S(1)}, f32[1024,128]{1,0:T(8,128)S(1)}) custom-call(s32[1]{0:T(128)} %bitcast.me_ref, f32[4,4]{1,0:T(4,128)S(1)} %copy-done, f32[16,4,8,128]{3,2,1,0:T(8,128)S(1)} %get-tuple-element.51.own_ref, ...), custom_call_target="tpu_custom_call" | custom-call | flops 40000000 | bytes 8000000 | tf_op jit(solution)/shard_map/inner_second/pallas_call | solution.py:460
  35.0 0.0 collective-permute-done.3.chip_ref
  35.0 1.3 %chip_second.1 = (f32[44,4,8,128]{3,2,1,0:T(8,128)S(1)}, f32[44,4,8,128]{3,2,1,0:T(8,128)S(1)}, f32[44,4,8,128]{3,2,1,0:T(8,128)S(1)}) custom-call(f32[4,4]{1,0:T(4,128)S(1)} %copy-done, f32[13,4,8,128]{3,2,1,0:T(8,128)S(1)} %collective-permute-done.3.chip_ref, ...), custom_call_target="tpu_custom_call", output_to_operand_aliasing={{0}: (4, {}), {1}: (5, {}), {2}: (6, {})} | custom-call | flops 40000000 | bytes 8000000 | tf_op jit(solution)/shard_map/chip_second/pallas_call | solution.py:460
  36.4 2.9 %collective-permute-done.2.next_ref = f32[13,4,8,128]{3,2,1,0:T(8,128)S(1)} collective-permute-done((f32[13,4,8,128]{3,2,1,0:T(8,128)S(1)}, f32[13,4,8,128]{3,2,1,0:T(8,128)S(1)}, u32[]{:S(2)}, u32[]{:S(2)}) %collective-permute-start.2) | collective-permute-done | bytes 213024 | tf_op jit(solution)/shard_map/ppermute | solution.py:446
  39.2 3.7 %second.1 = (f32[44,4,8,128]{3,2,1,0:T(8,128)S(1)}, f32[44,4,8,128]{3,2,1,0:T(8,128)S(1)}, f32[44,4,8,128]{3,2,1,0:T(8,128)S(1)}, f32[1024,128]{1,0:T(8,128)S(1)}) custom-call(s32[1]{0:T(128)} %bitcast.me_ref, f32[4,4]{1,0:T(4,128)S(1)} %copy-done, ...), custom_call_target="tpu_custom_call", output_to_operand_aliasing={{0}: (6, {}), {1}: (7, {}), {2}: (8, {}), {3}: (9, {})} | custom-call | flops 40000000 | bytes 8000000 | tf_op jit(solution)/shard_map/second/pallas_call | solution.py:460
  42.9 20.2 %all_to_all.11.in_ref = f32[16,64,128]{2,1,0:T(8,128)S(1)} all-to-all(f32[16,64,128]{2,1,0:T(8,128)S(1)} %bitcast.8), channel_id=1, replica_groups=mesh['lon'=16,'lat'=8,'dep'=2] {'lat','dep'}, dimensions={0} | all-to-all | bytes 1048576 | tf_op jit(solution)/shard_map/all_to_all | solution.py:494
  63.1 1.0 %finish.1 = (f32[4,8,8,256]{3,2,1,0:T(8,128)}, f32[4,8,8,256]{3,2,1,0:T(8,128)}) custom-call(s32[1]{0:T(128)} %bitcast.me_ref, f32[16,64,128]{2,1,0:T(8,128)S(1)} %all_to_all.11.in_ref), custom_call_target="tpu_custom_call" | custom-call | tf_op jit(solution)/shard_map/finish/pallas_call | solution.py:496
  (1 shorter events, 0.0 us)
Async XLA Ops:
  0.6 1.0 %copy-start.1 = (f32[4,8,8,256]{3,2,1,0:T(8,128)S(1)}, f32[4,8,8,256]{3,2,1,0:T(8,128)}, u32[]{:S(2)}) copy-start(f32[4,8,8,256]{3,2,1,0:T(8,128)} %param.5) | copy-start | bytes 786436
  20.8 1.5 %copy-start = (f32[4,4]{1,0:T(4,128)S(1)}, f32[4,4]{1,0:T(4,128)}, u32[]{:S(2)}) copy-start(f32[4,4]{1,0:T(4,128)} %coupling_ref.11) | copy-start | bytes 196
  21.5 0.8 %copy-start.2 = (f32[8,4]{0,1:T(4,128)S(1)}, f32[8,4]{0,1:T(4,128)}, u32[]{:S(2)}) copy-start(f32[8,4]{0,1:T(4,128)} %param.8) | copy-start | bytes 388
  21.5 2.8 %collective-permute-start.1 = (f32[13,6,8,128]{3,2,1,0:T(8,128)S(1)}, f32[13,6,8,128]{3,2,1,0:T(8,128)S(1)}, u32[]{:S(2)}, u32[]{:S(2)}) collective-permute-start(f32[13,6,8,128]{3,2,1,0:T(8,128)S(1)} %get-tuple-element.32), channel_id=1, source_target_pairs={{15,13},{13,15},{11,9},{9,11},{7,5},{5,7},{3,1},{1,3},{0,2},{2,0},... | collective-permute-start | bytes 958472 | tf_op jit(solution)/shard_map/ppermute | solution.py:447
  22.0 7.3 %collective-permute-start = (f32[13,6,8,128]{3,2,1,0:T(8,128)S(1)}, f32[13,6,8,128]{3,2,1,0:T(8,128)S(1)}, u32[]{:S(2)}, u32[]{:S(2)}) collective-permute-start(f32[13,6,8,128]{3,2,1,0:T(8,128)S(1)} %get-tuple-element.31), channel_id=1, source_target_pairs={{253,13},{9,15},{15,9},{5,11},{11,5},{1,7},{7,1},{2,3},{3,2},{6,0}... | collective-permute-start | bytes 958472 | tf_op jit(solution)/shard_map/ppermute | solution.py:446
  32.9 2.2 %collective-permute-start.3 = (f32[13,4,8,128]{3,2,1,0:T(8,128)S(1)}, f32[13,4,8,128]{3,2,1,0:T(8,128)S(1)}, u32[]{:S(2)}, u32[]{:S(2)}) collective-permute-start(f32[13,4,8,128]{3,2,1,0:T(8,128)S(1)} %get-tuple-element.50), channel_id=1, source_target_pairs={{15,13},{13,15},{11,9},{9,11},{7,5},{5,7},{3,1},{1,3},{0,2},{2,0},... | collective-permute-start | bytes 638984 | tf_op jit(solution)/shard_map/ppermute | solution.py:447
  33.0 6.3 %collective-permute-start.2 = (f32[13,4,8,128]{3,2,1,0:T(8,128)S(1)}, f32[13,4,8,128]{3,2,1,0:T(8,128)S(1)}, u32[]{:S(2)}, u32[]{:S(2)}) collective-permute-start(f32[13,4,8,128]{3,2,1,0:T(8,128)S(1)} %get-tuple-element.46), channel_id=1, source_target_pairs={{253,13},{9,15},{15,9},{5,11},{11,5},{1,7},{7,1},{2,3},{3,2},{6,0}... | collective-permute-start | bytes 638984 | tf_op jit(solution)/shard_map/ppermute | solution.py:446

commit v6 on v5

--- a/solution.py
+++ b/solution.py
@@ -23,8 +23,8 @@
 
 
 PATHS = (
-    ((3, 1), (2, 1), (1, 1), (0, 1), (0, 0), (1, 0), (2, 0), (3, 0)),
-    ((3, 1), (2, 1), (1, 1), (0, 1), (0, 0), (1, 0), (2, 0), (3, 0)),
+    ((1, 0), (2, 0), (3, 0), (0, 0), (0, 1), (3, 1), (2, 1), (1, 1)),
+    ((1, 0), (2, 0), (3, 0), (0, 0), (0, 1), (3, 1), (2, 1), (1, 1)),
 )
 
 
@@ -59,7 +59,7 @@
 
 
 def block_rank(block, chunk):
-    low, high = (places.index((chunk // 2, chunk % 2)) for places in PLACES)
+    low, high = (places.index((chunk % 8, chunk // 8)) for places in PLACES)
     rank = low if low == high else jnp.where(block < 8, low, high)
     odd = lax.rem(block, 2)
     return rank + odd * (15 - 2 * rank)
@@ -103,7 +103,7 @@
     odd = is_odd(me_ref[0])
     for o in range(OWN):
         for q in range(3):
-            parts = [in_ref[pl.ds(d * 48 + q * 16 + o, 8, stride=96), :] for d in range(2)]
+            parts = [in_ref[pl.ds(d * 384 + q * 16 + o, 8, stride=48), :] for d in range(2)]
             for half in range(2):
                 index = place + 64 * half
                 own_ref[local(odd, o), 2 * q + half] = jnp.where(upper, pick(parts[1], index), pick(parts[0], index))
@@ -391,7 +391,7 @@
             for d in range(2):
                 index = place + 8 * d
                 rows = jnp.where(lower, pick(pair[0], index), pick(pair[1], index))
-                out_ref[pl.ds(d * 64 + kind * 32 + q * 16 + o, 8, stride=128), :] = rows
+                out_ref[pl.ds(d * 512 + kind * 32 + q * 16 + o, 8, stride=64), :] = rows
 
 
 def inner_second_kernel(me_ref, coupling_ref, own_ref, gain, size, b_sum, u_a, u_b, out_ref):
@@ -455,7 +455,7 @@
         compiler_params=params(),
         name="pack",
     )(me, jnp.concatenate([x.astype(F32).reshape(-1, 256) for x in (source, sea_mask, classes)]))
-    got = lax.all_to_all(sent, ("lat", "dep"), 0, 0, tiled=False)
+    got = lax.all_to_all(sent, ("dep", "lat"), 0, 0, tiled=False)
     def call(kernel, given, numbers, state, more, work, name):
         return pl.pallas_call(
             kernel,
@@ -491,7 +491,7 @@
     state = call(chip_second_kernel, [coupling, mate, gain, size], 1, state[:3], [], [], "chip_second")
     state = call(second_kernel, [me, coupling, beyond, gain, size, gain_c], 2, list(state) + [sent], [], coarse, "second")
     sent = state[3]
-    got = lax.all_to_all(sent.reshape(16, 64, 128), ("lat", "dep"), 0, 0, tiled=False)
+    got = lax.all_to_all(sent.reshape(16, 64, 128), ("dep", "lat"), 0, 0, tiled=False)
     out = jax.ShapeDtypeStruct((FIELDS, 8, 8, 256), F32)
     return pl.pallas_call(
         finish_kernel,

time: 64.3 us -> 60.1 us (0.935)
  blocking collectives: 39.2 us -> 32.6 us
  starting transfers between devices: 1.26 us -> 2.75 us
  waiting for transfers between devices: 6.4 us -> 7.24 us
    all_to_all x2, blocking collectives: 39.2 us -> 32.6 us  [the longest x1 18 us: per_device(): got = lax.all_to_all(sent, ('dep', 'lat'), 0, 0, tiled=False)]
    ppermute x2, starting transfers between devices: 0.6 us -> 1.88 us  [trade(): return (lax.ppermute(to_chip, AXES, chips), from_next)]
    ppermute x2, waiting for transfers between devices: 6.39 us -> 7.24 us  [trade(): from_next = lax.ppermute(to_next, AXES, nexts)]
  transfers between devices with their start and end apart: 4 -> 4, of which waited for: 2 -> 2; matrix products, arithmetic and copies ran while one was open for 0% -> 0% of each run, Pallas kernels for 10% -> 11%
where the time goes in v6:
time: 60.1 us; the launch traced here: 59.9 us
  blocking collectives  32.6 us (54%)
  Pallas kernels  15.4 us (26%)
  waiting for transfers between devices  7.24 us (12%)
  starting transfers between devices  2.75 us (5%)
  other arithmetic  0.95 us (2%)
  between operations  0.72 us (1%)
    all_to_all x1, blocking collectives, per_device(): got = lax.all_to_all(sent, ('dep', 'lat'), 0, 0, tiled=False)  18 us
    all_to_all x1, blocking collectives, per_device(): lax.all_to_all(sent.reshape(16, 64, 128), ('dep', 'lat'), 0, 0, tiled=False)  14.6 us
    pallas_call x7, Pallas kernels, call(): pl.pallas_call(kernel, out_shape=tuple(state) + tuple(more), in_specs=sme...  14.2 us
    ppermute x2, waiting for transfers between devices, trade(): from_next = lax.ppermute(to_next, AXES, nexts)  7.24 us
    ppermute x2, starting transfers between devices, trade(): return (lax.ppermute(to_chip, AXES, chips), from_next)  1.88 us
  transfers between devices with their start and end apart: 4, of which 2 were waited for; matrix products, arithmetic and copies ran while one was open for 0% of the time, Pallas kernels for 11%

profile of v6, /device:TPU:1, one launch (start us, length us, event | category | flops | bytes accessed | tf_op | source)
XLA Modules:
  0.0 59.9 jit_solution(8818128190695164504)
XLA Ops:
  0.6 0.0 copy-start.1
  0.6 0.9 %convert_bitcast_fusion = (f32[64,256]{1,0:T(8,128)S(1)}, f32[64,256]{1,0:T(8,128)S(1)}) fusion(s32[8,8,256]{2,1,0:T(8,128)} %param.7, s32[8,8,256]{2,1,0:T(8,128)} %param.6), kind=kLoop, calls=%fused_computation.1 | loop fusion | flops 32768 | bytes 262144 | tf_op jit(solution)/shard_map/reshape | solution.py:457
  1.6 0.1 copy-done.1
  1.7 0.2 pack.1
  1.9 18.0 %all_to_all.10 = f32[16,48,128]{2,1,0:T(8,128)S(1)} all-to-all(f32[16,48,128]{2,1,0:T(8,128)S(1)} %pack.1), channel_id=1, replica_groups=mesh['lon'=16,'lat'=8,'dep'=2] {'dep','lat'}, dimensions={0} | all-to-all | bytes 786432 | tf_op jit(solution)/shard_map/all_to_all | solution.py:458
  19.9 0.0 copy-start
  19.9 0.6 %unpack.1 = (f32[16,6,8,128]{3,2,1,0:T(8,128)S(1)}, f32[13,6,8,128]{3,2,1,0:T(8,128)S(1)}, f32[13,6,8,128]{3,2,1,0:T(8,128)S(1)}) custom-call(s32[1]{0:T(128)} %bitcast.me_ref, f32[768,128]{1,0:T(8,128)S(1)} %bitcast.9), custom_call_target="tpu_custom_call" | custom-call | flops 40000000 | bytes 8000000 | tf_op jit(solution)/shard_map/unpack/pallas_call | solution.py:460
  20.5 0.0 copy-start.2
  20.5 1.1 %collective-permute-start.1 = (f32[13,6,8,128]{3,2,1,0:T(8,128)S(1)}, f32[13,6,8,128]{3,2,1,0:T(8,128)S(1)}, u32[]{:S(2)}, u32[]{:S(2)}) collective-permute-start(f32[13,6,8,128]{3,2,1,0:T(8,128)S(1)} %get-tuple-element.32), channel_id=1, source_target_pairs={{4,6},{6,4},{8,10},{10,8},{12,14},{14,12},{0,2},{2,0},{3,1},{1,3},... | collective-permute-start | bytes 958472 | tf_op jit(solution)/shard_map/ppermute | solution.py:447
  21.6 0.9 %collective-permute-start = (f32[13,6,8,128]{3,2,1,0:T(8,128)S(1)}, f32[13,6,8,128]{3,2,1,0:T(8,128)S(1)}, u32[]{:S(2)}, u32[]{:S(2)}) collective-permute-start(f32[13,6,8,128]{3,2,1,0:T(8,128)S(1)} %get-tuple-element.31), channel_id=1, source_target_pairs={{246,6},{10,4},{4,10},{14,8},{8,14},{2,12},{12,2},{1,0},{0,1},{13,... | collective-permute-start | bytes 958472 | tf_op jit(solution)/shard_map/ppermute | solution.py:446
  22.5 0.0 copy-done.2
  22.5 0.1 copy.28.table_ref
  22.6 0.0 copy-done
  22.6 1.9 %inner_first.1 = (f32[44,5,8,128]{3,2,1,0:T(8,128)S(1)}, f32[44,4,8,128]{3,2,1,0:T(8,128)S(1)}, f32[44,4,8,128]{3,2,1,0:T(8,128)S(1)}, f32[22,2,8,128]{3,2,1,0:T...) custom-call(f32[8,4]{1,0:T(8,128)S(1)} %copy.28.table_ref, f32[4,4]{1,0:T(4,128)S(1)} %copy-done, ...), custom_call_target="tpu_custom_call" | custom-call | flops 40000000 | bytes 8000000 | tf_op jit(solution)/shard_map/inner_first/pallas_call | solution.py:460
  24.5 0.0 collective-permute-done.1.chip_ref
  24.5 1.5 %chip_first.1 = (f32[44,5,8,128]{3,2,1,0:T(8,128)S(1)}, f32[44,4,8,128]{3,2,1,0:T(8,128)S(1)}, f32[44,4,8,128]{3,2,1,0:T(8,128)S(1)}, f32[22,2,8,128]{3,2,1,0:T(...) custom-call(f32[8,4]{1,0:T(8,128)S(1)} %copy.28.table_ref, ...), custom_call_target="tpu_custom_call", output_to_operand_aliasing={{0}: (3, {}), {1}: (4, {}), {2}: (5, {}), {3}: (6, {}), {4}... | custom-call | flops 40000000 | bytes 8000000 | tf_op jit(solution)/shard_map/chip_first/pallas_call | solution.py:460
  26.1 3.5 %collective-permute-done.next_ref = f32[13,6,8,128]{3,2,1,0:T(8,128)S(1)} collective-permute-done((f32[13,6,8,128]{3,2,1,0:T(8,128)S(1)}, f32[13,6,8,128]{3,2,1,0:T(8,128)S(1)}, u32[]{:S(2)}, u32[]{:S(2)}) %collective-permute-start) | collective-permute-done | bytes 319520 | tf_op jit(solution)/shard_map/ppermute | solution.py:446
  29.6 3.5 %first.1 = (f32[44,5,8,128]{3,2,1,0:T(8,128)S(1)}, f32[44,4,8,128]{3,2,1,0:T(8,128)S(1)}, f32[44,4,8,128]{3,2,1,0:T(8,128)S(1)}, f32[22,2,8,128]{3,2,1,0:T(8,128...) custom-call(f32[8,4]{1,0:T(8,128)S(1)} %copy.28.table_ref, ...), custom_call_target="tpu_custom_call", output_to_operand_aliasing={{0}: (3, {}), {1}: (4, {}), {2}: (5, {}), {3}: (6, {}), {4}... | custom-call | flops 40000000 | bytes 8000000 | tf_op jit(solution)/shard_map/first/pallas_call | solution.py:460
  33.1 0.8 %collective-permute-start.3 = (f32[13,4,8,128]{3,2,1,0:T(8,128)S(1)}, f32[13,4,8,128]{3,2,1,0:T(8,128)S(1)}, u32[]{:S(2)}, u32[]{:S(2)}) collective-permute-start(f32[13,4,8,128]{3,2,1,0:T(8,128)S(1)} %get-tuple-element.50), channel_id=1, source_target_pairs={{4,6},{6,4},{8,10},{10,8},{12,14},{14,12},{0,2},{2,0},{3,1},{1,3},... | collective-permute-start | bytes 638984 | tf_op jit(solution)/shard_map/ppermute | solution.py:447
  33.8 0.0 collective-permute-start.2
  33.8 1.7 %inner_second.1 = (f32[44,4,8,128]{3,2,1,0:T(8,128)S(1)}, f32[44,4,8,128]{3,2,1,0:T(8,128)S(1)}, f32[44,4,8,128]{3,2,1,0:T(8,128)S(1)}, f32[1024,128]{1,0:T(8,128)S(1)}) custom-call(s32[1]{0:T(128)} %bitcast.me_ref, f32[4,4]{1,0:T(4,128)S(1)} %copy-done, f32[16,4,8,128]{3,2,1,0:T(8,128)S(1)} %get-tuple-element.51.own_ref, ...), custom_call_target="tpu_custom_call" | custom-call | flops 40000000 | bytes 8000000 | tf_op jit(solution)/shard_map/inner_second/pallas_call | solution.py:460
  35.5 0.0 collective-permute-done.3.chip_ref
  35.6 1.3 %chip_second.1 = (f32[44,4,8,128]{3,2,1,0:T(8,128)S(1)}, f32[44,4,8,128]{3,2,1,0:T(8,128)S(1)}, f32[44,4,8,128]{3,2,1,0:T(8,128)S(1)}) custom-call(f32[4,4]{1,0:T(4,128)S(1)} %copy-done, f32[13,4,8,128]{3,2,1,0:T(8,128)S(1)} %collective-permute-done.3.chip_ref, ...), custom_call_target="tpu_custom_call", output_to_operand_aliasing={{0}: (4, {}), {1}: (5, {}), {2}: (6, {})} | custom-call | flops 40000000 | bytes 8000000 | tf_op jit(solution)/shard_map/chip_second/pallas_call | solution.py:460
  36.9 3.7 %collective-permute-done.2.next_ref = f32[13,4,8,128]{3,2,1,0:T(8,128)S(1)} collective-permute-done((f32[13,4,8,128]{3,2,1,0:T(8,128)S(1)}, f32[13,4,8,128]{3,2,1,0:T(8,128)S(1)}, u32[]{:S(2)}, u32[]{:S(2)}) %collective-permute-start.2) | collective-permute-done | bytes 213024 | tf_op jit(solution)/shard_map/ppermute | solution.py:446
  40.6 3.7 %second.1 = (f32[44,4,8,128]{3,2,1,0:T(8,128)S(1)}, f32[44,4,8,128]{3,2,1,0:T(8,128)S(1)}, f32[44,4,8,128]{3,2,1,0:T(8,128)S(1)}, f32[1024,128]{1,0:T(8,128)S(1)}) custom-call(s32[1]{0:T(128)} %bitcast.me_ref, f32[4,4]{1,0:T(4,128)S(1)} %copy-done, ...), custom_call_target="tpu_custom_call", output_to_operand_aliasing={{0}: (6, {}), {1}: (7, {}), {2}: (8, {}), {3}: (9, {})} | custom-call | flops 40000000 | bytes 8000000 | tf_op jit(solution)/shard_map/second/pallas_call | solution.py:460
  44.3 14.6 %all_to_all.11.in_ref = f32[16,64,128]{2,1,0:T(8,128)S(1)} all-to-all(f32[16,64,128]{2,1,0:T(8,128)S(1)} %bitcast.8), channel_id=1, replica_groups=mesh['lon'=16,'lat'=8,'dep'=2] {'dep','lat'}, dimensions={0} | all-to-all | bytes 1048576 | tf_op jit(solution)/shard_map/all_to_all | solution.py:494
  58.9 1.0 %finish.1 = (f32[4,8,8,256]{3,2,1,0:T(8,128)}, f32[4,8,8,256]{3,2,1,0:T(8,128)}) custom-call(s32[1]{0:T(128)} %bitcast.me_ref, f32[16,64,128]{2,1,0:T(8,128)S(1)} %all_to_all.11.in_ref), custom_call_target="tpu_custom_call" | custom-call | tf_op jit(solution)/shard_map/finish/pallas_call | solution.py:496
  (1 shorter events, 0.0 us)
Async XLA Ops:
  0.6 1.0 %copy-start.1 = (f32[4,8,8,256]{3,2,1,0:T(8,128)S(1)}, f32[4,8,8,256]{3,2,1,0:T(8,128)}, u32[]{:S(2)}) copy-start(f32[4,8,8,256]{3,2,1,0:T(8,128)} %param.5) | copy-start | bytes 786436
  19.9 2.7 %copy-start = (f32[4,4]{1,0:T(4,128)S(1)}, f32[4,4]{1,0:T(4,128)}, u32[]{:S(2)}) copy-start(f32[4,4]{1,0:T(4,128)} %coupling_ref.11) | copy-start | bytes 196
  20.5 2.0 %copy-start.2 = (f32[8,4]{0,1:T(4,128)S(1)}, f32[8,4]{0,1:T(4,128)}, u32[]{:S(2)}) copy-start(f32[8,4]{0,1:T(4,128)} %param.8) | copy-start | bytes 388
  20.5 4.0 %collective-permute-start.1 = (f32[13,6,8,128]{3,2,1,0:T(8,128)S(1)}, f32[13,6,8,128]{3,2,1,0:T(8,128)S(1)}, u32[]{:S(2)}, u32[]{:S(2)}) collective-permute-start(f32[13,6,8,128]{3,2,1,0:T(8,128)S(1)} %get-tuple-element.32), channel_id=1, source_target_pairs={{4,6},{6,4},{8,10},{10,8},{12,14},{14,12},{0,2},{2,0},{3,1},{1,3},... | collective-permute-start | bytes 958472 | tf_op jit(solution)/shard_map/ppermute | solution.py:447
  21.6 7.9 %collective-permute-start = (f32[13,6,8,128]{3,2,1,0:T(8,128)S(1)}, f32[13,6,8,128]{3,2,1,0:T(8,128)S(1)}, u32[]{:S(2)}, u32[]{:S(2)}) collective-permute-start(f32[13,6,8,128]{3,2,1,0:T(8,128)S(1)} %get-tuple-element.31), channel_id=1, source_target_pairs={{246,6},{10,4},{4,10},{14,8},{8,14},{2,12},{12,2},{1,0},{0,1},{13,... | collective-permute-start | bytes 958472 | tf_op jit(solution)/shard_map/ppermute | solution.py:446
  33.1 2.5 %collective-permute-start.3 = (f32[13,4,8,128]{3,2,1,0:T(8,128)S(1)}, f32[13,4,8,128]{3,2,1,0:T(8,128)S(1)}, u32[]{:S(2)}, u32[]{:S(2)}) collective-permute-start(f32[13,4,8,128]{3,2,1,0:T(8,128)S(1)} %get-tuple-element.50), channel_id=1, source_target_pairs={{4,6},{6,4},{8,10},{10,8},{12,14},{14,12},{0,2},{2,0},{3,1},{1,3},... | collective-permute-start | bytes 638984 | tf_op jit(solution)/shard_map/ppermute | solution.py:447
  33.8 6.8 %collective-permute-start.2 = (f32[13,4,8,128]{3,2,1,0:T(8,128)S(1)}, f32[13,4,8,128]{3,2,1,0:T(8,128)S(1)}, u32[]{:S(2)}, u32[]{:S(2)}) collective-permute-start(f32[13,4,8,128]{3,2,1,0:T(8,128)S(1)} %get-tuple-element.46), channel_id=1, source_target_pairs={{246,6},{10,4},{4,10},{14,8},{8,14},{2,12},{12,2},{1,0},{0,1},{13,... | collective-permute-start | bytes 638984 | tf_op jit(solution)/shard_map/ppermute | solution.py:446

commit v7 on v6

--- a/solution.py
+++ b/solution.py
@@ -23,13 +23,13 @@
 
 
 PATHS = (
-    ((1, 0), (2, 0), (3, 0), (0, 0), (0, 1), (3, 1), (2, 1), (1, 1)),
-    ((1, 0), (2, 0), (3, 0), (0, 0), (0, 1), (3, 1), (2, 1), (1, 1)),
+    ((1, 1), (2, 1), (3, 1), (0, 1), (0, 0), (3, 0), (2, 0), (1, 0)),
+    ((1, 1), (2, 1), (3, 1), (0, 1), (0, 0), (3, 0), (2, 0), (1, 0)),
 )
 
 
 def spots(path):
-    return [(2 * x + core, dep) for x, dep in path for core in ((0, 1) if dep else (1, 0))]
+    return [(2 * x + core, dep) for x, dep in path for core in ((1, 0) if dep else (0, 1))]
 
 
 PLACES = [spots(path) for path in PATHS]
@@ -55,7 +55,7 @@
 
 def is_odd(me):
     block, lat, dep = lax.div(me, 16), lax.rem(lax.div(me, 2), 8), lax.rem(me, 2)
-    return lax.rem(block + lat + dep + 1, 2)
+    return lax.rem(block + lat + dep, 2)
 
 
 def block_rank(block, chunk):

time: 60.1 us -> 60.5 us (level)
  no operation moved by 1% of the time
where the time goes in v7:
time: 60.5 us; the launch traced here: 60.3 us
  blocking collectives  33.1 us (55%)
  Pallas kernels  15.5 us (26%)
  waiting for transfers between devices  7.24 us (12%)
  starting transfers between devices  2.75 us (5%)
  other arithmetic  0.95 us (2%)
  between operations  0.72 us (1%)
    all_to_all x1, blocking collectives, per_device(): got = lax.all_to_all(sent, ('dep', 'lat'), 0, 0, tiled=False)  18 us
    all_to_all x1, blocking collectives, per_device(): lax.all_to_all(sent.reshape(16, 64, 128), ('dep', 'lat'), 0, 0, tiled=False)  15 us
    pallas_call x7, Pallas kernels, call(): pl.pallas_call(kernel, out_shape=tuple(state) + tuple(more), in_specs=sme...  14.2 us
    ppermute x2, waiting for transfers between devices, trade(): from_next = lax.ppermute(to_next, AXES, nexts)  7.24 us
    ppermute x2, starting transfers between devices, trade(): return (lax.ppermute(to_chip, AXES, chips), from_next)  1.88 us
  transfers between devices with their start and end apart: 4, of which 2 were waited for; matrix products, arithmetic and copies ran while one was open for 0% of the time, Pallas kernels for 11%

profile of v7, /device:TPU:1, one launch (start us, length us, event | category | flops | bytes accessed | tf_op | source)
XLA Modules:
  0.0 60.3 jit_solution(16262369899950658437)
XLA Ops:
  0.6 0.0 copy-start.1
  0.6 0.9 %convert_bitcast_fusion = (f32[64,256]{1,0:T(8,128)S(1)}, f32[64,256]{1,0:T(8,128)S(1)}) fusion(s32[8,8,256]{2,1,0:T(8,128)} %param.7, s32[8,8,256]{2,1,0:T(8,128)} %param.6), kind=kLoop, calls=%fused_computation.1 | loop fusion | flops 32768 | bytes 262144 | tf_op jit(solution)/shard_map/reshape | solution.py:457
  1.6 0.1 copy-done.1
  1.7 0.2 pack.1
  1.9 18.0 %all_to_all.10 = f32[16,48,128]{2,1,0:T(8,128)S(1)} all-to-all(f32[16,48,128]{2,1,0:T(8,128)S(1)} %pack.1), channel_id=1, replica_groups=mesh['lon'=16,'lat'=8,'dep'=2] {'dep','lat'}, dimensions={0} | all-to-all | bytes 786432 | tf_op jit(solution)/shard_map/all_to_all | solution.py:458
  19.9 0.0 copy-start
  19.9 0.6 %unpack.1 = (f32[16,6,8,128]{3,2,1,0:T(8,128)S(1)}, f32[13,6,8,128]{3,2,1,0:T(8,128)S(1)}, f32[13,6,8,128]{3,2,1,0:T(8,128)S(1)}) custom-call(s32[1]{0:T(128)} %bitcast.me_ref, f32[768,128]{1,0:T(8,128)S(1)} %bitcast.9), custom_call_target="tpu_custom_call" | custom-call | flops 40000000 | bytes 8000000 | tf_op jit(solution)/shard_map/unpack/pallas_call | solution.py:460
  20.5 0.0 copy-start.2
  20.5 1.1 %collective-permute-start.1 = (f32[13,6,8,128]{3,2,1,0:T(8,128)S(1)}, f32[13,6,8,128]{3,2,1,0:T(8,128)S(1)}, u32[]{:S(2)}, u32[]{:S(2)}) collective-permute-start(f32[13,6,8,128]{3,2,1,0:T(8,128)S(1)} %get-tuple-element.32), channel_id=1, source_target_pairs={{5,7},{7,5},{9,11},{11,9},{13,15},{15,13},{1,3},{3,1},{2,0},{0,2},... | collective-permute-start | bytes 958472 | tf_op jit(solution)/shard_map/ppermute | solution.py:447
  21.6 0.9 %collective-permute-start = (f32[13,6,8,128]{3,2,1,0:T(8,128)S(1)}, f32[13,6,8,128]{3,2,1,0:T(8,128)S(1)}, u32[]{:S(2)}, u32[]{:S(2)}) collective-permute-start(f32[13,6,8,128]{3,2,1,0:T(8,128)S(1)} %get-tuple-element.31), channel_id=1, source_target_pairs={{247,7},{11,5},{5,11},{15,9},{9,15},{3,13},{13,3},{0,1},{1,0},{12,... | collective-permute-start | bytes 958472 | tf_op jit(solution)/shard_map/ppermute | solution.py:446
  22.5 0.0 copy-done.2
  22.5 0.1 copy.28.table_ref
  22.6 0.0 copy-done
  22.6 1.9 %inner_first.1 = (f32[44,5,8,128]{3,2,1,0:T(8,128)S(1)}, f32[44,4,8,128]{3,2,1,0:T(8,128)S(1)}, f32[44,4,8,128]{3,2,1,0:T(8,128)S(1)}, f32[22,2,8,128]{3,2,1,0:T...) custom-call(f32[8,4]{1,0:T(8,128)S(1)} %copy.28.table_ref, f32[4,4]{1,0:T(4,128)S(1)} %copy-done, ...), custom_call_target="tpu_custom_call" | custom-call | flops 40000000 | bytes 8000000 | tf_op jit(solution)/shard_map/inner_first/pallas_call | solution.py:460
  24.5 0.0 collective-permute-done.1.chip_ref
  24.5 1.5 %chip_first.1 = (f32[44,5,8,128]{3,2,1,0:T(8,128)S(1)}, f32[44,4,8,128]{3,2,1,0:T(8,128)S(1)}, f32[44,4,8,128]{3,2,1,0:T(8,128)S(1)}, f32[22,2,8,128]{3,2,1,0:T(...) custom-call(f32[8,4]{1,0:T(8,128)S(1)} %copy.28.table_ref, ...), custom_call_target="tpu_custom_call", output_to_operand_aliasing={{0}: (3, {}), {1}: (4, {}), {2}: (5, {}), {3}: (6, {}), {4}... | custom-call | flops 40000000 | bytes 8000000 | tf_op jit(solution)/shard_map/chip_first/pallas_call | solution.py:460
  26.1 3.5 %collective-permute-done.next_ref = f32[13,6,8,128]{3,2,1,0:T(8,128)S(1)} collective-permute-done((f32[13,6,8,128]{3,2,1,0:T(8,128)S(1)}, f32[13,6,8,128]{3,2,1,0:T(8,128)S(1)}, u32[]{:S(2)}, u32[]{:S(2)}) %collective-permute-start) | collective-permute-done | bytes 319520 | tf_op jit(solution)/shard_map/ppermute | solution.py:446
  29.6 3.5 %first.1 = (f32[44,5,8,128]{3,2,1,0:T(8,128)S(1)}, f32[44,4,8,128]{3,2,1,0:T(8,128)S(1)}, f32[44,4,8,128]{3,2,1,0:T(8,128)S(1)}, f32[22,2,8,128]{3,2,1,0:T(8,128...) custom-call(f32[8,4]{1,0:T(8,128)S(1)} %copy.28.table_ref, ...), custom_call_target="tpu_custom_call", output_to_operand_aliasing={{0}: (3, {}), {1}: (4, {}), {2}: (5, {}), {3}: (6, {}), {4}... | custom-call | flops 40000000 | bytes 8000000 | tf_op jit(solution)/shard_map/first/pallas_call | solution.py:460
  33.1 0.8 %collective-permute-start.3 = (f32[13,4,8,128]{3,2,1,0:T(8,128)S(1)}, f32[13,4,8,128]{3,2,1,0:T(8,128)S(1)}, u32[]{:S(2)}, u32[]{:S(2)}) collective-permute-start(f32[13,4,8,128]{3,2,1,0:T(8,128)S(1)} %get-tuple-element.50), channel_id=1, source_target_pairs={{5,7},{7,5},{9,11},{11,9},{13,15},{15,13},{1,3},{3,1},{2,0},{0,2},... | collective-permute-start | bytes 638984 | tf_op jit(solution)/shard_map/ppermute | solution.py:447
  33.8 0.0 collective-permute-start.2
  33.8 1.7 %inner_second.1 = (f32[44,4,8,128]{3,2,1,0:T(8,128)S(1)}, f32[44,4,8,128]{3,2,1,0:T(8,128)S(1)}, f32[44,4,8,128]{3,2,1,0:T(8,128)S(1)}, f32[1024,128]{1,0:T(8,128)S(1)}) custom-call(s32[1]{0:T(128)} %bitcast.me_ref, f32[4,4]{1,0:T(4,128)S(1)} %copy-done, f32[16,4,8,128]{3,2,1,0:T(8,128)S(1)} %get-tuple-element.51.own_ref, ...), custom_call_target="tpu_custom_call" | custom-call | flops 40000000 | bytes 8000000 | tf_op jit(solution)/shard_map/inner_second/pallas_call | solution.py:460
  35.6 0.0 collective-permute-done.3.chip_ref
  35.6 1.3 %chip_second.1 = (f32[44,4,8,128]{3,2,1,0:T(8,128)S(1)}, f32[44,4,8,128]{3,2,1,0:T(8,128)S(1)}, f32[44,4,8,128]{3,2,1,0:T(8,128)S(1)}) custom-call(f32[4,4]{1,0:T(4,128)S(1)} %copy-done, f32[13,4,8,128]{3,2,1,0:T(8,128)S(1)} %collective-permute-done.3.chip_ref, ...), custom_call_target="tpu_custom_call", output_to_operand_aliasing={{0}: (4, {}), {1}: (5, {}), {2}: (6, {})} | custom-call | flops 40000000 | bytes 8000000 | tf_op jit(solution)/shard_map/chip_second/pallas_call | solution.py:460
  36.9 3.7 %collective-permute-done.2.next_ref = f32[13,4,8,128]{3,2,1,0:T(8,128)S(1)} collective-permute-done((f32[13,4,8,128]{3,2,1,0:T(8,128)S(1)}, f32[13,4,8,128]{3,2,1,0:T(8,128)S(1)}, u32[]{:S(2)}, u32[]{:S(2)}) %collective-permute-start.2) | collective-permute-done | bytes 213024 | tf_op jit(solution)/shard_map/ppermute | solution.py:446
  40.6 3.7 %second.1 = (f32[44,4,8,128]{3,2,1,0:T(8,128)S(1)}, f32[44,4,8,128]{3,2,1,0:T(8,128)S(1)}, f32[44,4,8,128]{3,2,1,0:T(8,128)S(1)}, f32[1024,128]{1,0:T(8,128)S(1)}) custom-call(s32[1]{0:T(128)} %bitcast.me_ref, f32[4,4]{1,0:T(4,128)S(1)} %copy-done, ...), custom_call_target="tpu_custom_call", output_to_operand_aliasing={{0}: (6, {}), {1}: (7, {}), {2}: (8, {}), {3}: (9, {})} | custom-call | flops 40000000 | bytes 8000000 | tf_op jit(solution)/shard_map/second/pallas_call | solution.py:460
  44.3 15.0 %all_to_all.11.in_ref = f32[16,64,128]{2,1,0:T(8,128)S(1)} all-to-all(f32[16,64,128]{2,1,0:T(8,128)S(1)} %bitcast.8), channel_id=1, replica_groups=mesh['lon'=16,'lat'=8,'dep'=2] {'dep','lat'}, dimensions={0} | all-to-all | bytes 1048576 | tf_op jit(solution)/shard_map/all_to_all | solution.py:494
  59.3 1.0 %finish.1 = (f32[4,8,8,256]{3,2,1,0:T(8,128)}, f32[4,8,8,256]{3,2,1,0:T(8,128)}) custom-call(s32[1]{0:T(128)} %bitcast.me_ref, f32[16,64,128]{2,1,0:T(8,128)S(1)} %all_to_all.11.in_ref), custom_call_target="tpu_custom_call" | custom-call | tf_op jit(solution)/shard_map/finish/pallas_call | solution.py:496
  (1 shorter events, 0.0 us)
Async XLA Ops:
  0.6 1.0 %copy-start.1 = (f32[4,8,8,256]{3,2,1,0:T(8,128)S(1)}, f32[4,8,8,256]{3,2,1,0:T(8,128)}, u32[]{:S(2)}) copy-start(f32[4,8,8,256]{3,2,1,0:T(8,128)} %param.5) | copy-start | bytes 786436
  19.9 2.7 %copy-start = (f32[4,4]{1,0:T(4,128)S(1)}, f32[4,4]{1,0:T(4,128)}, u32[]{:S(2)}) copy-start(f32[4,4]{1,0:T(4,128)} %coupling_ref.11) | copy-start | bytes 196
  20.5 2.0 %copy-start.2 = (f32[8,4]{0,1:T(4,128)S(1)}, f32[8,4]{0,1:T(4,128)}, u32[]{:S(2)}) copy-start(f32[8,4]{0,1:T(4,128)} %param.8) | copy-start | bytes 388
  20.5 4.0 %collective-permute-start.1 = (f32[13,6,8,128]{3,2,1,0:T(8,128)S(1)}, f32[13,6,8,128]{3,2,1,0:T(8,128)S(1)}, u32[]{:S(2)}, u32[]{:S(2)}) collective-permute-start(f32[13,6,8,128]{3,2,1,0:T(8,128)S(1)} %get-tuple-element.32), channel_id=1, source_target_pairs={{5,7},{7,5},{9,11},{11,9},{13,15},{15,13},{1,3},{3,1},{2,0},{0,2},... | collective-permute-start | bytes 958472 | tf_op jit(solution)/shard_map/ppermute | solution.py:447
  21.6 7.9 %collective-permute-start = (f32[13,6,8,128]{3,2,1,0:T(8,128)S(1)}, f32[13,6,8,128]{3,2,1,0:T(8,128)S(1)}, u32[]{:S(2)}, u32[]{:S(2)}) collective-permute-start(f32[13,6,8,128]{3,2,1,0:T(8,128)S(1)} %get-tuple-element.31), channel_id=1, source_target_pairs={{247,7},{11,5},{5,11},{15,9},{9,15},{3,13},{13,3},{0,1},{1,0},{12,... | collective-permute-start | bytes 958472 | tf_op jit(solution)/shard_map/ppermute | solution.py:446
  33.1 2.5 %collective-permute-start.3 = (f32[13,4,8,128]{3,2,1,0:T(8,128)S(1)}, f32[13,4,8,128]{3,2,1,0:T(8,128)S(1)}, u32[]{:S(2)}, u32[]{:S(2)}) collective-permute-start(f32[13,4,8,128]{3,2,1,0:T(8,128)S(1)} %get-tuple-element.50), channel_id=1, source_target_pairs={{5,7},{7,5},{9,11},{11,9},{13,15},{15,13},{1,3},{3,1},{2,0},{0,2},... | collective-permute-start | bytes 638984 | tf_op jit(solution)/shard_map/ppermute | solution.py:447
  33.8 6.8 %collective-permute-start.2 = (f32[13,4,8,128]{3,2,1,0:T(8,128)S(1)}, f32[13,4,8,128]{3,2,1,0:T(8,128)S(1)}, u32[]{:S(2)}, u32[]{:S(2)}) collective-permute-start(f32[13,4,8,128]{3,2,1,0:T(8,128)S(1)} %get-tuple-element.46), channel_id=1, source_target_pairs={{247,7},{11,5},{5,11},{15,9},{9,15},{3,13},{13,3},{0,1},{1,0},{12,... | collective-permute-start | bytes 638984 | tf_op jit(solution)/shard_map/ppermute | solution.py:446

commit v8 on v6

--- a/solution.py
+++ b/solution.py
@@ -443,8 +443,8 @@
     nexts = [(device_of(((g + 1) ^ 1) - 1), device_of(g)) for g in range(256)]
 
     def trade(to_chip, to_next):
-        from_next = lax.ppermute(to_next, AXES, nexts)
-        return lax.ppermute(to_chip, AXES, chips), from_next
+        from_chip = lax.ppermute(to_chip, AXES, chips)
+        return from_chip, lax.ppermute(to_next, AXES, nexts)
 
     sent = pl.pallas_call(
         pack_kernel,

time: 60.1 us -> 60.1 us (level)
  no operation moved by 1% of the time
where the time goes in v8:
time: 60.1 us; the launch traced here: 59.9 us
  blocking collectives  32.6 us (54%)
  Pallas kernels  15.4 us (26%)
  waiting for transfers between devices  7.24 us (12%)
  starting transfers between devices  2.75 us (5%)
  other arithmetic  0.95 us (2%)
  between operations  0.72 us (1%)
    all_to_all x1, blocking collectives, per_device(): got = lax.all_to_all(sent, ('dep', 'lat'), 0, 0, tiled=False)  18 us
    all_to_all x1, blocking collectives, per_device(): lax.all_to_all(sent.reshape(16, 64, 128), ('dep', 'lat'), 0, 0, tiled=False)  14.6 us
    pallas_call x7, Pallas kernels, call(): pl.pallas_call(kernel, out_shape=tuple(state) + tuple(more), in_specs=sme...  14.2 us
    ppermute x2, waiting for transfers between devices, trade(): return (from_chip, lax.ppermute(to_next, AXES, nexts))  7.24 us
    ppermute x2, starting transfers between devices, trade(): from_chip = lax.ppermute(to_chip, AXES, chips)  1.88 us
  transfers between devices with their start and end apart: 4, of which 2 were waited for; matrix products, arithmetic and copies ran while one was open for 0% of the time, Pallas kernels for 11%

profile of v8, /device:TPU:1, one launch (start us, length us, event | category | flops | bytes accessed | tf_op | source)
XLA Modules:
  0.0 59.9 jit_solution(8818128190695164504)
XLA Ops:
  0.6 0.0 copy-start.1
  0.6 0.9 %convert_bitcast_fusion = (f32[64,256]{1,0:T(8,128)S(1)}, f32[64,256]{1,0:T(8,128)S(1)}) fusion(s32[8,8,256]{2,1,0:T(8,128)} %param.7, s32[8,8,256]{2,1,0:T(8,128)} %param.6), kind=kLoop, calls=%fused_computation.1 | loop fusion | flops 32768 | bytes 262144 | tf_op jit(solution)/shard_map/reshape | solution.py:457
  1.6 0.1 copy-done.1
  1.7 0.2 pack.1
  1.9 18.0 %all_to_all.10 = f32[16,48,128]{2,1,0:T(8,128)S(1)} all-to-all(f32[16,48,128]{2,1,0:T(8,128)S(1)} %pack.1), channel_id=1, replica_groups=mesh['lon'=16,'lat'=8,'dep'=2] {'dep','lat'}, dimensions={0} | all-to-all | bytes 786432 | tf_op jit(solution)/shard_map/all_to_all | solution.py:458
  19.9 0.0 copy-start
  19.9 0.6 %unpack.1 = (f32[16,6,8,128]{3,2,1,0:T(8,128)S(1)}, f32[13,6,8,128]{3,2,1,0:T(8,128)S(1)}, f32[13,6,8,128]{3,2,1,0:T(8,128)S(1)}) custom-call(s32[1]{0:T(128)} %bitcast.me_ref, f32[768,128]{1,0:T(8,128)S(1)} %bitcast.9), custom_call_target="tpu_custom_call" | custom-call | flops 40000000 | bytes 8000000 | tf_op jit(solution)/shard_map/unpack/pallas_call | solution.py:460
  20.5 0.0 copy-start.2
  20.5 1.1 %collective-permute-start.1 = (f32[13,6,8,128]{3,2,1,0:T(8,128)S(1)}, f32[13,6,8,128]{3,2,1,0:T(8,128)S(1)}, u32[]{:S(2)}, u32[]{:S(2)}) collective-permute-start(f32[13,6,8,128]{3,2,1,0:T(8,128)S(1)} %get-tuple-element.32), channel_id=1, source_target_pairs={{4,6},{6,4},{8,10},{10,8},{12,14},{14,12},{0,2},{2,0},{3,1},{1,3},... | collective-permute-start | bytes 958472 | tf_op jit(solution)/shard_map/ppermute | solution.py:446
  21.6 0.9 %collective-permute-start = (f32[13,6,8,128]{3,2,1,0:T(8,128)S(1)}, f32[13,6,8,128]{3,2,1,0:T(8,128)S(1)}, u32[]{:S(2)}, u32[]{:S(2)}) collective-permute-start(f32[13,6,8,128]{3,2,1,0:T(8,128)S(1)} %get-tuple-element.31), channel_id=1, source_target_pairs={{246,6},{10,4},{4,10},{14,8},{8,14},{2,12},{12,2},{1,0},{0,1},{13,... | collective-permute-start | bytes 958472 | tf_op jit(solution)/shard_map/ppermute | solution.py:447
  22.5 0.0 copy-done.2
  22.5 0.1 copy.28.table_ref
  22.6 0.0 copy-done
  22.6 1.9 %inner_first.1 = (f32[44,5,8,128]{3,2,1,0:T(8,128)S(1)}, f32[44,4,8,128]{3,2,1,0:T(8,128)S(1)}, f32[44,4,8,128]{3,2,1,0:T(8,128)S(1)}, f32[22,2,8,128]{3,2,1,0:T...) custom-call(f32[8,4]{1,0:T(8,128)S(1)} %copy.28.table_ref, f32[4,4]{1,0:T(4,128)S(1)} %copy-done, ...), custom_call_target="tpu_custom_call" | custom-call | flops 40000000 | bytes 8000000 | tf_op jit(solution)/shard_map/inner_first/pallas_call | solution.py:460
  24.5 0.0 collective-permute-done.1.chip_ref
  24.5 1.5 %chip_first.1 = (f32[44,5,8,128]{3,2,1,0:T(8,128)S(1)}, f32[44,4,8,128]{3,2,1,0:T(8,128)S(1)}, f32[44,4,8,128]{3,2,1,0:T(8,128)S(1)}, f32[22,2,8,128]{3,2,1,0:T(...) custom-call(f32[8,4]{1,0:T(8,128)S(1)} %copy.28.table_ref, ...), custom_call_target="tpu_custom_call", output_to_operand_aliasing={{0}: (3, {}), {1}: (4, {}), {2}: (5, {}), {3}: (6, {}), {4}... | custom-call | flops 40000000 | bytes 8000000 | tf_op jit(solution)/shard_map/chip_first/pallas_call | solution.py:460
  26.1 3.5 %collective-permute-done.next_ref = f32[13,6,8,128]{3,2,1,0:T(8,128)S(1)} collective-permute-done((f32[13,6,8,128]{3,2,1,0:T(8,128)S(1)}, f32[13,6,8,128]{3,2,1,0:T(8,128)S(1)}, u32[]{:S(2)}, u32[]{:S(2)}) %collective-permute-start) | collective-permute-done | bytes 319520 | tf_op jit(solution)/shard_map/ppermute | solution.py:447
  29.6 3.5 %first.1 = (f32[44,5,8,128]{3,2,1,0:T(8,128)S(1)}, f32[44,4,8,128]{3,2,1,0:T(8,128)S(1)}, f32[44,4,8,128]{3,2,1,0:T(8,128)S(1)}, f32[22,2,8,128]{3,2,1,0:T(8,128...) custom-call(f32[8,4]{1,0:T(8,128)S(1)} %copy.28.table_ref, ...), custom_call_target="tpu_custom_call", output_to_operand_aliasing={{0}: (3, {}), {1}: (4, {}), {2}: (5, {}), {3}: (6, {}), {4}... | custom-call | flops 40000000 | bytes 8000000 | tf_op jit(solution)/shard_map/first/pallas_call | solution.py:460
  33.1 0.8 %collective-permute-start.3 = (f32[13,4,8,128]{3,2,1,0:T(8,128)S(1)}, f32[13,4,8,128]{3,2,1,0:T(8,128)S(1)}, u32[]{:S(2)}, u32[]{:S(2)}) collective-permute-start(f32[13,4,8,128]{3,2,1,0:T(8,128)S(1)} %get-tuple-element.50), channel_id=1, source_target_pairs={{4,6},{6,4},{8,10},{10,8},{12,14},{14,12},{0,2},{2,0},{3,1},{1,3},... | collective-permute-start | bytes 638984 | tf_op jit(solution)/shard_map/ppermute | solution.py:446
  33.8 0.0 collective-permute-start.2
  33.8 1.7 %inner_second.1 = (f32[44,4,8,128]{3,2,1,0:T(8,128)S(1)}, f32[44,4,8,128]{3,2,1,0:T(8,128)S(1)}, f32[44,4,8,128]{3,2,1,0:T(8,128)S(1)}, f32[1024,128]{1,0:T(8,128)S(1)}) custom-call(s32[1]{0:T(128)} %bitcast.me_ref, f32[4,4]{1,0:T(4,128)S(1)} %copy-done, f32[16,4,8,128]{3,2,1,0:T(8,128)S(1)} %get-tuple-element.51.own_ref, ...), custom_call_target="tpu_custom_call" | custom-call | flops 40000000 | bytes 8000000 | tf_op jit(solution)/shard_map/inner_second/pallas_call | solution.py:460
  35.5 0.0 collective-permute-done.3.chip_ref
  35.6 1.3 %chip_second.1 = (f32[44,4,8,128]{3,2,1,0:T(8,128)S(1)}, f32[44,4,8,128]{3,2,1,0:T(8,128)S(1)}, f32[44,4,8,128]{3,2,1,0:T(8,128)S(1)}) custom-call(f32[4,4]{1,0:T(4,128)S(1)} %copy-done, f32[13,4,8,128]{3,2,1,0:T(8,128)S(1)} %collective-permute-done.3.chip_ref, ...), custom_call_target="tpu_custom_call", output_to_operand_aliasing={{0}: (4, {}), {1}: (5, {}), {2}: (6, {})} | custom-call | flops 40000000 | bytes 8000000 | tf_op jit(solution)/shard_map/chip_second/pallas_call | solution.py:460
  36.9 3.7 %collective-permute-done.2.next_ref = f32[13,4,8,128]{3,2,1,0:T(8,128)S(1)} collective-permute-done((f32[13,4,8,128]{3,2,1,0:T(8,128)S(1)}, f32[13,4,8,128]{3,2,1,0:T(8,128)S(1)}, u32[]{:S(2)}, u32[]{:S(2)}) %collective-permute-start.2) | collective-permute-done | bytes 213024 | tf_op jit(solution)/shard_map/ppermute | solution.py:447
  40.6 3.7 %second.1 = (f32[44,4,8,128]{3,2,1,0:T(8,128)S(1)}, f32[44,4,8,128]{3,2,1,0:T(8,128)S(1)}, f32[44,4,8,128]{3,2,1,0:T(8,128)S(1)}, f32[1024,128]{1,0:T(8,128)S(1)}) custom-call(s32[1]{0:T(128)} %bitcast.me_ref, f32[4,4]{1,0:T(4,128)S(1)} %copy-done, ...), custom_call_target="tpu_custom_call", output_to_operand_aliasing={{0}: (6, {}), {1}: (7, {}), {2}: (8, {}), {3}: (9, {})} | custom-call | flops 40000000 | bytes 8000000 | tf_op jit(solution)/shard_map/second/pallas_call | solution.py:460
  44.3 14.6 %all_to_all.11.in_ref = f32[16,64,128]{2,1,0:T(8,128)S(1)} all-to-all(f32[16,64,128]{2,1,0:T(8,128)S(1)} %bitcast.8), channel_id=1, replica_groups=mesh['lon'=16,'lat'=8,'dep'=2] {'dep','lat'}, dimensions={0} | all-to-all | bytes 1048576 | tf_op jit(solution)/shard_map/all_to_all | solution.py:494
  58.9 1.0 %finish.1 = (f32[4,8,8,256]{3,2,1,0:T(8,128)}, f32[4,8,8,256]{3,2,1,0:T(8,128)}) custom-call(s32[1]{0:T(128)} %bitcast.me_ref, f32[16,64,128]{2,1,0:T(8,128)S(1)} %all_to_all.11.in_ref), custom_call_target="tpu_custom_call" | custom-call | tf_op jit(solution)/shard_map/finish/pallas_call | solution.py:496
  (1 shorter events, 0.0 us)
Async XLA Ops:
  0.6 1.0 %copy-start.1 = (f32[4,8,8,256]{3,2,1,0:T(8,128)S(1)}, f32[4,8,8,256]{3,2,1,0:T(8,128)}, u32[]{:S(2)}) copy-start(f32[4,8,8,256]{3,2,1,0:T(8,128)} %param.5) | copy-start | bytes 786436
  19.9 2.7 %copy-start = (f32[4,4]{1,0:T(4,128)S(1)}, f32[4,4]{1,0:T(4,128)}, u32[]{:S(2)}) copy-start(f32[4,4]{1,0:T(4,128)} %coupling_ref.11) | copy-start | bytes 196
  20.5 2.0 %copy-start.2 = (f32[8,4]{0,1:T(4,128)S(1)}, f32[8,4]{0,1:T(4,128)}, u32[]{:S(2)}) copy-start(f32[8,4]{0,1:T(4,128)} %param.8) | copy-start | bytes 388
  20.5 4.0 %collective-permute-start.1 = (f32[13,6,8,128]{3,2,1,0:T(8,128)S(1)}, f32[13,6,8,128]{3,2,1,0:T(8,128)S(1)}, u32[]{:S(2)}, u32[]{:S(2)}) collective-permute-start(f32[13,6,8,128]{3,2,1,0:T(8,128)S(1)} %get-tuple-element.32), channel_id=1, source_target_pairs={{4,6},{6,4},{8,10},{10,8},{12,14},{14,12},{0,2},{2,0},{3,1},{1,3},... | collective-permute-start | bytes 958472 | tf_op jit(solution)/shard_map/ppermute | solution.py:446
  21.6 7.9 %collective-permute-start = (f32[13,6,8,128]{3,2,1,0:T(8,128)S(1)}, f32[13,6,8,128]{3,2,1,0:T(8,128)S(1)}, u32[]{:S(2)}, u32[]{:S(2)}) collective-permute-start(f32[13,6,8,128]{3,2,1,0:T(8,128)S(1)} %get-tuple-element.31), channel_id=1, source_target_pairs={{246,6},{10,4},{4,10},{14,8},{8,14},{2,12},{12,2},{1,0},{0,1},{13,... | collective-permute-start | bytes 958472 | tf_op jit(solution)/shard_map/ppermute | solution.py:447
  33.1 2.5 %collective-permute-start.3 = (f32[13,4,8,128]{3,2,1,0:T(8,128)S(1)}, f32[13,4,8,128]{3,2,1,0:T(8,128)S(1)}, u32[]{:S(2)}, u32[]{:S(2)}) collective-permute-start(f32[13,4,8,128]{3,2,1,0:T(8,128)S(1)} %get-tuple-element.50), channel_id=1, source_target_pairs={{4,6},{6,4},{8,10},{10,8},{12,14},{14,12},{0,2},{2,0},{3,1},{1,3},... | collective-permute-start | bytes 638984 | tf_op jit(solution)/shard_map/ppermute | solution.py:446
  33.8 6.8 %collective-permute-start.2 = (f32[13,4,8,128]{3,2,1,0:T(8,128)S(1)}, f32[13,4,8,128]{3,2,1,0:T(8,128)S(1)}, u32[]{:S(2)}, u32[]{:S(2)}) collective-permute-start(f32[13,4,8,128]{3,2,1,0:T(8,128)S(1)} %get-tuple-element.46), channel_id=1, source_target_pairs={{246,6},{10,4},{4,10},{14,8},{8,14},{2,12},{12,2},{1,0},{0,1},{13,... | collective-permute-start | bytes 638984 | tf_op jit(solution)/shard_map/ppermute | solution.py:447
